TPU v7x, 32 devices: a whole 2x2x4 slice. The times are simulated.
32 devices in a mesh: fsdp: 16 (over z, y, x), seq: 2 (over core).
Axes of the slice: x: 2, y: 2, z: 4, core: 2. Of those that a mesh axis runs over, the one named last changes fastest.
Arguments:
- tokens: bfloat16 [2, 16, 1024, 768], P(None, 'fsdp', 'seq'), may hold values from -6 to 6
- lengths: int32 [2, 16], P(None, 'fsdp'), may hold values from 256 to 1024, as said below
- norm_gain: float32 [768], replicated, may hold values from 0.1 to 1.9
- in_weight: bfloat16 [768, 3352], P(('fsdp', 'seq')), may hold values from -0.21875 to 0.21875
- conv_weight: float32 [4, 1792], replicated, may hold values from -3 to 3
- conv_bias: float32 [1792], replicated, may hold values from -3 to 3
- dt_bias: float32 [24], replicated, may hold values from -7 to -3
- a_log: float32 [24], replicated, may hold values from 0 to 2.77
- skip_gain: float32 [24], replicated, may hold values from 0.5 to 2
- out_gain: float32 [1536], replicated, may hold values from 0.1 to 1.9
- out_weight: bfloat16 [1536, 768], P(None, ('fsdp', 'seq')), may hold values from -0.15625 to 0.15625
- out_grad: bfloat16 [2, 16, 1024, 768], P(None, 'fsdp', 'seq'), may hold values from -6 to 6
Outputs:
- mixed: bfloat16 [2, 16, 1024, 768], P(None, 'fsdp', 'seq')
- tokens_grad: float32 [2, 16, 1024, 768], P(None, 'fsdp', 'seq')
- norm_gain_grad: float32 [768], replicated
- in_weight_grad: float32 [768, 3352], P(('fsdp', 'seq'))
- conv_weight_grad: float32 [4, 1792], replicated
- conv_bias_grad: float32 [1792], replicated
- dt_bias_grad: float32 [24], replicated
- a_log_grad: float32 [24], replicated
- skip_gain_grad: float32 [24], replicated
- out_gain_grad: float32 [1536], replicated
- out_weight_grad: float32 [1536, 768], P(None, ('fsdp', 'seq'))
Inputs may be any that keep to these rules, and one draw needn't show every extreme that they name: `lengths`: among the 2 slots of each slot index s, one chosen from the seed has length 1024 and another 256; any others are drawn evenly between.
All inputs are finite; a program needn't handle non-finite values.
Results may differ from a plain program's by a relative error of at most 0.012.
Values may be sent and summed in bfloat16 or wider, within the bound.
A program may use at most 256 MiB of HBM per device.

v0:
```python
import jax
import jax.numpy as jnp
from jax import lax
from jax.sharding import PartitionSpec as P

D = 768
HEADS = 24
HEADDIM = 64
NSTATE = 128
CONV = 4
GROUP = 256
INNER = 1536
CONVCH = 1792
PROJ = 3352


eps_norm = 1e-05


def passed_along(block, axis, distance):
    devices = range(lax.axis_size(axis))
    route = [(i - distance, i) for i in devices if i - distance in devices]
    return lax.ppermute(block, axis, route)


def prefix(array, axis, combine, identity, reverse):
    length, place = (lax.axis_size(axis), lax.axis_index(axis))
    everything = jax.tree.map(lambda part: lax.all_gather(part, axis), array)
    start = jax.tree.map(
        lambda part, zero: jnp.broadcast_to(jnp.asarray(zero, part.dtype), part.shape),
        array,
        identity,
    )

    def lap(k, before):
        at = length - 1 - k if reverse else k
        reached = at > place if reverse else at < place
        new = combine(before, jax.tree.map(lambda part: part[at], everything))
        return jax.tree.map(lambda a, b: jnp.where(reached, a, b), new, before)

    return lax.fori_loop(0, length, lap, start)


def make_tools():

    def narrow_plain(value):
        return lax.optimization_barrier(value.astype(jnp.bfloat16)).astype(jnp.float32)

    narrow = jax.custom_vjp(narrow_plain)

    def narrow_keep(value):
        return (narrow_plain(value), None)

    def narrow_pass(saved_ops, cotangent):
        return (cotangent,)

    narrow.defvjp(narrow_keep, narrow_pass)

    def back_plain(value):
        return value

    narrow_back = jax.custom_vjp(back_plain)

    def back_keep(value):
        return (value, None)

    def back_narrow(saved_ops, cotangent):
        return (narrow_plain(cotangent),)

    narrow_back.defvjp(back_keep, back_narrow)

    def product_plain(left_op, right_op):
        return jnp.matmul(
            left_op.astype(jnp.bfloat16),
            right_op.astype(jnp.bfloat16),
            preferred_element_type=jnp.float32,
        )

    product = jax.custom_vjp(product_plain)

    def product_keep(left_op, right_op):
        return (product_plain(left_op, right_op), (left_op, right_op))

    def product_back(saved_ops, cotangent):
        left_op, right_op = saved_ops
        grad_low = cotangent.astype(jnp.bfloat16)
        left_grad = jnp.matmul(
            grad_low,
            jnp.swapaxes(right_op, -1, -2).astype(jnp.bfloat16),
            preferred_element_type=jnp.float32,
        )
        right_grad = jnp.matmul(
            jnp.swapaxes(left_op, -1, -2).astype(jnp.bfloat16),
            grad_low,
            preferred_element_type=jnp.float32,
        )
        return (left_grad, right_grad)

    product.defvjp(product_keep, product_back)
    return (narrow, narrow_back, product)


def front_norm(token_rows, norm_gain):
    inv_root = lax.rsqrt(jnp.mean(token_rows * token_rows, axis=-1, keepdims=True) + eps_norm)
    return token_rows * inv_root * norm_gain


def conv_section(conv_low, edge_rows, dt_raw, conv_weight, conv_bias, dt_bias, a_log):
    narrow, narrow_back, product = make_tools()
    row_count = conv_low.shape[0]
    padded = jnp.concatenate([edge_rows, conv_low], axis=0)
    conv_acc = conv_bias + conv_weight[0] * padded[0:row_count]
    for ordinal in range(1, CONV):
        conv_acc = conv_acc + conv_weight[ordinal] * padded[ordinal : ordinal + row_count]
    conv_out = narrow(jax.nn.silu(conv_acc))
    step_size = jax.nn.softplus(dt_raw + dt_bias)
    log_rate = step_size * -jnp.exp(a_log)
    return (conv_out, step_size, log_rate)


def within_part(scores, cumulative, step_blocks, x_blocks):
    narrow, narrow_back, product = make_tools()
    blocks = x_blocks.shape[0]
    causal = jnp.arange(GROUP)[:, None] >= jnp.arange(GROUP)[None, :]
    cum_heads = jnp.swapaxes(cumulative, 1, 2)
    log_gap = cum_heads[:, :, :, None] - cum_heads[:, :, None, :]
    log_gap = jnp.where(causal, log_gap, 0.0)
    fade_mask = jnp.where(causal, jnp.exp(log_gap), 0.0)
    mixing = narrow(scores[:, None] * fade_mask * jnp.swapaxes(step_blocks, 1, 2)[:, :, None, :])
    heads_x = x_blocks.reshape(blocks, GROUP, HEADS, HEADDIM).transpose(0, 2, 1, 3)
    within = product(mixing, heads_x)
    return within.transpose(0, 2, 1, 3).reshape(blocks, GROUP, INNER)


def group_local(conv_out, step_size, log_rate):
    narrow, narrow_back, product = make_tools()
    blocks = conv_out.shape[0] // GROUP
    x_blocks = conv_out[:, :INNER].reshape(blocks, GROUP, INNER)
    key_part = conv_out[:, INNER : INNER + NSTATE].reshape(blocks, GROUP, NSTATE)
    query_part = conv_out[:, INNER + NSTATE :].reshape(blocks, GROUP, NSTATE)
    step_blocks = step_size.reshape(blocks, GROUP, HEADS)
    cumulative = jnp.cumsum(log_rate.reshape(blocks, GROUP, HEADS), axis=1)
    block_total = cumulative[:, -1]
    scores = narrow_back(product(query_part, jnp.swapaxes(key_part, 1, 2)))
    within = within_part(scores, cumulative, step_blocks, x_blocks)
    weight_in = jnp.exp(block_total[:, None, :] - cumulative) * step_blocks
    scaled = narrow(x_blocks * jnp.repeat(weight_in, HEADDIM, axis=-1))
    states = narrow_back(product(jnp.swapaxes(key_part, 1, 2), scaled))
    running = jnp.zeros((NSTATE, INNER), jnp.float32)
    decay_run = jnp.ones((HEADS,), jnp.float32)
    starts = []
    decays = []
    for ordinal in range(blocks):
        starts.append(running)
        decays.append(decay_run)
        block_decay = jnp.exp(block_total[ordinal])
        running = running * jnp.repeat(block_decay, HEADDIM)[None, :] + states[ordinal]
        decay_run = decay_run * block_decay
    return (within, cumulative, jnp.stack(starts), jnp.stack(decays), decay_run, running)


def group_finish(
    conv_out, cumulative, starts, decays, entry_state, within, skip_gain, gate_part, out_gain
):
    narrow, narrow_back, product = make_tools()
    row_count = conv_out.shape[0]
    blocks = row_count // GROUP
    x_part = conv_out[:, :INNER]
    query_part = conv_out[:, INNER + NSTATE :].reshape(blocks, GROUP, NSTATE)
    held_state = narrow(
        jnp.repeat(decays, HEADDIM, axis=-1)[:, None, :] * entry_state[None] + starts
    )
    carried = narrow_back(product(query_part, held_state)) * jnp.repeat(
        jnp.exp(cumulative), HEADDIM, axis=-1
    )
    mixed_ssd = (within + carried).reshape(row_count, INNER)
    ssd = narrow_back(mixed_ssd + jnp.repeat(skip_gain, HEADDIM) * x_part)
    gated = ssd * jax.nn.silu(gate_part)
    gate_root = lax.rsqrt(jnp.mean(gated * gated, axis=-1, keepdims=True) + eps_norm)
    return narrow(gated * gate_root * out_gain)


def chain_join(earlier, later):
    decay_a, state_a = earlier
    decay_b, state_b = later
    return (decay_a * decay_b, state_a * jnp.repeat(decay_b, HEADDIM)[None, :] + state_b)


def shards(
    tokens,
    lengths,
    norm_gain,
    in_weight,
    conv_weight,
    conv_bias,
    dt_bias,
    a_log,
    skip_gain,
    out_gain,
    out_weight,
    out_grad,
):
    micro_count = tokens.shape[0]
    row_count = tokens.shape[2]
    positions = lax.axis_index("seq") * row_count + jnp.arange(row_count, dtype=jnp.int32)
    identity = (jnp.ones((HEADS,), jnp.float32), jnp.zeros((NSTATE, INNER), jnp.float32))
    in_acc = jnp.zeros((D, PROJ), jnp.float32)
    out_acc = jnp.zeros((INNER, D), jnp.float32)
    small_acc = (
        jnp.zeros_like(norm_gain),
        jnp.zeros_like(conv_weight),
        jnp.zeros_like(conv_bias),
        jnp.zeros_like(dt_bias),
        jnp.zeros_like(a_log),
        jnp.zeros_like(skip_gain),
        jnp.zeros_like(out_gain),
    )
    mixed_list = []
    grad_list = []
    for micro in range(micro_count):
        front_in, front_out = (
            lax.all_gather(in_weight, ("fsdp", "seq"), axis=0, tiled=True),
            lax.all_gather(out_weight, ("fsdp", "seq"), axis=1, tiled=True),
        )
        valid_rows = (positions < lengths[micro, 0]).astype(jnp.float32)[:, None]
        token_rows = tokens[micro, 0].astype(jnp.float32)
        normed, front_back = jax.vjp(front_norm, token_rows, norm_gain)
        normed_low = normed.astype(jnp.bfloat16)
        projected = jnp.dot(normed_low, front_in, preferred_element_type=jnp.float32)
        gate_part = projected[:, :INNER]
        conv_low = projected[:, INNER : INNER + CONVCH].astype(jnp.bfloat16)
        dt_raw = projected[:, INNER + CONVCH :]
        edge_rows = passed_along(conv_low[row_count - (CONV - 1) :], "seq", 1)
        (conv_out, step_size, log_rate), conv_back = jax.vjp(
            conv_section,
            conv_low.astype(jnp.float32),
            edge_rows.astype(jnp.float32),
            dt_raw,
            conv_weight,
            conv_bias,
            dt_bias,
            a_log,
        )
        local_out, local_back = jax.vjp(group_local, conv_out, step_size, log_rate)
        within, cumulative, starts, decays, dev_decay, dev_state = local_out
        entry_decay, entry_state = prefix(
            (dev_decay, dev_state), "seq", chain_join, identity, False
        )
        out_normed, finish_back = jax.vjp(
            group_finish,
            conv_out,
            cumulative,
            starts,
            decays,
            entry_state,
            within,
            skip_gain,
            gate_part,
            out_gain,
        )
        out_low = out_normed.astype(jnp.bfloat16)
        branch = jnp.dot(out_low, front_out, preferred_element_type=jnp.float32)
        mixed_list.append((valid_rows * (token_rows + branch)).astype(jnp.bfloat16))
        back_in, back_out = (
            lax.all_gather(in_weight, ("fsdp", "seq"), axis=0, tiled=True),
            lax.all_gather(out_weight, ("fsdp", "seq"), axis=1, tiled=True),
        )
        grad_rows = valid_rows * out_grad[micro, 0].astype(jnp.float32)
        grad_low = grad_rows.astype(jnp.bfloat16)
        out_acc = out_acc + jnp.einsum(
            "ti,td->id", out_low, grad_low, preferred_element_type=jnp.float32
        )
        grad_normed_out = jnp.einsum(
            "td,id->ti", grad_low, back_out, preferred_element_type=jnp.float32
        )
        finish_grads = finish_back(grad_normed_out)
        g_conv_a, g_cum, g_starts, g_decays, g_entry, g_within, g_skip, g_gate, g_out_gain = (
            finish_grads
        )
        after_decay, after_grad = prefix((dev_decay, g_entry), "seq", chain_join, identity, True)
        g_dev_decay = jnp.sum(
            (after_grad * entry_state).reshape(NSTATE, HEADS, HEADDIM), axis=(0, 2)
        )
        g_conv_b, g_step, g_rate = local_back(
            (g_within, g_cum, g_starts, g_decays, g_dev_decay, after_grad)
        )
        conv_grads = conv_back((g_conv_a + g_conv_b, g_step, g_rate))
        g_conv_in, g_edge, g_dt_raw, g_conv_w, g_conv_bias, g_dt_bias, g_a_log = conv_grads
        returned = passed_along(g_edge, "seq", -1)
        g_conv_in = g_conv_in + jnp.pad(returned, ((row_count - (CONV - 1), 0), (0, 0)))
        g_proj = jnp.concatenate([g_gate, g_conv_in, g_dt_raw], axis=-1).astype(jnp.bfloat16)
        in_acc = in_acc + jnp.einsum(
            "td,tp->dp", normed_low, g_proj, preferred_element_type=jnp.float32
        )
        g_normed = jnp.einsum("tp,dp->td", g_proj, back_in, preferred_element_type=jnp.float32)
        g_tokens, g_norm_gain = front_back(g_normed)
        grad_list.append(grad_rows + g_tokens)
        small_acc = jax.tree.map(
            jnp.add,
            small_acc,
            (g_norm_gain, g_conv_w, g_conv_bias, g_dt_bias, g_a_log, g_skip, g_out_gain),
        )
    in_grad, out_w_grad = (
        lax.psum_scatter(in_acc, ("fsdp", "seq"), scatter_dimension=0, tiled=True),
        lax.psum_scatter(out_acc, ("fsdp", "seq"), scatter_dimension=1, tiled=True),
    )
    norm_grad, conv_w_grad, conv_b_grad, dtb_grad, alog_grad, skip_grad, gain_grad = lax.psum(
        small_acc, ("fsdp", "seq")
    )
    mixed = jnp.stack(mixed_list)[:, None]
    tokens_grad = jnp.stack(grad_list)[:, None]
    return (
        mixed,
        tokens_grad,
        norm_grad,
        in_grad,
        conv_w_grad,
        conv_b_grad,
        dtb_grad,
        alog_grad,
        skip_grad,
        gain_grad,
        out_w_grad,
    )


def solution(mesh):
    placed = (
        P(None, "fsdp", "seq", None),
        P(None, "fsdp"),
        P(),
        P(("fsdp", "seq"), None),
        P(),
        P(),
        P(),
        P(),
        P(),
        P(),
        P(None, ("fsdp", "seq")),
        P(None, "fsdp", "seq", None),
    )
    return jax.shard_map(
        shards,
        mesh=mesh,
        in_specs=placed,
        out_specs=(
            P(None, "fsdp", "seq", None),
            P(None, "fsdp", "seq", None),
            P(),
            P(("fsdp", "seq"), None),
            P(),
            P(),
            P(),
            P(),
            P(),
            P(),
            P(None, ("fsdp", "seq")),
        ),
        check_vma=False,
    )
```

profile of v0, /device:TPU:0, one launch (start us, length us, event | category | flops | bytes accessed | tf_op | source)
XLA Modules:
  0.0 774.1 jit_solution(9079831359179479105)
XLA Ops:
  16.4 54.5 %all-gather.15.cloned.1.call-done = bf16[1536,768]{0,1:T(8,128)(2,1)} async-done(((bf16[1536,24]{0,1:T(8,128)(2,1)}), bf16[1536,768]{0,1:T(8,128)(2,1)}) %all-gather.15.cloned.1.call-update) | async-done | bytes 2359312 | tf_op jit(solution)/shard_map/all_gather | solution.py:223
  70.9 5.1 fusion.95
  76.0 62.3 %all-gather.11.cloned.1.call-done = bf16[768,3352]{1,0:T(8,128)(2,1)} async-done(((bf16[24,3352]{1,0:T(8,128)(2,1)}), bf16[768,3352]{1,0:T(8,128)(2,1)}) %all-gather.11.cloned.1.call-update) | async-done | bytes 5148688 | tf_op jit(solution)/shard_map/all_gather | solution.py:222
  138.3 5.5 fusion.203
  200.7 20.0 %multiply_convert_fusion.3 = (bf16[512,1792]{0,1:T(8,128)(2,1)}, f32[512,1792]{0,1:T(8,128)}, bf16[512,1792]{0,1:T(8,128)(2,1)S(1)}, f32[512,1792]{0,1:T(8,128)}) fusion(f32[512,1792]{0,1:T(8,128)} %slice_convert_fusion.1, f32[1792]{0:T(1024)S(1)} %get-tuple-element.654, f32[3,1792]{0,1:T(8,128)S(1)} %convert_element_type.271, ...), kind=kLoop, calls=%fused_computation.73 | loop fusion | flops 29360128 | bytes 18428928 | tf_op jit(solution)/shard_map/jvp()/convert_element_type | solution.py:47
  230.4 10.3 %multiply_convert_fusion.1 = (bf16[2,24,256,256]{3,2,1,0:T(8,128)(2,1)}, bf16[2,24,256,256]{3,2,1,0:T(8,128)(2,1)}) fusion(f32[2,24,256]{2,1,0:T(8,128)} %copy.372, f32[2,24,256]{2,1,0:T(8,128)} %get-tuple-element.766, f32[2,256,256]{2,1,0:T(8,128)S(1)} %fusion.126, pred[256,256]{1,0:T(8,128)(4,1)} %iota_compare_fusion, f32[2,24,256]{2,1,0:T(8,128)} %copy.387, ...), kind=kLoop, calls=%fused_computation.22 | loop fusion | flops 37748736 | bytes 13893632 | tf_op jit(solution)/shard_map/jvp()/convert_element_type | solution.py:47
  244.2 7.0 fusion.66
  275.9 6.9 fusion.68
  289.3 8.7 %all-gather.19.cloned.1.call-start = ((), (), s32[]{:S(2)}) async-start(), calls=%async_computation.7 | async-start | bytes 2359296 | tf_op jit(solution)/shard_map/all_gather | solution.py:28
  303.3 6.5 multiply_add_fusion.5
  317.5 6.5 multiply_add_fusion.7
  327.5 7.8 %multiply_reduce_fusion.19 = (f32[512]{0:T(512)S(1)}, f32[512,1536]{0,1:T(8,128)S(1)}, f32[512]{0:T(512)S(1)}, f32[512,1536]{0,1:T(8,128)S(1)}) fusion(f32[512,3352]{0,1:T(8,128)} %copy-done.20, f32[512,1536]{0,1:T(8,128)} %copy.473, f32[512,1792]{0,1:T(8,128)} %convert_element_type.274, f32[1536]{0:T(1024)S(1)} %mul.1040, f32[512,3352]{0,1:T(8,128)} %copy-done.21, ...), kind=kLoop, calls=%fused_computation.120 | loop fusion | flops 14154752 | bytes 25176064 | tf_op jit(solution)/shard_map/jvp()/reduce_sum | solution.py:179
  336.1 4.9 multiply_reduce_fusion.12
  342.1 10.6 %fusion.24 = (bf16[512,1536]{0,1:T(8,128)(2,1)}, bf16[512,1536]{0,1:T(8,128)(2,1)S(1)}, bf16[512,1536]{0,1:T(8,128)(2,1)}, bf16[512,1536]{0,1:T(8,128)(2,1)}, bf...) fusion(f32[512,3352]{0,1:T(8,128)} %copy-done.20, f32[512,1536]{0,1:T(8,128)S(1)} %get-tuple-element.710, ...), kind=kLoop, calls=%fused_computation.80 | loop fusion | flops 37748736 | bytes 40914944 | tf_op jit(solution)/shard_map/convert.7
  377.6 6.2 fusion.63
  383.8 18.6 %fusion.9 = (f32[2,24,256]{2,1,0:T(8,128)}, f32[2,24,256]{2,1,0:T(8,128)}, f32[2,24,256]{2,1,0:T(8,128)}, bf16[2,256,256]{2,1,0:T(8,128)(2,1)}, bf16[2,256,256]{...) fusion(f32[2,24,256]{2,1,0:T(8,128)S(1)} %copy-done.108, ...), kind=kOutput, calls=%fused_computation.28 | convolution fusion | flops 496689152 | bytes 17858560 | tf_op jit(solution)/shard_map/transpose(jvp())/dot_general | solution.py:131
  419.8 5.9 fusion.58
  432.1 5.1 mul.1118
  443.6 5.1 mul.1172
  485.3 7.4 multiply_add_fusion.3
  503.7 7.4 multiply_add_fusion.2
  515.0 12.9 %multiply_reduce_fusion.10 = (f32[1792]{0:T(1024)S(1)}, f32[1792]{0:T(1024)S(1)}, f32[1792]{0:T(1024)S(1)}, f32[1792]{0:T(1024)S(1)}, f32[1792]{0:T(1024)S(1)}, /*index=5*/f32[512,1792]{0,1:T(8,128)}) fusion(f32[512,1792]{0,1:T(8,128)} %slice_convert_fusion.1, f32[3,1792]{0,1:T(8,128)S(1)} %copy-done.45, bf16[512,3352]{0,1:T(8,128)(2,1)} %copy-done.27, ...), kind=kLoop, calls=%fused_computation.68 | loop fusion | flops 23846144 | bytes 19980288 | tf_op jit(solution)/shard_map/transpose(jvp())/reduce_sum | solution.py:114
  528.0 10.5 %multiply_reduce_fusion.6 = (f32[1792]{0:T(1024)S(1)}, f32[1792]{0:T(1024)S(1)}, f32[1792]{0:T(1024)S(1)}, f32[1792]{0:T(1024)S(1)}, f32[1792]{0:T(1024)S(1)}, /*index=5*/f32[512,1792]{0,1:T(8,128)}) fusion(f32[512,1792]{0,1:T(8,128)S(1)} %copy-done.9, f32[3,1792]{0,1:T(8,128)S(1)} %copy-done.43, bf16[512,3352]{0,1:T(8,128)(2,1)S(1)} %copy-done.26, ...), kind=kLoop, calls=%fused_computation.64 | loop fusion | flops 23846144 | bytes 19980288 | tf_op jit(solution)/shard_map/transpose(jvp())/reduce_sum | solution.py:114
  538.5 8.5 %broadcast_multiply_fusion = (f32[512,1792]{0,1:T(8,128)}, f32[512,1792]{0,1:T(8,128)}, f32[512,1792]{0,1:T(8,128)}, f32[512,1792]{0,1:T(8,128)}, f32[512,1792]{...) fusion(f32[512,1792]{0,1:T(8,128)} %get-tuple-element.708, ...), kind=kLoop, calls=%fused_computation.133 | loop fusion | flops 7340032 | bytes 36728832 | tf_op jit(solution)/shard_map/transpose(jvp())/mul | solution.py:114
  561.6 5.0 reduce-window.34
  574.0 5.0 reduce-window.36
  583.6 11.8 %pad_add_fusion.1 = f32[515,1792]{0,1:T(8,128)} fusion(f32[512,1792]{0,1:T(8,128)} %copy-done.15, f32[512,1792]{0,1:T(8,128)} %copy-done.14, f32[512,1792]{0,1:T(8,128)} %copy-done.13, f32[512,1792]{0,1:T(8,128)} %copy-done.16), kind=kLoop, calls=%fused_computation.46 | loop fusion | flops 2768640 | bytes 18371584 | tf_op jit(solution)/shard_map/transpose(jvp())/add_any | solution.py:112
  595.4 7.7 pad_add_fusion
  615.4 9.9 %convolution_add_fusion = f32[768,3352]{1,0:T(8,128)} fusion(f32[768,3352]{1,0:T(8,128)S(1)} %fusion.71, bf16[512,24]{0,1:T(8,128)(2,1)S(1)} %get-tuple-element.704, bf16[512,1792]{0,1:T(8,128)(2,1)S(1)} %fusion.20, bf16[512,1536]{0,1:T(8,128)(2,1)S(1)} %copy-done.54, f32[512]{0:T(512)S(1)} %copy-done.104, f32[768]{0:T(1024)S(1)} %copy-done.92, ...), kind=kOutput, calls=%fused_computation.26 | convolution fusion | flops 2650564608 | bytes 25139200 | tf_op jit(solution)/shard_map/td,tp->dp/dot_general | solution.py:292
  637.6 5.3 fusion.41
  642.8 42.0 %all-reduce.43 = (f32[768]{0:T(1024)}, f32[4,1792]{1,0:T(4,128)}, f32[1792]{0:T(1024)}, f32[24]{0:T(128)}, f32[24]{0:T(128)}, /*index=5*/f32[24]{0:T(128)}, f32[1536]{0:T(1024)}) all-reduce(f32[768]{0:T(1024)S(1)} %add.491, f32[4,1792]{1,0:T(4,128)S(1)} %add_add_fusion.4, ...), channel_id=1, replica_groups=mesh['fsdp'=16,'seq'=2] {'fsdp','seq'}, use_global_device_ids=true, to_apply=%region_58.60 | all-reduce | flops 11336 | bytes 90688 | tf_op jit(solution)/shard_map/psum | solution.py:307
  689.3 77.5 %reduce-scatter.7.cloned.1.call-done = f32[24,3352]{1,0:T(8,128)} async-done(((f32[768,3352]{1,0:T(8,128)}), f32[24,3352]{1,0:T(8,128)}) %reduce-scatter.7.cloned.1.call-update) | async-done | bytes 321808
  (651 shorter events, 304.9 us)
Async XLA Ops:
  7.2 63.7 %all-gather.15.cloned.1.call-start = ((), (), s32[]{:S(2)}) async-start(), calls=%async_computation.4 | async-start | bytes 2433024 | tf_op jit(solution)/shard_map/all_gather | solution.py:223
  7.9 130.4 %all-gather.11.cloned.1.call-start = ((), (), s32[]{:S(2)}) async-start(), calls=%async_computation.2 | async-start | bytes 5474304 | tf_op jit(solution)/shard_map/all_gather | solution.py:222
  8.7 289.3 %all-gather.17.cloned.1.call-start = ((), (), s32[]{:S(2)}) async-start(), calls=%async_computation.5 | async-start | bytes 2359296 | tf_op jit(solution)/shard_map/all_gather | solution.py:28
  11.5 64.4 %copy-start.150 = (f32[512]{0:T(512)}, f32[512]{0:T(512)S(1)}, u32[]{:S(2)}) copy-start(f32[512]{0:T(512)S(1)} %fusion.170) | copy-start | bytes 6148
  13.8 186.8 %copy-start.124 = (f32[1792]{0:T(1024)}, f32[1792]{0:T(1024)S(1)}, u32[]{:S(2)}) copy-start(f32[1792]{0:T(1024)S(1)} %get-tuple-element.652) | copy-start | bytes 21508
  13.8 186.8 %copy-start.126 = (f32[1792]{0:T(1024)}, f32[1792]{0:T(1024)S(1)}, u32[]{:S(2)}) copy-start(f32[1792]{0:T(1024)S(1)} %get-tuple-element.653) | copy-start | bytes 21508
  13.8 186.8 %copy-start.128 = (f32[1792]{0:T(1024)}, f32[1792]{0:T(1024)S(1)}, u32[]{:S(2)}) copy-start(f32[1792]{0:T(1024)S(1)} %get-tuple-element.654) | copy-start | bytes 21508
  13.8 186.8 %copy-start.130 = (f32[1792]{0:T(1024)}, f32[1792]{0:T(1024)S(1)}, u32[]{:S(2)}) copy-start(f32[1792]{0:T(1024)S(1)} %get-tuple-element.655) | copy-start | bytes 21508
  15.6 60.4 %copy-start.152 = (f32[512]{0:T(512)}, f32[512]{0:T(512)S(1)}, u32[]{:S(2)}) copy-start(f32[512]{0:T(512)S(1)} %get-tuple-element.634) | copy-start | bytes 6148
  15.6 60.4 %copy-start.154 = (f32[512]{0:T(512)}, f32[512]{0:T(512)S(1)}, u32[]{:S(2)}) copy-start(f32[512]{0:T(512)S(1)} %get-tuple-element.635) | copy-start | bytes 6148
  16.3 139.6 %copy-start.173 = (f32[24]{0:T(128)}, f32[24]{0:T(128)S(1)}, u32[]{:S(2)}) copy-start(f32[24]{0:T(128)S(1)} %exponential_negate_fusion) | copy-start | bytes 292
  16.3 122.0 %copy-start.106 = (f32[512]{0:T(512)}, f32[512]{0:T(512)S(1)}, u32[]{:S(2)}) copy-start(f32[512]{0:T(512)S(1)} %fusion.172) | copy-start | bytes 6148
  16.3 131.9 %copy-start.103 = (f32[512]{0:T(512)}, f32[512]{0:T(512)S(1)}, u32[]{:S(2)}) copy-start(f32[512]{0:T(512)S(1)} %fusion.174) | copy-start | bytes 6148
  16.3 121.9 %copy-start.23 = (bf16[2,1,512,768]{3,2,1,0:T(8,128)(2,1)S(1)}, bf16[2,1,512,768]{3,2,1,0:T(8,128)(2,1)}, u32[]{:S(2)}) copy-start(bf16[2,1,512,768]{3,2,1,0:T(8,128)(2,1)} %param.21) | copy-start | bytes 4718596
  16.3 121.9 %copy-start.91 = (f32[768]{0:T(1024)S(1)}, f32[768]{0:T(1024)}, u32[]{:S(2)}) copy-start(f32[768]{0:T(1024)} %param.23) | copy-start | bytes 9220
  158.1 22.6 %copy-start.73 = (f32[512,24]{0,1:T(8,128)}, f32[512,24]{0,1:T(8,128)S(1)}, u32[]{:S(2)}) copy-start(f32[512,24]{0,1:T(8,128)S(1)} %get-tuple-element.716) | copy-start | bytes 147460
  158.1 22.6 %copy-start.75 = (f32[512,24]{0,1:T(8,128)}, f32[512,24]{0,1:T(8,128)S(1)}, u32[]{:S(2)}) copy-start(f32[512,24]{0,1:T(8,128)S(1)} %get-tuple-element.792) | copy-start | bytes 147460
  159.2 21.4 %copy-start.77 = (f32[2,24,2,128]{3,1,2,0:T(8,128)}, f32[2,24,2,128]{3,1,2,0:T(8,128)S(1)}, u32[]{:S(2)}) copy-start(f32[2,24,2,128]{3,1,2,0:T(8,128)S(1)} %reduce-window.30) | copy-start | bytes 147460
  159.5 21.2 %copy-start.133 = (f32[2,24,2]{1,2,0:T(2,128)}, f32[2,24,2]{1,2,0:T(2,128)S(1)}, u32[]{:S(2)}) copy-start(f32[2,24,2]{1,2,0:T(2,128)S(1)} %slice.240) | copy-start | bytes 1156
  163.1 36.4 %collective-permute-start = (bf16[3,1792]{0,1:T(8,128)(2,1)S(1)}, bf16[3,1792]{0,1:T(8,128)(2,1)}, u32[]{:S(2)}, u32[]{:S(2)}) collective-permute-start(bf16[3,1792]{0,1:T(8,128)(2,1)S(1)} %copy-done.93), channel_id=1, source_target_pairs={{0,1},{2,3},{4,5},{6,7},{8,9},{10,11},{12,13},{14,15},{16,17},{18,... | collective-permute-start | bytes 32264 | tf_op jit(solution)/shard_map/ppermute | solution.py:23
  166.1 34.5 %collective-permute-start.1 = (bf16[3,1792]{0,1:T(8,128)(2,1)S(1)}, bf16[3,1792]{0,1:T(8,128)(2,1)S(1)}, u32[]{:S(2)}, u32[]{:S(2)}) collective-permute-start(bf16[3,1792]{0,1:T(8,128)(2,1)S(1)} %slice.230), channel_id=1, source_target_pairs={{0,1},{2,3},{4,5},{6,7},{8,9},{10,11},{12,13},{14,15},{16,17},{18,... | collective-permute-start | bytes 32264 | tf_op jit(solution)/shard_map/ppermute | solution.py:23
  167.5 26.4 %copy-start.101 = (f32[2,256,24]{1,2,0:T(8,128)}, f32[2,256,24]{1,2,0:T(8,128)S(1)}, u32[]{:S(2)}) copy-start(f32[2,256,24]{1,2,0:T(8,128)S(1)} %get-tuple-element.768) | copy-start | bytes 147460
  227.0 86.4 %all-gather.13.cloned.1.call-start = ((), (), s32[]{:S(2)}) async-start(), calls=%async_computation.3 | async-start | bytes 2359296 | tf_op jit(solution)/shard_map/all_gather | solution.py:28
  289.3 186.5 %all-gather.19.cloned.1.call-start = ((), (), s32[]{:S(2)}) async-start(), calls=%async_computation.7 | async-start | bytes 2359296 | tf_op jit(solution)/shard_map/all_gather | solution.py:28
  373.6 122.9 %all-gather.21.cloned.1.call-start = ((), (), s32[]{:S(2)}) async-start(), calls=%async_computation.8 | async-start | bytes 2359296 | tf_op jit(solution)/shard_map/all_gather | solution.py:28
  462.1 227.3 %reduce-scatter.5.cloned.1.call-start = ((), (), s32[]{:S(2)}) async-start(), calls=%async_computation.6 | async-start | bytes 4866048 | tf_op jit(solution)/shard_map/reduce_scatter | solution.py:305
  475.7 291.2 %reduce-scatter.7.cloned.1.call-start = ((), (), s32[]{:S(2)}) async-start(), calls=%async_computation.9 | async-start | bytes 10948608
  553.2 51.0 %collective-permute-start.2 = (f32[3,1792]{1,0:T(4,128)S(1)}, f32[3,1792]{1,0:T(4,128)S(1)}, u32[]{:S(2)}, u32[]{:S(2)}) collective-permute-start(f32[3,1792]{1,0:T(4,128)S(1)} %copy.415), channel_id=1, source_target_pairs={{1,0},{3,2},{5,4},{7,6},{9,8},{11,10},{13,12},{15,14},{17,16},{19,... | collective-permute-start | bytes 64520 | tf_op jit(solution)/shard_map/ppermute | solution.py:23
  581.9 22.7 %collective-permute-start.3 = (f32[3,1792]{1,0:T(4,128)S(1)}, f32[3,1792]{1,0:T(4,128)S(1)}, u32[]{:S(2)}, u32[]{:S(2)}) collective-permute-start(f32[3,1792]{1,0:T(4,128)S(1)} %copy.445), channel_id=1, source_target_pairs={{1,0},{3,2},{5,4},{7,6},{9,8},{11,10},{13,12},{15,14},{17,16},{19,... | collective-permute-start | bytes 64520 | tf_op jit(solution)/shard_map/ppermute | solution.py:23
  637.5 47.3 %copy-start.153 = (f32[512]{0:T(512)S(1)}, f32[512]{0:T(512)}, u32[]{:S(2)}) copy-start(f32[512]{0:T(512)} %copy-done.152) | copy-start | bytes 6148
  637.5 47.3 %copy-start.155 = (f32[512]{0:T(512)S(1)}, f32[512]{0:T(512)}, u32[]{:S(2)}) copy-start(f32[512]{0:T(512)} %copy-done.154) | copy-start | bytes 6148
  637.5 47.3 %copy-start.38 = (bf16[2,1,512,768]{3,2,1,0:T(8,128)(2,1)S(1)}, bf16[2,1,512,768]{3,2,1,0:T(8,128)(2,1)}, u32[]{:S(2)}) copy-start(bf16[2,1,512,768]{3,2,1,0:T(8,128)(2,1)} %param.32) | copy-start | bytes 4718596
  (162 other events, 899.2 us)
Sparse Core Ops, SparseCore 0:
  10.9 59.9 all-gather.14
  73.8 64.4 all-gather.10
  227.1 8.6 all-gather.16
  289.4 8.6 all-gather.12
  373.7 8.7 all-gather.18
  462.2 8.5 all-gather.20
  476.9 108.1 reduce-scatter.4
  625.4 141.3 reduce-scatter.6
where the time goes:
time: 784 us; the launch traced here: 774 us
  other arithmetic  205 us (26%)
  waiting for transfers between devices  196 us (25%)
  local copies, waits for them, and re-layouts  147 us (19%)
  matrix products  147 us (19%)
  blocking collectives  45.9 us (6%)
  between operations  17 us (2%)
  starting transfers between devices  16.5 us (2%)
    unnamed x9, waiting for transfers between devices  79 us
    all_gather x1, waiting for transfers between devices, shards(): lax.all_gather(in_weight, ('fsdp', 'seq'), axis=0, tiled=True)  62.3 us
    all_gather x1, waiting for transfers between devices, shards(): lax.all_gather(out_weight, ('fsdp', 'seq'), axis=1, tiled=True)  54.5 us
    psum x1, blocking collectives, shards(): lax.psum(small_acc, ('fsdp', 'seq'))  42 us
    dot_general x4, matrix products, within_part(): within = product(mixing, heads_x)  34.5 us
    convert_element_type x6, other arithmetic, narrow_plain(): value.astype(jnp.bfloat16)  34.2 us
    dot_general x8, matrix products, product_plain(): jnp.matmul(left_op.astype(jnp.bfloat16), right_op.astype(jnp.bfloat16), p...  29.5 us
    another operation x13, other arithmetic  28.8 us
  transfers between devices with their start and end apart: 12, of which 3 were waited for; matrix products, arithmetic and copies ran while one was open for 48% of the time, Pallas kernels for 0%

commit v1 on v0

v1 whole, which is shorter than its diff:
```python
import functools

import jax
import jax.numpy as jnp
from jax import lax
from jax.experimental import pallas as pl
from jax.experimental.pallas import tpu as pltpu
from jax.sharding import PartitionSpec as P

D = 768
HEADS = 24
HEADDIM = 64
NSTATE = 128
CONV = 4
GROUP = 256
INNER = 1536
CONVCH = 1792
PROJ = 3352
EPS = 1e-05

BLOCKS = 3
ROWS = BLOCKS * GROUP
LANES = 128
AT_DT = CONVCH
AT_GATE = CONVCH + LANES
AT_OUT = AT_GATE + INNER
WIDE = AT_OUT + INNER
QUADS = INNER // 256

BF = jnp.bfloat16
F32 = jnp.float32


def dot(a, b):
    return lax.dot_general(a, b, (((1,), (0,)), ((), ())), preferred_element_type=F32)


def dot_nt(a, b):
    return lax.dot_general(a, b, (((1,), (1,)), ((), ())), preferred_element_type=F32)


def sigmoid(v):
    return 0.5 * jnp.tanh(0.5 * v) + 0.5


def halves(v):
    high = v.astype(BF)
    return high, (v - high.astype(F32)).astype(BF)


def side_by_side(v):
    return jnp.concatenate(halves(v), axis=1)


def exact_sum(triangle, v):
    high, rest = halves(v)
    low = (v - high.astype(F32) - rest.astype(F32)).astype(BF)
    parts = dot(triangle, jnp.concatenate([high, rest, low], axis=1))
    return parts[:, :LANES] + parts[:, LANES : 2 * LANES] + parts[:, 2 * LANES :]


def rows_of(b):
    return pl.ds(pl.multiple_of(b * GROUP, GROUP), GROUP)


def quad_of(q):
    return pl.ds(pl.multiple_of(q * 256, 256), 256)


def fold(v):
    total = v[0:8]
    for i in range(1, v.shape[0] // 8):
        total = total + v[8 * i : 8 * i + 8]
    return total


def iota(shape, dim):
    return lax.broadcasted_iota(jnp.int32, shape, dim)


def mixer(
    tok, og, w, norm_gain, convp, headp, innerp,
    mixed, tgrad, wgrad, g_norm, g_conv, g_head, g_inner,
    normed, normed_t, db_t, clow, cout, wide, ssd, dssd, outn, dproj, back, dtb, cumb,
    cut, spread, sco, run1, run2, held, dheld, dst, dqb, halo, halo_next,
    flow, edge_in, state_in, dstate_in, dedge_in, send_sem, recv_sem,
):
    seq = lax.axis_index("seq")
    other = {"seq": 1 - seq}

    barrier = pltpu.get_barrier_semaphore()
    pl.semaphore_signal(barrier, inc=1, device_id=other, device_id_type=pl.DeviceIdType.MESH)
    pl.semaphore_wait(barrier, 1)

    def remote(i, src, dst):
        return pltpu.make_async_remote_copy(
            src_ref=src, dst_ref=dst, send_sem=send_sem.at[i], recv_sem=recv_sem.at[i],
            device_id=other, device_id_type=pl.DeviceIdType.MESH,
        )

    edge_copy = remote(0, clow.at[pl.ds(2 * GROUP - 16, 16), :], edge_in)
    state_copy = remote(1, run2, state_in)
    dstate_copy = remote(2, dheld.at[0], dstate_in)
    dedge_copy = remote(3, halo_next.at[0], dedge_in)

    is_second = (seq == 1).astype(F32)
    is_first = 1.0 - is_second

    def make_spread(q, _):
        shape = (256, 256)
        head = (iota(shape, 1) + q * 256) >> 6
        spread[:, quad_of(q)] = (head == (iota(shape, 0) & 127)).astype(F32).astype(BF)
        return 0

    lax.fori_loop(0, QUADS, make_spread, 0)
    tri_shape = (GROUP, GROUP)
    lower = (iota(tri_shape, 0) >= iota(tri_shape, 1)).astype(F32).astype(BF)
    upper = (iota(tri_shape, 0) <= iota(tri_shape, 1)).astype(F32).astype(BF)
    half = GROUP // 2
    causal = iota((half, half), 0) >= iota((half, half), 1)
    causal_t = iota((half, half), 0) <= iota((half, half), 1)
    first_head = iota((GROUP, LANES), 1) < HEADDIM

    g_norm[...] = jnp.zeros_like(g_norm)
    g_conv[...] = jnp.zeros_like(g_conv)
    g_head[...] = jnp.zeros_like(g_head)
    g_inner[...] = jnp.zeros_like(g_inner)

    def norm_rows(i, _):
        rows = pl.ds(pl.multiple_of(i * 64, 64), 64)
        v = tok[rows, :].astype(F32)
        root = lax.rsqrt(jnp.mean(v * v, axis=1, keepdims=True) + EPS)
        normed[rows, :] = (v * root * norm_gain[...]).astype(BF)
        return 0

    lax.fori_loop(0, ROWS // 64, norm_rows, 0)

    def proj_conv(j, _):
        clow[:, quad_of(j)] = dot(normed[...], w[:, quad_of(j)]).astype(BF)
        return 0

    lax.fori_loop(0, CONVCH // 256, proj_conv, 0)
    edge_copy.start()
    dtb[...] = dot(normed[...], w[:, AT_DT:AT_GATE])

    def turn(b, _):
        rows = rows_of(b)
        normed_t[:, rows] = normed[rows, :].T
        db_t[:, rows] = og[rows, :].T
        return 0

    lax.fori_loop(0, BLOCKS, turn, 0)

    def proj_gate(j, _):
        at = pl.ds(pl.multiple_of(AT_GATE + j * 256, 128), 256)
        wide[:, quad_of(j)] = dot(normed[...], w[:, at])
        return 0

    lax.fori_loop(0, QUADS, proj_gate, 0)

    edge_copy.wait()
    halo[0] = edge_in[8:16, :].astype(F32) * is_second
    halo[1] = clow[GROUP - 16 : GROUP, :].astype(F32)[8:16]
    halo[2] = jnp.zeros((8, CONVCH), F32)

    def conv_acc(values, before, cols):
        rows = values.shape[0]
        ext = jnp.concatenate([before, values], axis=0)
        shifted = [ext[5 + k : 5 + k + rows] for k in range(CONV)]
        acc = convp[4:5, cols]
        for k in range(CONV):
            acc = acc + convp[k : k + 1, cols] * shifted[k]
        return acc, shifted

    def head_rows(b):
        z = dtb[rows_of(b), :] + headp[0:1, :]
        step = jnp.maximum(z, 0.0) + jnp.log1p(jnp.exp(-jnp.abs(z)))
        return z, step

    def shifted_log(cum, step):
        return cum - jnp.log(jnp.maximum(step, 1e-37))

    def to_first(v, q):
        return pltpu.roll(v, lax.rem(LANES - 4 * q, LANES), 1)

    def forward_block(b, with_states):
        rows = rows_of(b)

        def conv_cols(c, _):
            cols = pl.ds(pl.multiple_of(c * LANES, LANES), LANES)
            acc, _ = conv_acc(clow[rows, cols].astype(F32), halo[b, :, cols], cols)
            cout[rows, cols] = (acc * sigmoid(acc)).astype(BF)
            return 0

        lax.fori_loop(0, CONVCH // LANES, conv_cols, 0)

        z, step = head_rows(b)
        cum = exact_sum(lower, step * -jnp.exp(headp[1:2, :]))
        cumb[rows, :] = cum
        total = cum[GROUP - 1 : GROUP, :]
        moved_t = shifted_log(cum, step).T
        for q in range(QUADS):
            cut[q, 0:4, :] = moved_t[4 * q : 4 * q + 4, :]
        weight = side_by_side(jnp.exp(total - cum) * step)
        key = cout[rows, INNER : INNER + NSTATE]
        query = cout[rows, INNER + NSTATE :]
        key_t = key.T
        sco[...] = dot_nt(query, key)

        def quad(q, _):
            cols = quad_of(q)
            xq = cout[rows, cols]
            if with_states:
                scaled = (xq.astype(F32) * dot(weight, spread[:, cols])).astype(BF)
                part = dot(key_t, scaled)
                if with_states == 1:
                    run1[:, cols] = part
                else:
                    run2[:, cols] = part
            near = to_first(cum, q)
            skip = innerp[1:2, cols]
            for j in range(2):
                lanes = slice(j * LANES, (j + 1) * LANES)
                xp = xq[:, lanes]
                zero = jnp.zeros_like(xp)
                x_ab = (jnp.where(first_head, xp, zero), jnp.where(first_head, zero, xp))
                top, bottom = [], []
                for e in range(2):
                    h = 2 * j + e
                    col_top, col_bottom = near[:half, h : h + 1], near[half:, h : h + 1]
                    row = cut[q, h : h + 1, :]
                    row_left, row_right = row[:, :half], row[:, half:]
                    gap = jnp.where(causal, col_top - row_left, -1e30)
                    top.append((sco[:half, :half] * jnp.exp(gap)).astype(BF))
                    bottom.append((sco[half:, :half] * jnp.exp(col_bottom - row_left)).astype(BF))
                    gap = jnp.where(causal, col_bottom - row_right, -1e30)
                    bottom.append((sco[half:, half:] * jnp.exp(gap)).astype(BF))
                out_top = dot(
                    jnp.concatenate(top, axis=1), jnp.concatenate([v[:half] for v in x_ab], axis=0)
                )
                out_bottom = dot(jnp.concatenate(bottom, axis=1), jnp.concatenate(x_ab, axis=0))
                place = pl.ds(pl.multiple_of(q * 256 + j * LANES, LANES), LANES)
                xf = xp.astype(F32) * skip[:, lanes]
                top_rows = pl.ds(pl.multiple_of(b * GROUP, GROUP), half)
                bottom_rows = pl.ds(pl.multiple_of(b * GROUP + half, half), half)
                ssd[top_rows, place] = out_top + xf[:half]
                ssd[bottom_rows, place] = out_bottom + xf[half:]
            return 0

        lax.fori_loop(0, QUADS, quad, 0)

    def decay_of(b):
        last = cumb[pl.ds(b * GROUP + GROUP - 8, 8), :]
        return dot(side_by_side(jnp.exp(last)), spread[...])[7:8, :]

    forward_block(0, 1)
    forward_block(1, 2)
    decay_0, decay_1 = decay_of(0), decay_of(1)
    run2[...] = run2[...] + decay_1 * run1[...]
    state_copy.start()
    forward_block(2, 0)
    state_copy.wait()

    entry = state_in[...] * is_second
    held[0] = entry.astype(BF)
    state_in[...] = entry
    run1[...] = run1[...] + decay_0 * state_in[...]
    held[1] = run1[...].astype(BF)
    run2[...] = entry

    def carry_block(b, _):
        rows = rows_of(b)
        query = cout[rows, INNER + NSTATE :]
        fade = side_by_side(jnp.exp(cumb[rows, :]))

        def quad(q, _):
            cols = quad_of(q)
            ssd[rows, cols] += dot(query, held[b, :, cols]) * dot(fade, spread[:, cols])
            return 0

        return lax.fori_loop(0, QUADS, quad, 0)

    lax.fori_loop(0, 2, carry_block, 0)

    gain = innerp[0:1, :]

    def gate_block(b, _):
        rows = rows_of(b)

        def grad_quad(q, _):
            at = pl.ds(pl.multiple_of(AT_OUT + q * 256, 128), 256)
            back[0:GROUP, quad_of(q)] = dot(og[rows, :], w[:, at])
            return 0

        lax.fori_loop(0, QUADS, grad_quad, 0)

        def gate_rows(i, _):
            here = pl.ds(pl.multiple_of(b * GROUP + i * 16, 16), 16)
            d_out = back[pl.ds(pl.multiple_of(i * 16, 16), 16), 0:INNER]
            g, s = wide[here, 0:INNER], ssd[here, :]
            sg = sigmoid(g)
            silu = g * sg
            gated = s * silu
            root = lax.rsqrt(jnp.mean(gated * gated, axis=1, keepdims=True) + EPS)
            v = gated * root
            outn[here, :] = (v * gain).astype(BF)
            g_inner[0:8, :] += fold(d_out * v)
            a = gain * d_out
            d_gated = root * (a - v * jnp.mean(v * a, axis=1, keepdims=True))
            d_s = (d_gated * silu).astype(BF)
            dssd[here, :] = d_s
            g_inner[8:16, :] += fold(d_s.astype(F32) * cout[here, 0:INNER].astype(F32))
            dproj[here, AT_GATE:AT_OUT] = (d_gated * s * (sg * (1.0 + g * (1.0 - sg)))).astype(BF)
            return 0

        return lax.fori_loop(0, GROUP // 16, gate_rows, 0)

    lax.fori_loop(0, BLOCKS, gate_block, 0)

    def state_back(b, _):
        rows = rows_of(b)
        query_t = cout[rows, INNER + NSTATE :].T
        fade = side_by_side(jnp.exp(cumb[rows, :]))

        def quad(q, dq):
            cols = quad_of(q)
            dz = (dot(fade, spread[:, cols]) * dssd[rows, cols].astype(F32)).astype(BF)
            dheld[b, :, cols] = dot(query_t, dz)
            return dq + dot_nt(dz, held[b, :, cols])

        dqb[rows, :] = lax.fori_loop(0, QUADS, quad, jnp.zeros((GROUP, NSTATE), F32))
        return 0

    lax.fori_loop(0, 2, state_back, 0)
    dqb[2 * GROUP :, :] = jnp.zeros((GROUP, NSTATE), F32)
    dheld[0] = dheld[0] + decay_0 * dheld[1]
    dstate_copy.start()

    def out_block(b, _):
        rows = rows_of(b)
        branch = dot_nt(outn[rows, :], w[:, AT_OUT:])
        mixed[rows, :] = (tok[rows, :].astype(F32) + branch).astype(BF)
        return 0

    lax.fori_loop(0, BLOCKS, out_block, 0)

    def out_grad_quad(q, _):
        at = pl.ds(pl.multiple_of(AT_OUT + q * 256, 128), 256)
        wgrad[:, at] = dot(db_t[...], outn[:, quad_of(q)]).astype(BF)
        return 0

    lax.fori_loop(0, QUADS, out_grad_quad, 0)

    def backward_block(b, state):
        rows = rows_of(b)
        z, step = head_rows(b)
        cum = cumb[rows, :]
        total = cum[GROUP - 1 : GROUP, :]
        moved = shifted_log(cum, step)
        cum_t = cum.T
        for q in range(QUADS):
            cut[q, 0:4, :] = cum_t[4 * q : 4 * q + 4, :]
        weight = side_by_side(jnp.exp(total - cum) * step)
        key = cout[rows, INNER : INNER + NSTATE]
        query = cout[rows, INNER + NSTATE :]
        sco[...] = dot_nt(key, query)
        ds = back.at[0:GROUP, INNER : INNER + 256]
        ds[...] = jnp.zeros((GROUP, GROUP), F32)

        def quad(q, carry):
            dk, give, take = carry
            cols = quad_of(q)
            xq = cout[rows, cols]
            dq4 = dssd[rows, cols]
            skip = innerp[1:2, cols]
            if state is not None:
                spread_w = dot(weight, spread[:, cols])
                d_states = dst[state, :, cols]
                dx_state = spread_w * dot(key, d_states)
                flow[0:8, cols] = fold(xq.astype(F32) * dx_state)
                dk = dk + dot_nt((xq.astype(F32) * spread_w).astype(BF), d_states)
            near = to_first(moved, q)
            for j in range(2):
                lanes = slice(j * LANES, (j + 1) * LANES)
                xp, dp = xq[:, lanes], dq4[:, lanes]
                zero = jnp.zeros_like(xp)
                d_ab = (jnp.where(first_head, dp, zero), jnp.where(first_head, zero, dp))
                top, bottom = [], []
                for e in range(2):
                    h = 2 * j + e
                    dm_top = dot_nt(xp[:half], d_ab[e])
                    dm_bottom = dot_nt(xp[half:], d_ab[e][half:])
                    col_top, col_bottom = near[:half, h : h + 1], near[half:, h : h + 1]
                    row = cut[q, h : h + 1, :]
                    row_left, row_right = row[:, :half], row[:, half:]
                    fade = jnp.exp(jnp.where(causal_t, row_left - col_top, -1e30))
                    ds[:half, :half] += dm_top[:, :half] * fade
                    top.append((sco[:half, :half] * fade).astype(BF))
                    fade = jnp.exp(row_right - col_top)
                    ds[:half, half:] += dm_top[:, half:] * fade
                    top.append((sco[:half, half:] * fade).astype(BF))
                    fade = jnp.exp(jnp.where(causal_t, row_right - col_bottom, -1e30))
                    ds[half:, half:] += dm_bottom * fade
                    bottom.append((sco[half:, half:] * fade).astype(BF))
                dx_top = dot(jnp.concatenate(top, axis=1), jnp.concatenate(d_ab, axis=0))
                dx_bottom = dot(
                    jnp.concatenate(bottom, axis=1),
                    jnp.concatenate([v[half:] for v in d_ab], axis=0),
                )
                dxp = jnp.concatenate([dx_top, dx_bottom], axis=0)
                if state is not None:
                    dxp = dxp + dx_state[:, lanes]
                place = pl.ds(pl.multiple_of(q * 256 + j * LANES, LANES), LANES)
                xf, df = xp.astype(F32), dp.astype(F32)
                kept = skip[:, lanes]
                pick = (
                    iota((2 * LANES, LANES), 1)
                    == 4 * q + 2 * j + ((iota((2 * LANES, LANES), 0) & 127) >> 6)
                )
                pick = pick.astype(F32).astype(BF)
                give = give + dot(side_by_side(xf * dxp), pick)
                take = take + dot(side_by_side(df * (ssd[rows, place] - kept * xf)), pick)
                wide[rows, place] = dxp + kept * df
            return dk, give, take

        nothing = jnp.zeros((GROUP, LANES), F32)
        dk, give, take = lax.fori_loop(0, QUADS, quad, (nothing, nothing, nothing))
        d_scores = ds[...].astype(BF)
        wide[rows, INNER : INNER + NSTATE] = dk + dot(d_scores, query)
        wide[rows, INNER + NSTATE : CONVCH] = dqb[rows, :] + dot(d_scores.T, key)

        back_sum = exact_sum(upper, take - give)
        if state is not None:
            summed = jnp.sum(flow[...], axis=0, keepdims=True)
            if state == 1:
                kept = jnp.sum(run1[...] * dstate_in[...], axis=0, keepdims=True)
                summed = summed + decay_1 * kept
            else:
                kept = jnp.sum(run2[...] * state_in[...], axis=0, keepdims=True)
                summed = summed + decay_0 * kept
            high, low = halves(jnp.broadcast_to(summed, (8, INNER)))
            by_head = dot_nt(high, spread[0:LANES, :]) + dot_nt(low, spread[0:LANES, :])
            back_sum = back_sum + by_head[0:1, :]
        rate = -jnp.exp(headp[1:2, :])
        sg = sigmoid(z)
        ratio = jnp.where(z < -15.0, 1.0, sg / jnp.maximum(step, 1e-37))
        d_pre = give * ratio + rate * back_sum * sg
        g_head[0:8, :] += fold(d_pre)
        g_head[8:16, :] += fold(back_sum * (step * rate))
        dproj[rows, AT_DT:AT_GATE] = d_pre.astype(BF)

    backward_block(2, None)
    dstate_copy.wait()
    dstate_in[...] = dstate_in[...] * is_first
    dst[1] = dstate_in[...].astype(BF)
    state_in[...] = dheld[1] + decay_1 * dstate_in[...]
    dst[0] = state_in[...].astype(BF)
    backward_block(1, 1)
    backward_block(0, 0)

    def edge_cols(c, _):
        cols = pl.ds(pl.multiple_of(c * LANES, LANES), LANES)
        for b in range(2):
            first = clow[b * GROUP : b * GROUP + 16, cols].astype(F32)
            acc, _ = conv_acc(first, halo[b, :, cols], cols)
            sg = sigmoid(acc)
            d_acc = wide[b * GROUP : b * GROUP + 16, cols] * (sg * (1.0 + acc * (1.0 - sg)))
            halo_next[b, :, cols] = d_acc[0:8]
        return 0

    lax.fori_loop(0, CONVCH // LANES, edge_cols, 0)
    halo_next[2] = jnp.zeros((8, CONVCH), F32)
    dedge_copy.start()

    def conv_back(b, after):
        rows = rows_of(b)

        def conv_cols(c, _):
            cols = pl.ds(pl.multiple_of(c * LANES, LANES), LANES)
            acc, shifted = conv_acc(clow[rows, cols].astype(F32), halo[b, :, cols], cols)
            sg = sigmoid(acc)
            d_acc = wide[rows, cols] * (sg * (1.0 + acc * (1.0 - sg)))
            for k in range(CONV):
                g_conv[8 * k : 8 * k + 8, cols] += fold(d_acc * shifted[k])
            g_conv[32:40, cols] += fold(d_acc)
            ext = jnp.concatenate([d_acc, after[:, cols]], axis=0)
            d_in = convp[3:4, cols] * d_acc
            for k in range(CONV - 1):
                d_in = d_in + convp[k : k + 1, cols] * ext[3 - k : 3 - k + GROUP]
            dproj[rows, cols] = d_in.astype(BF)
            return 0

        lax.fori_loop(0, CONVCH // LANES, conv_cols, 0)

    conv_back(2, halo_next.at[2])
    conv_back(0, halo_next.at[1])
    dedge_copy.wait()
    dedge_in[...] = dedge_in[...] * is_first
    conv_back(1, dedge_in)

    def in_grad_quad(j, _):
        wgrad[:, quad_of(j)] = dot(normed_t[...], dproj[:, quad_of(j)]).astype(BF)
        return 0

    lax.fori_loop(0, AT_OUT // 256, in_grad_quad, 0)
    last = slice(AT_OUT - 128, AT_OUT)
    wgrad[:, last] = dot(normed_t[...], dproj[:, last]).astype(BF)

    def in_block(b, _):
        rows = rows_of(b)
        tgrad[rows, :] = dot_nt(dproj[rows, :], w[:, 0:AT_OUT])
        return 0

    lax.fori_loop(0, BLOCKS, in_block, 0)

    def norm_back(i, _):
        rows = pl.ds(pl.multiple_of(i * 32, 32), 32)
        v = tok[rows, :].astype(F32)
        root = lax.rsqrt(jnp.mean(v * v, axis=1, keepdims=True) + EPS)
        y = v * root
        dn = tgrad[rows, :]
        g_norm[...] += fold(dn * y)
        bb = norm_gain[...] * dn
        d_v = root * (bb - y * jnp.mean(y * bb, axis=1, keepdims=True))
        tgrad[rows, :] = og[rows, :].astype(F32) + d_v
        return 0

    lax.fori_loop(0, ROWS // 32, norm_back, 0)


def call_mixer(tok, og, w, norm_gain, convp, headp, innerp):
    vmem = pl.BlockSpec(memory_space=pltpu.VMEM)
    outs = (
        ((ROWS, D), BF), ((ROWS, D), F32), ((D, WIDE), BF), ((8, D), F32),
        ((40, CONVCH), F32), ((16, LANES), F32), ((16, INNER), F32),
    )
    scratch = (
        ((ROWS, D), BF), ((D, ROWS), BF), ((D, ROWS), BF), ((ROWS, CONVCH), BF),
        ((ROWS, CONVCH), BF), ((ROWS, CONVCH), F32), ((ROWS, INNER), F32), ((ROWS, INNER), BF),
        ((ROWS, INNER), BF), ((ROWS, AT_OUT), BF), ((GROUP, CONVCH), F32), ((ROWS, LANES), F32),
        ((ROWS, LANES), F32), ((QUADS, 8, GROUP), F32), ((256, INNER), BF), ((GROUP, GROUP), F32),
        ((NSTATE, INNER), F32), ((NSTATE, INNER), F32), ((2, NSTATE, INNER), BF),
        ((2, NSTATE, INNER), F32), ((2, NSTATE, INNER), BF), ((ROWS, NSTATE), F32),
        ((3, 8, CONVCH), F32), ((3, 8, CONVCH), F32), ((8, INNER), F32), ((16, CONVCH), BF), ((NSTATE, INNER), F32),
        ((NSTATE, INNER), F32), ((8, CONVCH), F32),
    )
    return pl.pallas_call(
        mixer,
        out_shape=[jax.ShapeDtypeStruct(s, t) for s, t in outs],
        in_specs=[vmem] * 7,
        out_specs=[vmem] * len(outs),
        scratch_shapes=[pltpu.VMEM(s, t) for s, t in scratch]
        + [pltpu.SemaphoreType.DMA((4,)), pltpu.SemaphoreType.DMA((4,))],
        compiler_params=pltpu.CompilerParams(
            collective_id=0, has_side_effects=True, vmem_limit_bytes=62 * 1024 * 1024
        ),
        name="mixer",
    )(tok, og, w, norm_gain, convp, headp, innerp)


def shards(
    tokens, lengths, norm_gain, in_weight, conv_weight, conv_bias, dt_bias, a_log, skip_gain,
    out_gain, out_weight, out_grad,
):
    both = ("fsdp", "seq")
    row_count = tokens.shape[2]
    positions = lax.axis_index("seq") * row_count + jnp.arange(row_count, dtype=jnp.int32)
    first_long = lengths[0, 0] > lengths[1, 0]
    short_valid = (positions < jnp.minimum(lengths[0, 0], lengths[1, 0]))[:, None]

    def packed(a):
        return jnp.concatenate(
            [jnp.where(first_long, a[0, 0], a[1, 0]),
             jnp.where(first_long, a[1, 0, :GROUP], a[0, 0, :GROUP])], axis=0)

    tok = packed(tokens)
    og = packed(out_grad)
    mask = jnp.concatenate([jnp.ones((row_count, 1), bool), short_valid[:GROUP]], axis=0)
    og = jnp.where(mask, og, jnp.zeros_like(og))
    own = in_weight.shape[0]
    sent = jnp.concatenate(
        [in_weight[:, INNER:], jnp.zeros((own, LANES - HEADS), BF), in_weight[:, :INNER],
         out_weight.T], axis=1)
    w = lax.all_gather(sent, both, axis=0, tiled=True)
    convp = jnp.concatenate([conv_weight, conv_bias[None], jnp.zeros((3, CONVCH), F32)], axis=0)
    headp = jnp.pad(jnp.stack([dt_bias, a_log]), ((0, 6), (0, LANES - HEADS)))
    innerp = jnp.pad(jnp.stack([out_gain, jnp.repeat(skip_gain, HEADDIM)]), ((0, 6), (0, 0)))
    mixed, tgrad, wgrad, g_norm, g_conv, g_head, g_inner = call_mixer(
        tok, og, w, norm_gain[None], convp, headp, innerp
    )
    summed = lax.psum_scatter(wgrad, both, scatter_dimension=0, tiled=True).astype(F32)
    in_grad = jnp.concatenate(
        [summed[:, AT_GATE:AT_OUT], summed[:, :CONVCH], summed[:, AT_DT : AT_DT + HEADS]], axis=1
    )
    out_w_grad = summed[:, AT_OUT:].T
    small = (
        g_norm.sum(0), g_conv.reshape(5, 8, CONVCH).sum(1), g_head.reshape(2, 8, LANES).sum(1),
        g_inner.reshape(2, 8, INNER).sum(1),
    )
    norm_grad, conv_g, head_g, inner_g = lax.psum(small, both)

    def unpacked(a):
        long = a[:row_count]
        short = jnp.where(short_valid, jnp.pad(a[row_count:], ((0, row_count - GROUP), (0, 0))), 0)
        short = short.astype(a.dtype)
        return jnp.stack([jnp.where(first_long, long, short), jnp.where(first_long, short, long)])[
            :, None
        ]

    return (
        unpacked(mixed), unpacked(tgrad), norm_grad, in_grad, conv_g[:4], conv_g[4],
        head_g[0, :HEADS], head_g[1, :HEADS],
        inner_g[1].reshape(HEADS, HEADDIM).sum(1), inner_g[0], out_w_grad,
    )


def solution(mesh):
    spread = P(None, "fsdp", "seq", None)
    both = ("fsdp", "seq")
    return jax.shard_map(
        shards,
        mesh=mesh,
        in_specs=(
            spread, P(None, "fsdp"), P(), P(both, None), P(), P(), P(), P(), P(), P(),
            P(None, both), spread,
        ),
        out_specs=(
            spread, spread, P(), P(both, None), P(), P(), P(), P(), P(), P(), P(None, both),
        ),
        check_vma=False,
    )
```

time: 784 us -> 325 us (0.41); the launches traced: 774 us -> 324 us
  other arithmetic: 205 us -> 16.7 us
  matrix products: 147 us -> 0 us
  local copies, waits for them, and re-layouts: 147 us -> 16.7 us
  Pallas kernels: 0 us -> 110 us
  waiting for transfers between devices: 196 us -> 123 us
  starting transfers between devices: 16.5 us -> 0.08 us
    dot_general x36 -> x0, matrix products: 147 us -> none  [the longest x4 34.5 us: within_part(): within = product(mixing, heads_x)]
    pallas_call x0 -> x1, Pallas kernels: none -> 110 us  [call_mixer(): pl.pallas_call(mixer, out_shape=[jax.ShapeDtypeStruct(s, t) for s, t in o...]
    reshape x44 -> x0, local copies, waits for them, and re-layouts: 66.9 us -> none  [the longest x4 14.7 us: group_local(): x_blocks = conv_out[:, :INNER].reshape(blocks, GROUP, INNER)]
    reduce_sum x25 -> x5, other arithmetic: 58.5 us -> 4.69 us  [the longest x1 1.65 us: shards(): g_conv.reshape(5, 8, CONVCH).sum(1)]
    all_gather x6 -> x1, waiting for transfers between devices: 117 us -> 63.9 us  [shards(): w = lax.all_gather(sent, both, axis=0, tiled=True)]
    convert_element_type x20 -> x1, other arithmetic: 51.3 us -> 0.97 us  [shards(): lax.psum_scatter(wgrad, both, scatter_dimension=0, tiled=True).astype(F32)]
    another operation x14 -> x4, other arithmetic: 31.4 us -> 2.52 us  [the longest x1 1.27 us: shards(): headp = jnp.pad(jnp.stack([dt_bias, a_log]), ((0, 6), (0, LANES - HEADS)))]
    unnamed x364 -> x18, local copies, waits for them, and re-layouts: 24.3 us -> 0.04 us
  transfers between devices with their start and end apart: 12 -> 2, of which waited for: 3 -> 2; matrix products, arithmetic and copies ran while one was open for 48% -> 8% of each run, Pallas kernels for 0% -> 0%
where the time goes in v1:
time: 325 us; the launch traced here: 324 us
  waiting for transfers between devices  123 us (38%)
  Pallas kernels  110 us (34%)
  blocking collectives  40.8 us (13%)
  between operations  16.8 us (5%)
  local copies, waits for them, and re-layouts  16.7 us (5%)
  other arithmetic  16.7 us (5%)
    pallas_call x1, Pallas kernels, call_mixer(): pl.pallas_call(mixer, out_shape=[jax.ShapeDtypeStruct(s, t) for s, t in o...  110 us
    all_gather x1, waiting for transfers between devices, shards(): w = lax.all_gather(sent, both, axis=0, tiled=True)  63.9 us
    unnamed x3, waiting for transfers between devices  58.9 us
    psum x1, blocking collectives, shards(): norm_grad, conv_g, head_g, inner_g = lax.psum(small, both)  40.8 us
  transfers between devices with their start and end apart: 2, of which 2 were waited for; matrix products, arithmetic and copies ran while one was open for 8% of the time, Pallas kernels for 0%

profile of v1, /device:TPU:0, one launch (start us, length us, event | category | flops | bytes accessed | tf_op | source)
XLA Modules:
  0.0 324.4 jit_solution(17086061759969716966)
XLA Ops:
  7.2 0.9 slice.98
  8.1 0.9 slice.97
  9.0 1.8 concatenate.22
  10.9 1.3 fusion
  14.9 1.3 broadcast_in_dim.62.norm_gain
  16.2 0.7 stack.36
  16.9 0.7 broadcast_in_dim.63
  17.6 0.7 broadcast_in_dim.65
  18.5 1.3 select_maximum_fusion.1.headp
  19.7 1.4 select_bitcast_fusion.6
  21.4 1.1 pad_maximum_fusion.tok
  23.1 1.3 maximum_select_fusion.og
  24.4 0.7 maximum_maximum_fusion.convp
  25.1 63.9 %all-gather.2.cloned.1.call-done.w = bf16[768,4992]{1,0:T(8,128)(2,1)} async-done(((bf16[24,4992]{1,0:T(8,128)(2,1)}), bf16[768,4992]{1,0:T(8,128)(2,1)}) %all-gather.2.cloned.1.call-update) | async-done | bytes 7667728 | tf_op jit(solution)/shard_map/all_gather | solution.py:584
  89.0 110.5 %mixer.1 = (bf16[768,768]{1,0:T(8,128)(2,1)}, f32[768,768]{1,0:T(8,128)}, bf16[768,4992]{1,0:T(8,128)(2,1)}, f32[8,768]{1,0:T(8,128)}, f32[40,1792]{1,0:T(8,128)...) custom-call(bf16[768,768]{1,0:T(8,128)(2,1)} %pad_maximum_fusion.tok, bf16[768,768]{1,0:T(8,128)(2,1)} %maximum_select_fusion.og, ...), custom_call_target="tpu_custom_call" | custom-call | tf_op jit(solution)/shard_map/mixer/pallas_call | solution.py:547
  199.5 0.9 reduce_sum.45
  201.0 0.9 bitcast_reduce_fusion.1
  201.9 1.7 bitcast_reduce_fusion
  203.6 40.8 %all-reduce.6 = (f32[768]{0:T(1024)}, f32[5,1792]{1,0:T(8,128)}, f32[2,128]{1,0:T(2,128)}, f32[2,1536]{1,0:T(2,128)}) all-reduce(f32[768]{0:T(1024)S(1)} %reduce_sum.45, f32[5,1792]{1,0:T(8,128)} %bitcast_reduce_fusion, f32[2,128]{1,0:T(2,128)} %bitcast_reduce_fusion.2, ...), channel_id=1, replica_groups=mesh['fsdp'=16,'seq'=2] {'fsdp','seq'}, use_global_device_ids=true, to_apply=%region_1.2 | all-reduce | flops 13056 | bytes 104448 | tf_op jit(solution)/shard_map/psum | solution.py:600
  244.4 1.4 slice.114
  245.8 1.4 slice_reduce_fusion.1
  247.2 0.8 reshape_squeeze.3
  248.0 0.6 reduce_sum.49
  248.7 1.4 slice_reduce_fusion
  250.5 1.3 maximum_bitcast_fusion.1
  252.1 1.9 maximum_bitcast_fusion
  254.5 58.8 %reduce-scatter.4.cloned.1.call-done = bf16[24,4992]{1,0:T(8,128)(2,1)} async-done(((bf16[768,4992]{1,0:T(8,128)(2,1)}), bf16[24,4992]{1,0:T(8,128)(2,1)}) %reduce-scatter.4.cloned.1.call-update) | async-done | bytes 239632
  313.3 1.0 convert_element_type.15
  314.3 0.7 slice_bitcast_fusion
  315.0 0.9 slice.112
  315.9 0.9 slice.113
  316.8 0.7 pad_maximum_fusion.1
  (37 shorter events, 2.9 us)
Async XLA Ops:
  7.2 81.8 %all-gather.2.cloned.1.call-start = ((), (), s32[]{:S(2)}) async-start(), calls=%async_computation.1 | async-start | bytes 7907328 | tf_op jit(solution)/shard_map/all_gather | solution.py:584
  9.0 12.2 %copy-start = (bf16[2,1,512,768]{3,2,1,0:T(8,128)(2,1)S(1)}, bf16[2,1,512,768]{3,2,1,0:T(8,128)(2,1)}, u32[]{:S(2)}) copy-start(bf16[2,1,512,768]{3,2,1,0:T(8,128)(2,1)} %param.23) | copy-start | bytes 4718596
  9.0 12.2 %copy-start.1 = (bf16[2,1,512,768]{3,2,1,0:T(8,128)(2,1)S(1)}, bf16[2,1,512,768]{3,2,1,0:T(8,128)(2,1)}, u32[]{:S(2)}) copy-start(bf16[2,1,512,768]{3,2,1,0:T(8,128)(2,1)} %param.12) | copy-start | bytes 4718596
  10.9 302.5 %reduce-scatter.4.cloned.1.call-start = ((), (), s32[]{:S(2)}) async-start(), calls=%async_computation.2 | async-start | bytes 7907328
  14.9 2.7 copy-start.6
  22.5 1.9 copy-start.4
  199.5 1.0 copy-start.5
  199.5 49.2 %copy-start.3 = (bf16[768,768]{1,0:T(8,128)(2,1)S(1)}, bf16[768,768]{1,0:T(8,128)(2,1)}, u32[]{:S(2)}) copy-start(bf16[768,768]{1,0:T(8,128)(2,1)} %get-tuple-element.18) | copy-start | bytes 3538948
  199.5 49.2 %copy-start.2 = (f32[768,768]{1,0:T(8,128)S(1)}, f32[768,768]{1,0:T(8,128)}, u32[]{:S(2)}) copy-start(f32[768,768]{1,0:T(8,128)} %get-tuple-element.19) | copy-start | bytes 7077892
  244.4 5.8 %copy-start.7 = (pred[512]{0:T(512)(128)(4,1)S(1)}, pred[512]{0:T(512)(128)(4,1)}, u32[]{:S(2)}) copy-start(pred[512]{0:T(512)(128)(4,1)} %copy-done.6) | copy-start | bytes 1540
  252.1 1.9 copy-start.8
Sparse Core Ops, SparseCore 0:
  11.5 77.4 all-gather.1
  199.6 113.6 reduce-scatter.3

commit v2 on v1

v2 whole, which is shorter than its diff:
```python
import functools
import types

import jax
import jax.numpy as jnp
from jax import lax
from jax.experimental import pallas as pl
from jax.experimental.pallas import tpu as pltpu
from jax.sharding import PartitionSpec as P

D = 768
HEADS = 24
HEADDIM = 64
NSTATE = 128
CONV = 4
GROUP = 256
INNER = 1536
CONVCH = 1792
PROJ = 3352
EPS = 1e-05

BLOCKS = 3
ROWS = BLOCKS * GROUP
EDGE = 16
LANES = 128
QUADS = INNER // 256
AT_DT = 256
AT_X = 512
AT_GATE = AT_X + INNER
AT_OUT = AT_GATE + INNER
WIDE = AT_OUT + INNER
CX = 2 * NSTATE
CHUNK = 768
CHUNKS = QUADS + 1
SLOTS = 4
GATHERS = ((0, 512), (512, 512), (1024, 1024), (AT_GATE, INNER), (AT_OUT, INNER))
PLANE = 4

BF = jnp.bfloat16
F32 = jnp.float32
MESH = pl.DeviceIdType.MESH


def dot(a, b):
    return lax.dot_general(a, b, (((1,), (0,)), ((), ())), preferred_element_type=F32)


def dot_nt(a, b):
    return lax.dot_general(a, b, (((1,), (1,)), ((), ())), preferred_element_type=F32)


def sigmoid(v):
    return 0.5 * jnp.tanh(0.5 * v) + 0.5


def halves(v):
    high = v.astype(BF)
    return high, (v - high.astype(F32)).astype(BF)


def side_by_side(v):
    return jnp.concatenate(halves(v), axis=1)


def exact_sum(triangle, v):
    high, rest = halves(v)
    low = (v - high.astype(F32) - rest.astype(F32)).astype(BF)
    parts = dot(triangle, jnp.concatenate([high, rest, low], axis=1))
    return parts[:, :LANES] + parts[:, LANES : 2 * LANES] + parts[:, 2 * LANES :]


def span(start, size, multiple=None):
    return pl.ds(pl.multiple_of(start, multiple or size), size)


def rows_of(b):
    return span(b * GROUP, GROUP)


def heads_of(q):
    return span(q * 256, 256)


def fold(v):
    total = v[0:8]
    for i in range(1, v.shape[0] // 8):
        total = total + v[8 * i : 8 * i + 8]
    return total


def iota(shape, dim):
    return lax.broadcasted_iota(jnp.int32, shape, dim)


def loop(count, body):
    def step(i, _):
        body(i)
        return 0

    lax.fori_loop(0, count, step, 0)


def silu_slope(v, sg):
    return sg * (1.0 + v * (1.0 - sg))


def mixer(names, fused, nz, *refs):
    r = types.SimpleNamespace(**dict(zip(names, refs)))
    seq = lax.axis_index("seq")
    f = lax.axis_index("fsdp")
    z_at, p_at = f // PLANE, f % PLANE
    sibling = {"seq": 1 - seq}
    is_second = (seq == 1).astype(F32)
    is_first = 1.0 - is_second

    def plane_peer(j):
        if j == 1:
            return p_at + 1 - 2 * (p_at % 2)
        if j == 2:
            return p_at + 2 - 4 * (p_at // 2)
        return 3 - p_at

    def z_peer(j):
        return (z_at + j + nz) % nz

    def on_plane(j):
        return {"fsdp": z_at * PLANE + plane_peer(j)}

    def on_chain(j):
        return {"fsdp": z_peer(j) * PLANE + p_at}

    peers = [sibling]
    if fused:
        peers += [on_plane(j) for j in range(1, PLANE)] + [on_chain(j) for j in range(1, nz)]
    barrier = pltpu.get_barrier_semaphore()
    for peer in peers:
        pl.semaphore_signal(barrier, inc=1, device_id=peer, device_id_type=MESH)
    pl.semaphore_wait(barrier, len(peers))

    def remote(src, dst, send, recv, device):
        return pltpu.make_async_remote_copy(
            src_ref=src, dst_ref=dst, send_sem=send, recv_sem=recv, device_id=device,
            device_id_type=MESH,
        )

    def pair_copy(i, src, dst):
        return remote(src, dst, r.pair_send.at[i], r.pair_recv.at[i], sibling)

    w = r.w
    own = D // (2 * nz * PLANE) if fused else 0
    slab = 2 * own

    def part(c):
        low, size = GATHERS[c]
        return span(low + seq * (size // 2), size // 2, 128)

    def slab_of(index):
        return span(index * slab, slab, 16)

    def gather_copy(c, k, index, device):
        at = w.at[slab_of(index), part(c)]
        return remote(at, at, r.g_send.at[c, k], r.g_recv.at[c, k], device)

    def chain_copy(c, j):
        return gather_copy(c, j - 1, f, on_chain(j))

    def plane_copy(c, j, back):
        index = (z_at - back + nz) % nz * PLANE + p_at
        return gather_copy(c, nz - 1 + (j - 1) * nz + back, index, on_plane(j))

    def last_copy(c):
        at = w.at[:, part(c)]
        k = nz - 1 + (PLANE - 1) * nz
        return remote(at, at, r.g_send.at[c, k], r.g_recv.at[c, k], sibling)

    def gather_own(c):
        cols = part(c)
        mine, theirs = r.shard[:, cols], r.shard_in[:, cols]
        first = jnp.where(seq == 0, mine, theirs)
        second = jnp.where(seq == 0, theirs, mine)
        w[slab_of(f), cols] = jnp.concatenate([first, second], axis=0).astype(BF)

    def gather_1(c):
        for j in range(1, nz):
            chain_copy(c, j).start()
        for j in range(1, PLANE):
            plane_copy(c, j, 0).start()

    def gather_2(c):
        for back in range(1, nz):
            chain_copy(c, back).wait_recv()
            for j in range(1, PLANE):
                plane_copy(c, j, back).start()

    def gather_3(c):
        for j in range(1, PLANE):
            for back in range(nz):
                plane_copy(c, j, back).wait_recv()
        last_copy(c).start()

    def gather_4(c):
        last_copy(c).wait_recv()

    def gather_end(c):
        for j in range(1, nz):
            chain_copy(c, j).wait_send()
        for j in range(1, PLANE):
            for back in range(nz):
                plane_copy(c, j, back).wait_send()
        last_copy(c).wait_send()

    def size_of(g):
        return 256 if isinstance(g, int) and g == QUADS else CHUNK // 2

    def lanes_of(g, which):
        size = size_of(g)
        return span(which * size, size, 128)

    def place_of(g):
        return g % SLOTS

    def sum_copy_0(g):
        n = size_of(g)
        src = r.wg.at[place_of(g), :, :, :, lanes_of(g, 1 - seq)]
        dst = r.r0.at[g, :, :, :, 0:n]
        return remote(src, dst, r.s_send.at[g, 0], r.s_recv.at[g, 0], sibling)

    def sum_copy_1(g, j):
        n = size_of(g)
        src = r.wg.at[place_of(g), :, plane_peer(j), :, lanes_of(g, seq)]
        dst = r.r1.at[g, j - 1, :, :, 0:n]
        return remote(src, dst, r.s_send.at[g, j], r.s_recv.at[g, j], on_plane(j))

    def sum_copy_2(g, j):
        n = size_of(g)
        k = PLANE - 1 + j
        src = r.wg.at[place_of(g), z_peer(j), p_at, :, lanes_of(g, seq)]
        dst = r.r2.at[g, j - 1, :, 0:n]
        return remote(src, dst, r.s_send.at[g, k], r.s_recv.at[g, k], on_chain(j))

    def sum_copy_3(g):
        n = size_of(g)
        k = PLANE - 1 + nz
        src = r.fin.at[g, span((1 - seq) * own, own, 8), 0:n]
        dst = r.gsum.at[g, :, 0:n]
        return remote(src, dst, r.s_send.at[g, k], r.s_recv.at[g, k], sibling)

    def sum_0(g):
        if fused:
            sum_copy_0(g).start()

    def sum_1(g):
        if not fused:
            return
        copy = sum_copy_0(g)
        copy.wait_send()
        copy.wait_recv()
        n, here, lanes = size_of(g), place_of(g), lanes_of(g, seq)

        def add(i):
            zi, pi = i // PLANE, i % PLANE
            mine = r.wg[here, zi, pi, :, lanes].astype(F32)
            r.wg[here, zi, pi, :, lanes] = (mine + r.r0[g, zi, pi, :, 0:n].astype(F32)).astype(BF)

        loop(nz * PLANE, add)
        for j in (3, 1, 2):
            sum_copy_1(g, j).start()

    def sum_2(g):
        if not fused:
            return
        n, here, lanes = size_of(g), place_of(g), lanes_of(g, seq)
        for j in range(1, PLANE):
            copy = sum_copy_1(g, j)
            copy.wait_send()
            copy.wait_recv()

        def add(zi):
            total = r.wg[here, zi, p_at, :, lanes].astype(F32)
            for j in range(PLANE - 1):
                total = total + r.r1[g, j, zi, :, 0:n].astype(F32)
            r.wg[here, zi, p_at, :, lanes] = total.astype(BF)

        loop(nz, add)
        for j in range(1, nz):
            sum_copy_2(g, j).start()

    def sum_3(g):
        if not fused:
            return
        n, here, lanes = size_of(g), place_of(g), lanes_of(g, seq)
        for j in range(1, nz):
            copy = sum_copy_2(g, j)
            copy.wait_send()
            copy.wait_recv()
        total = r.wg[here, z_at, p_at, :, lanes].astype(F32)
        for j in range(nz - 1):
            total = total + r.r2[g, j, :, 0:n].astype(F32)
        r.fin[g, :, 0:n] = total
        sum_copy_3(g).start()

    def sum_4(g):
        if not fused:
            return
        copy = sum_copy_3(g)
        copy.wait_send()
        copy.wait_recv()

    def put_grad(g, low, value):
        size = value.shape[1]
        if fused:
            parts = value.astype(BF).reshape(nz, PLANE, slab, size)
            r.wg[place_of(g), :, :, :, low : low + size] = parts
        else:
            r.wgrad[:, span(g * CHUNK + low, size, 128)] = value.astype(BF)

    edge_copy = pair_copy(0, r.tok.at[2 * GROUP - EDGE : 2 * GROUP, :], r.edge_in)
    edge_copy.start()
    if fused:
        shard_copy = pair_copy(1, r.shard, r.shard_in)
        shard_copy.start()

    def make_spread(q):
        shape = (256, 256)
        head = (iota(shape, 1) + q * 256) >> 6
        r.spread[:, span(q * 256, 256)] = (head == (iota(shape, 0) & 127)).astype(F32).astype(BF)

    if fused:
        shard_copy.wait()
        for c in range(len(GATHERS)):
            gather_own(c)
            if c < 2:
                gather_1(c)

    loop(QUADS, make_spread)
    tri_shape = (GROUP, GROUP)
    lower = (iota(tri_shape, 0) >= iota(tri_shape, 1)).astype(F32).astype(BF)
    upper = (iota(tri_shape, 0) <= iota(tri_shape, 1)).astype(F32).astype(BF)
    half = GROUP // 2
    causal = iota((half, half), 0) >= iota((half, half), 1)
    causal_t = iota((half, half), 0) <= iota((half, half), 1)
    first_head = iota((GROUP, LANES), 1) < HEADDIM
    rate = -jnp.exp(r.headp[1:2, :])

    r.g_norm[...] = jnp.zeros_like(r.g_norm)
    r.g_conv[...] = jnp.zeros_like(r.g_conv)
    r.g_head[...] = jnp.zeros_like(r.g_head)
    r.g_inner[...] = jnp.zeros_like(r.g_inner)
    r.halo[2] = jnp.zeros((8, CONVCH), F32)
    r.dproj[:, AT_DT + LANES : AT_X] = jnp.zeros((ROWS, AT_X - AT_DT - LANES), BF)

    def norm_of(v):
        root = lax.rsqrt(jnp.mean(v * v, axis=1, keepdims=True) + EPS)
        return (v * root * r.norm_gain[...]).astype(BF)

    def norm_rows(i):
        rows = span(i * 64, 64)
        r.normed[rows, :] = norm_of(r.tok[rows, :].astype(F32))

    loop(ROWS // 64, norm_rows)
    edge_copy.wait()
    r.normed[ROWS:, :] = norm_of(r.edge_in[...].astype(F32) * is_second)

    def turn(b):
        rows = rows_of(b)
        r.normed_t[:, rows] = r.normed[rows, :].T
        r.db_t[:, rows] = r.og[rows, :].T

    loop(BLOCKS, turn)

    if fused:
        gather_2(0)
        gather_2(1)
        gather_1(2)
        gather_3(0)
        gather_4(0)

    def conv_acc(values, before, cols):
        rows = values.shape[0]
        ext = jnp.concatenate([before, values], axis=0)
        shifted = [ext[5 + k : 5 + k + rows] for k in range(CONV)]
        acc = r.convp[4:5, cols]
        for k in range(CONV):
            acc = acc + r.convp[k : k + 1, cols] * shifted[k]
        return acc, shifted

    def project(at, to):
        low = dot(r.normed[...], w[:, at]).astype(BF)
        r.clow[:, to] = low
        r.halo[0, :, to] = low[ROWS : ROWS + EDGE].astype(F32)[EDGE - 8 :]
        r.halo[1, :, to] = low[GROUP - 16 : GROUP].astype(F32)[8:]

    def conv_forward(b, cols):
        rows = rows_of(b)
        acc, _ = conv_acc(r.clow[rows, cols].astype(F32), r.halo[b, :, cols], cols)
        r.cout[rows, cols] = (acc * sigmoid(acc)).astype(BF)

    project(pl.ds(0, CX), pl.ds(0, CX))
    r.dtb[...] = dot(r.normed[0:ROWS, :], w[:, AT_DT : AT_DT + LANES])

    def head_rows(b):
        z = r.dtb[rows_of(b), :] + r.headp[0:1, :]
        step = jnp.maximum(z, 0.0) + jnp.log1p(jnp.exp(-jnp.abs(z)))
        return z, step

    def prepare(b):
        rows = rows_of(b)
        conv_forward(b, pl.ds(0, LANES))
        conv_forward(b, pl.ds(LANES, LANES))
        z, step = head_rows(b)
        cum = exact_sum(lower, step * rate)
        moved = cum - jnp.log(jnp.maximum(step, 1e-37))
        r.cumb[rows, :] = cum
        r.moved[rows, :] = moved
        cum_t, moved_t = cum.T, moved.T
        for q in range(QUADS):
            r.cut[b, q, 0:4, :] = moved_t[4 * q : 4 * q + 4, :]
            r.cut[b, q, 4:8, :] = cum_t[4 * q : 4 * q + 4, :]
        r.weight[rows, :] = side_by_side(jnp.exp(cum[GROUP - 1 : GROUP, :] - cum) * step)
        r.fade[rows, :] = side_by_side(jnp.exp(cum))
        key, query = r.cout[rows, 0:NSTATE], r.cout[rows, NSTATE:CX]
        r.turned[b, 0:NSTATE, :] = key.T
        r.turned[b, NSTATE:CX, :] = query.T
        r.sco[b] = dot_nt(query, key)

    loop(BLOCKS, prepare)

    def to_first(v, q):
        return pltpu.roll(v, (LANES - 4 * q) % LANES, 1)

    def forward_block(b, q):
        rows = rows_of(b)
        cols = span(CX + q * 256, 256)
        heads = span(q * 256, 256)
        for i in range(2):
            conv_forward(b, span(CX + q * 256 + i * LANES, LANES))
        xq = r.cout[rows, cols]

        @pl.when(b < 2)
        def _():
            spread_w = dot(r.weight[rows, :], r.spread[:, heads])
            scaled = (xq.astype(F32) * spread_w).astype(BF)
            r.runs[b, :, heads] = dot(r.turned[b, 0:NSTATE, :], scaled)

        near = to_first(r.cumb[rows, :], q)
        skip = r.innerp[1:2, heads]
        for j in range(2):
            lanes = slice(j * LANES, (j + 1) * LANES)
            xp = xq[:, lanes]
            zero = jnp.zeros_like(xp)
            x_ab = (jnp.where(first_head, xp, zero), jnp.where(first_head, zero, xp))
            top, bottom = [], []
            for e in range(2):
                h = 2 * j + e
                col_top, col_bottom = near[:half, h : h + 1], near[half:, h : h + 1]
                row = r.cut[b, q, h : h + 1, :]
                row_left, row_right = row[:, :half], row[:, half:]
                gap = jnp.where(causal, col_top - row_left, -1e30)
                top.append((r.sco[b, :half, :half] * jnp.exp(gap)).astype(BF))
                fade = jnp.exp(col_bottom - row_left)
                bottom.append((r.sco[b, half:, :half] * fade).astype(BF))
                gap = jnp.where(causal, col_bottom - row_right, -1e30)
                bottom.append((r.sco[b, half:, half:] * jnp.exp(gap)).astype(BF))
            out_top = dot(
                jnp.concatenate(top, axis=1), jnp.concatenate([v[:half] for v in x_ab], axis=0)
            )
            out_bottom = dot(jnp.concatenate(bottom, axis=1), jnp.concatenate(x_ab, axis=0))
            place = span(q * 256 + j * LANES, LANES)
            xf = xp.astype(F32) * skip[:, lanes]
            r.ssd[span(b * GROUP, half), place] = out_top + xf[:half]
            r.ssd[span(b * GROUP + half, half), place] = out_bottom + xf[half:]

    def forward_quad(q):
        if fused:

            @pl.when(q == 0)
            def _():
                gather_3(1)
                gather_2(2)
                gather_1(3)
                gather_4(1)

            @pl.when(q == 1)
            def _():
                gather_3(2)
                gather_1(4)

            @pl.when(q == 2)
            def _():
                gather_4(2)
                gather_2(3)

            @pl.when(q == 3)
            def _():
                gather_2(4)

            @pl.when(q == 4)
            def _():
                gather_3(3)

        project(span(AT_X + q * 256, 256), span(CX + q * 256, 256))
        loop(BLOCKS, lambda b: forward_block(b, q))

    loop(QUADS, forward_quad)

    def decay_of(b):
        last = r.cumb[b * GROUP + GROUP - 8 : (b + 1) * GROUP, :]
        return dot(side_by_side(jnp.exp(last)), r.spread[...])[7:8, :]

    decay_0, decay_1 = decay_of(0), decay_of(1)
    r.runs[1] = r.runs[1] + decay_1 * r.runs[0]
    state_copy = pair_copy(2, r.runs.at[1], r.state_in)
    state_copy.start()
    if fused:
        gather_3(4)
        gather_4(3)

    def carry_block(b):
        rows = rows_of(b)
        query = r.cout[rows, NSTATE:CX]

        def quad(q):
            cols = span(q * 256, 256)
            r.ssd[rows, cols] += dot(query, r.held[b, :, cols]) * dot(
                r.fade[rows, :], r.spread[:, cols]
            )

        loop(QUADS, quad)

    gain = r.innerp[0:1, :]

    def gate_project(b):
        rows = rows_of(b)

        def quad(q):
            cols = span(q * 256, 256)
            r.gate[:, cols] = dot(r.normed[rows, :], w[:, span(AT_GATE + q * 256, 256)])

        loop(QUADS, quad)

    def out_back(b):
        rows = rows_of(b)

        def quad(q):
            cols = span(q * 256, 256)
            r.back[:, cols] = dot(r.og[rows, :], w[:, span(AT_OUT + q * 256, 256)])

        loop(QUADS, quad)

    def gate_block(b):
        def gate_rows(i):
            here = span(b * GROUP + i * 16, 16)
            local = span(i * 16, 16)
            d_out, g, s = r.back[local, :], r.gate[local, :], r.ssd[here, :]
            sg = sigmoid(g)
            silu = g * sg
            gated = s * silu
            root = lax.rsqrt(jnp.mean(gated * gated, axis=1, keepdims=True) + EPS)
            v = gated * root
            r.dproj[here, AT_X:AT_GATE] = (v * gain).astype(BF)
            r.g_inner[0:8, :] += fold(d_out * v)
            a = gain * d_out
            d_gated = root * (a - v * jnp.mean(v * a, axis=1, keepdims=True))
            d_s = (d_gated * silu).astype(BF)
            r.dssd[here, :] = d_s
            r.g_inner[8:16, :] += fold(d_s.astype(F32) * r.cout[here, CX:].astype(F32))
            r.dproj[here, AT_GATE:AT_OUT] = (d_gated * s * silu_slope(g, sg)).astype(BF)

        loop(GROUP // 16, gate_rows)

    gate_project(2)
    if fused:
        gather_4(4)
    out_back(2)
    gate_block(2)
    state_copy.wait()
    r.state_in[...] = r.state_in[...] * is_second
    r.held[0] = r.state_in[...].astype(BF)
    r.runs[0] = r.runs[0] + decay_0 * r.state_in[...]
    r.held[1] = r.runs[0].astype(BF)
    r.runs[1] = r.state_in[...]

    def gate_long(b):
        gate_project(b)
        out_back(b)
        carry_block(b)
        gate_block(b)

    loop(2, gate_long)

    def state_back(b):
        rows = rows_of(b)

        def quad(q, dq):
            cols = span(q * 256, 256)
            spread_f = dot(r.fade[rows, :], r.spread[:, cols])
            dz = (spread_f * r.dssd[rows, cols].astype(F32)).astype(BF)
            r.dheld[b, :, cols] = dot(r.turned[b, NSTATE:CX, :], dz)
            return dq + dot_nt(dz, r.held[b, :, cols])

        r.dqb[rows, :] = lax.fori_loop(0, QUADS, quad, jnp.zeros((GROUP, NSTATE), F32))

    loop(2, state_back)
    r.dqb[2 * GROUP :, :] = jnp.zeros((GROUP, NSTATE), F32)
    r.dheld[0] = r.dheld[0] + decay_0 * r.dheld[1]
    dstate_copy = pair_copy(3, r.dheld.at[0], r.dstate_in)
    dstate_copy.start()

    def out_block(b):
        rows = rows_of(b)
        branch = dot_nt(r.dproj[rows, AT_X:AT_GATE], w[:, AT_OUT:])
        r.normed[rows, :] = (r.tok[rows, :].astype(F32) + branch).astype(BF)

    loop(BLOCKS, out_block)
    mixed_copy = pltpu.make_async_copy(r.normed.at[0:ROWS, :], r.mixed, r.local.at[0])
    mixed_copy.start()

    def ds_of(b):
        return r.back.at[:, heads_of(b)]

    def give_of(b):
        return r.back.at[:, span(CHUNK + b * LANES, LANES)]

    def take_of(b):
        return r.back.at[:, span(CHUNK + (BLOCKS + b) * LANES, LANES)]

    def prepare_back(b):
        rows = rows_of(b)
        r.sco[b] = dot_nt(r.cout[rows, 0:NSTATE], r.cout[rows, NSTATE:CX])
        ds_of(b)[...] = jnp.zeros((GROUP, GROUP), F32)
        nothing = jnp.zeros((GROUP, LANES), F32)
        r.dkb[rows, :] = nothing
        give_of(b)[...] = nothing
        take_of(b)[...] = nothing

    loop(BLOCKS, prepare_back)
    dstate_copy.wait()
    r.dstate_in[...] = r.dstate_in[...] * is_first
    r.dst[1] = r.dstate_in[...].astype(BF)
    r.state_in[...] = r.dheld[1] + decay_1 * r.dstate_in[...]
    r.dst[0] = r.state_in[...].astype(BF)

    def backward_block(b, q):
        rows = rows_of(b)
        heads = span(q * 256, 256)
        xq = r.cout[rows, span(CX + q * 256, 256)]
        dq4 = r.dssd[rows, heads]
        skip = r.innerp[1:2, heads]
        dx, ds = r.gate.at[:, heads_of(b)], ds_of(b)
        give, take = give_of(b), take_of(b)

        @pl.when(b < 2)
        def _():
            spread_w = dot(r.weight[rows, :], r.spread[:, heads])
            d_states = r.dst[b, :, heads]
            dx_state = spread_w * dot(r.cout[rows, 0:NSTATE], d_states)
            r.flow[b, 0:8, heads] = fold(xq.astype(F32) * dx_state)
            r.dkb[rows, :] += dot_nt((xq.astype(F32) * spread_w).astype(BF), d_states)
            dx[...] = dx_state

        @pl.when(b == 2)
        def _():
            dx[...] = jnp.zeros((GROUP, 256), F32)

        near = to_first(r.moved[rows, :], q)
        for j in range(2):
            lanes = slice(j * LANES, (j + 1) * LANES)
            xp, dp = xq[:, lanes], dq4[:, lanes]
            zero = jnp.zeros_like(xp)
            d_ab = (jnp.where(first_head, dp, zero), jnp.where(first_head, zero, dp))
            top, bottom = [], []
            for e in range(2):
                h = 2 * j + e
                dm_top = dot_nt(xp[:half], d_ab[e])
                dm_bottom = dot_nt(xp[half:], d_ab[e][half:])
                col_top, col_bottom = near[:half, h : h + 1], near[half:, h : h + 1]
                row = r.cut[b, q, 4 + h : 5 + h, :]
                row_left, row_right = row[:, :half], row[:, half:]
                fade = jnp.exp(jnp.where(causal_t, row_left - col_top, -1e30))
                ds[:half, :half] += dm_top[:, :half] * fade
                top.append((r.sco[b, :half, :half] * fade).astype(BF))
                fade = jnp.exp(row_right - col_top)
                ds[:half, half:] += dm_top[:, half:] * fade
                top.append((r.sco[b, :half, half:] * fade).astype(BF))
                fade = jnp.exp(jnp.where(causal_t, row_right - col_bottom, -1e30))
                ds[half:, half:] += dm_bottom * fade
                bottom.append((r.sco[b, half:, half:] * fade).astype(BF))
            dx_top = dot(jnp.concatenate(top, axis=1), jnp.concatenate(d_ab, axis=0))
            dx_bottom = dot(
                jnp.concatenate(bottom, axis=1), jnp.concatenate([v[half:] for v in d_ab], axis=0)
            )
            dxp = jnp.concatenate([dx_top, dx_bottom], axis=0) + dx[:, lanes]
            xf, df = xp.astype(F32), dp.astype(F32)
            kept = skip[:, lanes]
            head = 4 * q + 2 * j + ((iota((2 * LANES, LANES), 0) & 127) >> 6)
            pick = (iota((2 * LANES, LANES), 1) == head).astype(F32).astype(BF)
            ssd = r.ssd[rows, span(q * 256 + j * LANES, LANES)]
            give[...] += dot(side_by_side(xf * dxp), pick)
            take[...] += dot(side_by_side(df * (ssd - kept * xf)), pick)
            dx[:, lanes] = dxp + kept * df

    def edge_grad(b, source, cols):
        first = r.clow[b * GROUP : b * GROUP + 16, cols].astype(F32)
        acc, _ = conv_acc(first, r.halo[b, :, cols], cols)
        d_acc = r.gate[0:16, span(b * 256 + source, LANES)] * silu_slope(acc, sigmoid(acc))
        r.halo_next[b, :, cols] = d_acc[0:8]

    def conv_back(b, source, cols, to, after):
        rows = rows_of(b)
        acc, shifted = conv_acc(r.clow[rows, cols].astype(F32), r.halo[b, :, cols], cols)
        d_acc = r.gate[:, span(b * 256 + source, LANES)] * silu_slope(acc, sigmoid(acc))
        for k in range(CONV):
            r.g_conv[8 * k : 8 * k + 8, cols] += fold(d_acc * shifted[k])
        r.g_conv[32:40, cols] += fold(d_acc)
        ext = jnp.concatenate([d_acc, after], axis=0)
        d_in = r.convp[3:4, cols] * d_acc
        for k in range(CONV - 1):
            d_in = d_in + r.convp[k : k + 1, cols] * ext[3 - k : 3 - k + GROUP]
        r.dproj[rows, to] = d_in.astype(BF)

    def edge_copy_back(i, cols):
        src, dst = r.halo_next.at[0, :, cols], r.dedge_in.at[:, cols]
        return remote(src, dst, r.edge_send.at[i], r.edge_recv.at[i], sibling)

    def conv_back_all(i, at, to):
        cols = span(at, 256)

        def chunk(k):
            return k * LANES, span(at + k * LANES, LANES), span(to + k * LANES, LANES)

        for k in range(2):
            edge_grad(0, *chunk(k)[:2])
            edge_grad(1, *chunk(k)[:2])
        edge_copy_back(i, cols).start()
        for k in range(2):
            conv_back(2, *chunk(k), jnp.zeros((8, LANES), F32))
            conv_back(0, *chunk(k), r.halo_next[1, :, chunk(k)[1]])
        edge_copy_back(i, cols).wait()
        for k in range(2):
            conv_back(1, *chunk(k), r.dedge_in[:, chunk(k)[1]] * is_first)

    def backward_quad(q):
        heads = span(q * 256, 256)
        put_grad(q, 512, dot(r.db_t[...], r.dproj[:, span(AT_X + q * 256, 256)]))
        put_grad(q, 256, dot(r.normed_t[...], r.dproj[:, span(AT_GATE + q * 256, 256)]))

        @pl.when(q >= 1)
        def _():
            sum_1(q - 1)

        loop(BLOCKS, lambda b: backward_block(b, q))

        @pl.when(q >= 2)
        def _():
            sum_2(q - 2)

        @pl.when(q >= 3)
        def _():
            sum_3(q - 3)

        conv_back_all(q, CX + q * 256, AT_X + q * 256)
        put_grad(q, 0, dot(r.normed_t[...], r.dproj[:, span(AT_X + q * 256, 256)]))
        sum_0(q)

    loop(QUADS, backward_quad)
    last = QUADS

    def backward_rest(b):
        rows = rows_of(b)
        key, query = r.cout[rows, 0:NSTATE], r.cout[rows, NSTATE:CX]
        d_scores = ds_of(b)[...].astype(BF)
        r.gate[:, span(b * 256, NSTATE, 128)] = r.dkb[rows, :] + dot(d_scores, query)
        r.gate[:, span(b * 256 + NSTATE, NSTATE, 128)] = r.dqb[rows, :] + dot(d_scores.T, key)
        give = give_of(b)[...]
        give_of(b)[...] = exact_sum(upper, take_of(b)[...] - give)
        z, step = head_rows(b)
        ratio = jnp.where(z < -15.0, 1.0, sigmoid(z) / jnp.maximum(step, 1e-37))
        take_of(b)[...] = give * ratio

    loop(BLOCKS, backward_rest)

    def block_total(b, run, grad, decay):
        kept = jnp.sum(run[...] * grad[...], axis=0, keepdims=True)
        summed = jnp.sum(r.flow[b], axis=0, keepdims=True) + decay * kept
        high, low = halves(jnp.broadcast_to(summed, (8, INNER)))
        by_head = dot_nt(high, r.spread[0:LANES, :]) + dot_nt(low, r.spread[0:LANES, :])
        rows = rows_of(b)
        give_of(b)[...] = give_of(b)[...] + by_head[0:1, :]

    block_total(0, r.runs.at[1], r.state_in, decay_0)
    block_total(1, r.runs.at[0], r.dstate_in, decay_1)

    def step_grad(b):
        rows = rows_of(b)
        z, step = head_rows(b)
        back_sum = give_of(b)[...]
        d_pre = take_of(b)[...] + rate * back_sum * sigmoid(z)
        r.g_head[0:8, :] += fold(d_pre)
        r.g_head[8:16, :] += fold(back_sum * (step * rate))
        r.dproj[rows, AT_DT : AT_DT + LANES] = d_pre.astype(BF)

    loop(BLOCKS, step_grad)
    sum_1(last - 1)
    conv_back_all(last, 0, 0)
    put_grad(last, 0, dot(r.normed_t[...], r.dproj[:, 0:AT_X]))
    sum_0(last)
    sum_2(last - 2)
    sum_3(last - 3)

    def in_block(b):
        rows = rows_of(b)
        r.ssd[rows, 0:D] = dot_nt(r.dproj[rows, :], w[:, 0:AT_OUT])

    in_block(2)
    sum_1(last)
    sum_2(last - 1)
    sum_3(last - 2)
    loop(2, in_block)
    sum_2(last)
    sum_3(last - 1)

    def norm_back(i):
        rows = span(i * 32, 32)
        v = r.tok[rows, :].astype(F32)
        root = lax.rsqrt(jnp.mean(v * v, axis=1, keepdims=True) + EPS)
        y = v * root
        dn = r.ssd[rows, 0:D]
        r.g_norm[...] += fold(dn * y)
        bb = r.norm_gain[...] * dn
        d_v = root * (bb - y * jnp.mean(y * bb, axis=1, keepdims=True))
        r.ssd[rows, 0:D] = r.og[rows, :].astype(F32) + d_v

    loop(ROWS // 32, norm_back)
    tgrad_copy = pltpu.make_async_copy(r.ssd.at[:, 0:D], r.tgrad, r.local.at[1])
    tgrad_copy.start()

    def total(v):
        return jnp.sum(v, axis=0, keepdims=True)

    for k in range(CONV + 1):
        r.small[0, k : k + 1, :] = total(r.g_conv[8 * k : 8 * k + 8, :])
    r.small[0, 5:6, 0:INNER] = total(r.g_inner[0:8, :])
    r.small[0, 5:6, INNER : INNER + LANES] = total(r.g_head[0:8, :])
    r.small[0, 5:6, INNER + LANES :] = total(r.g_head[8:16, :])
    r.small[0, 6:7, 0:INNER] = total(r.g_inner[8:16, :])
    r.small[0, 6:7, INNER:] = jnp.zeros((1, CX), F32)
    r.small[0, 7:8, 0:D] = total(r.g_norm[...])
    r.small[0, 7:8, D:] = jnp.zeros((1, CONVCH - D), F32)
    if fused:

        def exchange(level, first, count, device):
            copies = []
            for j in range(count):
                k = first + j
                copy = remote(
                    r.small.at[level], r.small_in.at[k], r.t_send.at[k], r.t_recv.at[k],
                    device(j + 1),
                )
                copy.start()
                copies.append(copy)
            for copy in copies:
                copy.wait()
            value = r.small[level]
            for j in range(count):
                value = value + r.small_in[first + j]
            return value

        r.small[1] = exchange(0, 0, 1, lambda j: sibling)
        r.small[2] = exchange(1, 1, PLANE - 1, on_plane)
        r.small_out[...] = exchange(2, PLANE, nz - 1, on_chain)
        sum_3(last)
        for g in range(CHUNKS):
            sum_4(g)
            n = size_of(g)
            mine = r.fin[g, span(seq * own, own, 8), 0:n]
            theirs = r.gsum[g, :, 0:n]
            r.wsum[g, 0, :, 0:n] = jnp.where(seq == 0, mine, theirs)
            r.wsum[g, 1, :, 0:n] = jnp.where(seq == 0, theirs, mine)
        for c in range(len(GATHERS)):
            gather_end(c)
    else:
        r.small_out[...] = r.small[0]
    mixed_copy.wait()
    tgrad_copy.wait()


def call_mixer(fused, nz, tok, og, weights, norm_gain, convp, headp, innerp):
    vmem = pl.BlockSpec(memory_space=pltpu.VMEM)
    hbm = pl.BlockSpec(memory_space=pl.ANY)
    own = D // (2 * nz * PLANE) if fused else 0
    ins = ["tok", "og", "shard" if fused else "w", "norm_gain", "convp", "headp", "innerp"]
    outs = {"mixed": ((ROWS, D), BF), "tgrad": ((ROWS, D), F32), "small_out": ((8, CONVCH), F32)}
    scratch = {
        "normed": ((ROWS + EDGE, D), BF), "normed_t": ((D, ROWS), BF), "db_t": ((D, ROWS), BF),
        "clow": ((ROWS + EDGE, CONVCH), BF), "cout": ((ROWS, CONVCH), BF),
        "gate": ((GROUP, INNER), F32), "back": ((GROUP, INNER), F32), "ssd": ((ROWS, INNER), F32),
        "dssd": ((ROWS, INNER), BF), "dproj": ((ROWS, AT_OUT), BF),
        "dtb": ((ROWS, LANES), F32), "cumb": ((ROWS, LANES), F32), "moved": ((ROWS, LANES), F32),
        "weight": ((ROWS, 256), BF), "fade": ((ROWS, 256), BF),
        "cut": ((BLOCKS, QUADS, 8, GROUP), F32), "spread": ((256, INNER), BF),
        "turned": ((BLOCKS, CX, GROUP), BF), "sco": ((BLOCKS, GROUP, GROUP), F32), "dkb": ((ROWS, LANES), F32), "dqb": ((ROWS, LANES), F32),
        "runs": ((2, NSTATE, INNER), F32), "held": ((2, NSTATE, INNER), BF),
        "dheld": ((2, NSTATE, INNER), F32), "dst": ((2, NSTATE, INNER), BF),
        "flow": ((2, 8, INNER), F32), "halo": ((BLOCKS, 8, CONVCH), F32),
        "halo_next": ((2, 8, CONVCH), F32), "edge_in": ((EDGE, D), BF),
        "state_in": ((NSTATE, INNER), F32), "dstate_in": ((NSTATE, INNER), F32),
        "dedge_in": ((8, CONVCH), F32), "g_norm": ((8, D), F32), "g_conv": ((40, CONVCH), F32),
        "g_head": ((16, LANES), F32), "g_inner": ((16, INNER), F32), "small": ((3, 8, CONVCH), F32),
    }
    dma = pltpu.SemaphoreType.DMA
    sems = {
        "pair_send": dma((4,)), "pair_recv": dma((4,)), "edge_send": dma((CHUNKS,)),
        "edge_recv": dma((CHUNKS,)), "local": dma((2,)),
    }
    if fused:
        part = CHUNK // 2
        outs["wsum"] = ((CHUNKS, 2, own, part), F32)
        scratch |= {
            "w": ((D, WIDE), BF), "shard_in": ((own, WIDE), F32),
            "wg": ((SLOTS, nz, PLANE, 2 * own, CHUNK), BF),
            "r0": ((CHUNKS, nz, PLANE, 2 * own, part), BF),
            "r1": ((CHUNKS, PLANE - 1, nz, 2 * own, part), BF),
            "r2": ((CHUNKS, nz - 1, 2 * own, part), BF), "fin": ((CHUNKS, 2 * own, part), F32),
            "gsum": ((CHUNKS, own, part), F32), "small_in": ((PLANE + nz - 1, 8, CONVCH), F32),
        }
        arrivals = nz - 1 + (PLANE - 1) * nz + 1
        sems |= {
            "g_send": dma((len(GATHERS), arrivals)), "g_recv": dma((len(GATHERS), arrivals)),
            "s_send": dma((CHUNKS, PLANE + nz)), "s_recv": dma((CHUNKS, PLANE + nz)),
            "t_send": dma((PLANE + nz - 1,)), "t_recv": dma((PLANE + nz - 1,)),
        }
    else:
        outs["wgrad"] = ((D, QUADS * CHUNK + AT_X), BF)
    names = ins + list(outs) + list(scratch) + list(sems)
    return pl.pallas_call(
        functools.partial(mixer, names, fused, nz),
        out_shape=[jax.ShapeDtypeStruct(s, t) for s, t in outs.values()],
        in_specs=[vmem] * len(ins),
        out_specs=[hbm, hbm, vmem, vmem],
        scratch_shapes=[pltpu.VMEM(s, t) for s, t in scratch.values()] + list(sems.values()),
        compiler_params=pltpu.CompilerParams(
            collective_id=0, has_side_effects=True, vmem_limit_bytes=63 * 1024 * 1024
        ),
        name="mixer",
    )(tok, og, weights, norm_gain, convp, headp, innerp)


def shards(
    tokens, lengths, norm_gain, in_weight, conv_weight, conv_bias, dt_bias, a_log, skip_gain,
    out_gain, out_weight, out_grad,
):
    both = ("fsdp", "seq")
    row_count = tokens.shape[2]
    own = in_weight.shape[0]
    nf = lax.axis_size("fsdp")
    fused = nf % PLANE == 0 and (2 * own) % 16 == 0 and own % 8 == 0
    nz = nf // PLANE if fused else 1
    positions = lax.axis_index("seq") * row_count + jnp.arange(row_count, dtype=jnp.int32)
    first_long = lengths[0, 0] > lengths[1, 0]
    short_valid = (positions < jnp.minimum(lengths[0, 0], lengths[1, 0]))[:, None]

    def packed(a):
        return jnp.concatenate(
            [jnp.where(first_long, a[0, 0], a[1, 0]),
             jnp.where(first_long, a[1, 0, :GROUP], a[0, 0, :GROUP])], axis=0)

    tok = packed(tokens)
    og = packed(out_grad)
    mask = jnp.concatenate([jnp.ones((row_count, 1), bool), short_valid[:GROUP]], axis=0)
    og = jnp.where(mask, og, jnp.zeros_like(og))
    kind = F32 if fused else BF
    own_weights = jnp.concatenate(
        [in_weight[:, 2 * INNER :], jnp.zeros((own, 2 * LANES - HEADS), BF),
         in_weight[:, INNER : 2 * INNER], in_weight[:, :INNER], out_weight.T], axis=1
    ).astype(kind)
    weights = own_weights
    if not fused:
        weights = lax.all_gather(own_weights, both, axis=0, tiled=True)

    def key_first(a):
        return jnp.concatenate([a[..., INNER:], a[..., :INNER]], axis=-1)

    convp = key_first(
        jnp.concatenate([conv_weight, conv_bias[None], jnp.zeros((3, CONVCH), F32)], axis=0)
    )
    headp = jnp.pad(jnp.stack([dt_bias, a_log]), ((0, 6), (0, LANES - HEADS)))
    innerp = jnp.pad(jnp.stack([out_gain, jnp.repeat(skip_gain, HEADDIM)]), ((0, 6), (0, 0)))
    mixed, tgrad, small, wsum = call_mixer(
        fused, nz, tok, og, weights, norm_gain[None], convp, headp, innerp
    )
    if fused:
        chunks = wsum[:QUADS].transpose(2, 0, 1, 3).reshape(own, QUADS, 3, 256)
        rest = wsum[QUADS, :, :, :256].transpose(1, 0, 2).reshape(own, AT_X)
    else:
        summed = lax.psum_scatter(wsum, both, scatter_dimension=0, tiled=True).astype(F32)
        chunks = summed[:, : QUADS * CHUNK].reshape(own, QUADS, 3, 256)
        rest = summed[:, QUADS * CHUNK :]
        small = lax.psum(small, both)
    x_grad, gate_grad, out_w_grad = (chunks[:, :, i].reshape(own, INNER) for i in range(3))
    in_grad = jnp.concatenate([gate_grad, x_grad, rest[:, : AT_DT + HEADS]], axis=1)
    conv_g = jnp.concatenate([small[:5, CX:], small[:5, :CX]], axis=1)

    def unpacked(a):
        long = a[:row_count]
        short = jnp.where(short_valid, jnp.pad(a[row_count:], ((0, row_count - GROUP), (0, 0))), 0)
        short = short.astype(a.dtype)
        return jnp.stack([jnp.where(first_long, long, short), jnp.where(first_long, short, long)])[
            :, None
        ]

    return (
        unpacked(mixed), unpacked(tgrad), small[7, :D], in_grad, conv_g[:4], conv_g[4],
        small[5, INNER : INNER + HEADS], small[5, INNER + LANES : INNER + LANES + HEADS],
        small[6, :INNER].reshape(HEADS, HEADDIM).sum(1), small[5, :INNER], out_w_grad.T,
    )


def solution(mesh):
    spread = P(None, "fsdp", "seq", None)
    both = ("fsdp", "seq")
    return jax.shard_map(
        shards,
        mesh=mesh,
        in_specs=(
            spread, P(None, "fsdp"), P(), P(both, None), P(), P(), P(), P(), P(), P(),
            P(None, both), spread,
        ),
        out_specs=(
            spread, spread, P(), P(both, None), P(), P(), P(), P(), P(), P(), P(None, both),
        ),
        check_vma=False,
    )
```

time: 325 us -> 199 us (0.61)
  waiting for transfers between devices: 123 us -> 0 us
  Pallas kernels: 110 us -> 172 us
  blocking collectives: 40.8 us -> 0 us
  between operations: 16.8 us -> 3.49 us
  local copies, waits for them, and re-layouts: 16.7 us -> 9.39 us
    all_gather x1 -> x0, waiting for transfers between devices: 63.9 us -> none  [shards(): w = lax.all_gather(sent, both, axis=0, tiled=True)]
    pallas_call x1, Pallas kernels: 110 us -> 172 us  [call_mixer(): pl.pallas_call(functools.partial(mixer, names, fused, nz), out_shape=[jax...]
    unnamed x3 -> x0, waiting for transfers between devices: 58.9 us -> none
    psum x1 -> x0, blocking collectives: 40.8 us -> none  [shards(): norm_grad, conv_g, head_g, inner_g = lax.psum(small, both)]
    slice x6 -> x10, local copies, waits for them, and re-layouts: 7 us -> 2.4 us  [the longest x1 1.15 us: shards(): chunks[:, :, i].reshape(own, INNER)]
    reduce_sum x5 -> x1, other arithmetic: 4.69 us -> 0.63 us  [shards(): small[6, :INNER].reshape(HEADS, HEADDIM).sum(1)]
  transfers between devices with their start and end apart: 2 -> 0, of which waited for: 2 -> 0; matrix products, arithmetic and copies ran while one was open for 8% -> 0% of each run, Pallas kernels for 0% -> 0%
where the time goes in v2:
time: 199 us
  Pallas kernels  172 us (86%)
  other arithmetic  13.8 us (7%)
  local copies, waits for them, and re-layouts  9.39 us (5%)
  between operations  3.49 us (2%)
    pallas_call x1, Pallas kernels, call_mixer(): pl.pallas_call(functools.partial(mixer, names, fused, nz), out_shape=[jax...  172 us

profile of v2, /device:TPU:0, one launch (start us, length us, event | category | flops | bytes accessed | tf_op | source)
XLA Modules:
  0.0 198.6 jit_solution(12560911111050201353)
XLA Ops:
  0.6 1.3 fusion.3
  3.3 2.2 %select_bitcast_fusion.4 = (bf16[512,768]{1,0:T(8,128)(2,1)S(1)}, bf16[512,768]{1,0:T(8,128)(2,1)S(1)}) fusion(bf16[2,1,512,768]{3,2,1,0:T(8,128)(2,1)} %param.23, pred[]{:T(512)} %bitcast, bf16[2,1,512,768]{3,2,1,0:T(8,128)(2,1)} %param.12), kind=kLoop, calls=%fused_computation.10 | loop fusion | flops 786432 | bytes 4718593 | tf_op jit(solution)/shard_map/jit(_where)/select_n | solution.py:964
  5.4 0.2 copy-done
  5.6 0.5 copy-done.1
  6.1 0.1 select_bitcast_fusion.6
  7.5 1.3 maximum_select_fusion.refs_1_
  8.9 1.1 pad_maximum_fusion.refs_0_
  10.0 0.1 concatenate.27
  10.1 0.8 convert_element_type.15.refs_2_
  11.1 0.6 pad_maximum_fusion.2.refs_4_
  11.8 0.1 stack_reshape.3
  11.9 0.6 select_maximum_fusion.refs_6_
  12.5 0.6 select_maximum_fusion.1.refs_5_
  13.2 0.6 broadcast_in_dim.62.refs_3_
  13.7 171.9 %mixer.1 = (bf16[768,768]{1,0:T(8,128)(2,1)}, f32[768,768]{1,0:T(8,128)}, f32[8,1792]{1,0:T(8,128)}, f32[7,2,24,384]{3,2,1,0:T(8,128)}) custom-call(bf16[768,768]{1,0:T(8,128)(2,1)} %pad_maximum_fusion.refs_0_, bf16[768,768]{1,0:T(8,128)(2,1)} %maximum_select_fusion.refs_1_, f32[24,5120]{1,0:T(8,128)} %convert_element_type.15.refs_2_, ...), custom_call_target="tpu_custom_call" | custom-call | tf_op jit(solution)/shard_map/mixer/pallas_call | solution.py:935
  185.6 1.0 slice_bitcast_fusion
  186.7 0.2 copy.25
  186.9 0.5 reshape.44
  187.4 1.1 slice_reduce_fusion
  188.7 0.8 slice_bitcast_fusion.1
  189.5 0.7 pad_maximum_fusion.1
  190.3 0.3 select_bitcast_fusion.1
  190.6 1.9 maximum_bitcast_fusion
  192.5 0.4 select_bitcast_fusion.3
  192.9 1.3 maximum_bitcast_fusion.1
  194.2 0.6 fusion
  194.8 0.6 fusion.1
  195.4 0.6 slice_reduce_fusion.3
  196.1 0.6 reduce_sum.9
  196.7 0.5 slice_bitcast_fusion.2
  197.2 0.6 slice_reduce_fusion.5
  197.8 0.7 copy.32
  (50 shorter events, 0.6 us)
Async XLA Ops:
  3.3 2.4 %copy-start = (bf16[2,1,512,768]{3,2,1,0:T(8,128)(2,1)S(1)}, bf16[2,1,512,768]{3,2,1,0:T(8,128)(2,1)}, u32[]{:S(2)}) copy-start(bf16[2,1,512,768]{3,2,1,0:T(8,128)(2,1)} %param.23) | copy-start | bytes 4718596
  3.3 2.8 %copy-start.1 = (bf16[2,1,512,768]{3,2,1,0:T(8,128)(2,1)S(1)}, bf16[2,1,512,768]{3,2,1,0:T(8,128)(2,1)}, u32[]{:S(2)}) copy-start(bf16[2,1,512,768]{3,2,1,0:T(8,128)(2,1)} %param.12) | copy-start | bytes 4718596
  8.8 1.1 copy-start.4
  8.8 1.2 slice-start
  8.8 1.2 copy-start.6
  8.8 2.1 %copy-start.9 = (f32[1792]{0:T(1024)S(1)}, f32[1792]{0:T(1024)}, u32[]{:S(2)}) copy-start(f32[1792]{0:T(1024)} %param.17) | copy-start | bytes 21508
  8.8 2.2 %copy-start.7 = (f32[4,1792]{1,0:T(4,128)S(1)}, f32[4,1792]{1,0:T(4,128)}, u32[]{:S(2)}) copy-start(f32[4,1792]{1,0:T(4,128)} %param.16) | copy-start | bytes 86020
  8.8 2.9 %copy-start.11 = (f32[24]{0:T(128)S(1)}, f32[24]{0:T(128)}, u32[]{:S(2)}) copy-start(f32[24]{0:T(128)} %param.20) | copy-start | bytes 292
  8.8 3.0 %copy-start.8 = (f32[1536]{0:T(1024)S(1)}, f32[1536]{0:T(1024)}, u32[]{:S(2)}) copy-start(f32[1536]{0:T(1024)} %param.21) | copy-start | bytes 18436
  10.0 2.6 %copy-start.12 = (f32[24]{0:T(128)S(1)}, f32[24]{0:T(128)}, u32[]{:S(2)}) copy-start(f32[24]{0:T(128)} %param.19) | copy-start | bytes 292
  10.0 2.6 %copy-start.13 = (f32[24]{0:T(128)S(1)}, f32[24]{0:T(128)}, u32[]{:S(2)}) copy-start(f32[24]{0:T(128)} %param.18) | copy-start | bytes 292
  10.0 3.2 %copy-start.10 = (f32[768]{0:T(1024)S(1)}, f32[768]{0:T(1024)}, u32[]{:S(2)}) copy-start(f32[768]{0:T(1024)} %param.14) | copy-start | bytes 9220
  187.4 2.8 %copy-start.2 = (f32[768,768]{1,0:T(8,128)S(1)}, f32[768,768]{1,0:T(8,128)}, u32[]{:S(2)}) copy-start(f32[768,768]{1,0:T(8,128)} %get-tuple-element.16) | copy-start | bytes 7077892
  190.6 1.9 copy-start.3
  192.9 1.3 copy-start.5

commit v3 on v2

--- a/solution.py
+++ b/solution.py
@@ -31,7 +31,9 @@
 WIDE = AT_OUT + INNER
 CX = 2 * NSTATE
 CHUNK = 768
-CHUNKS = QUADS + 1
+WIDE_CHUNKS = 4
+CHUNKS = WIDE_CHUNKS + QUADS + 1
+UNITS = 7
 SLOTS = 4
 GATHERS = ((0, 512), (512, 512), (1024, 1024), (AT_GATE, INNER), (AT_OUT, INNER))
 PLANE = 4
@@ -135,6 +137,25 @@
     barrier = pltpu.get_barrier_semaphore()
     for peer in peers:
         pl.semaphore_signal(barrier, inc=1, device_id=peer, device_id_type=MESH)
+
+    part_rows = r.tokens.shape[2]
+    raw = [buf.at[0:part_rows, m * D : (m + 1) * D] for buf in (r.dssd, r.cout) for m in range(2)]
+    raw_copies = []
+    for i in range(4):
+        src = (r.tokens, r.out_grad)[i // 2].at[i % 2, 0]
+        raw_copies.append(pltpu.make_async_copy(src, raw[i], r.local.at[2 + i]))
+        raw_copies[i].start()
+
+    if fused:
+        wide = 2 * INNER
+        r.shard[:, 0:CX] = r.in_weight[:, wide : wide + CX].astype(F32)
+        steps = r.in_weight[:, wide + CX :].astype(F32)
+        fill = jnp.zeros((steps.shape[0], AT_X - CX - HEADS), F32)
+        r.shard[:, CX:AT_X] = jnp.concatenate([steps, fill], axis=1)
+        r.shard[:, AT_X:AT_GATE] = r.in_weight[:, INNER:wide].astype(F32)
+        r.shard[:, AT_GATE:AT_OUT] = r.in_weight[:, 0:INNER].astype(F32)
+        r.shard[:, AT_OUT:] = r.out_weight[...].astype(F32)
+
     pl.semaphore_wait(barrier, len(peers))
 
     def remote(src, dst, send, recv, device):
@@ -164,13 +185,20 @@
     def chain_copy(c, j):
         return gather_copy(c, j - 1, f, on_chain(j))
 
-    def plane_copy(c, j, back):
-        index = (z_at - back + nz) % nz * PLANE + p_at
-        return gather_copy(c, nz - 1 + (j - 1) * nz + back, index, on_plane(j))
+    def plane_copy(c, kind, back):
+        low, size = GATHERS[c]
+        owner = (p_at, p_at, plane_peer(1), plane_peer(2))[kind]
+        cols = part(c)
+        if kind >= 2:
+            cols = span(low + seq * (size // 2) + (kind - 2) * (size // 4), size // 4, 128)
+        at = w.at[slab_of((z_at - back + nz) % nz * PLANE + owner), cols]
+        k = nz - 1 + back * 4 + kind
+        device = on_plane((1, 2, 2, 1)[kind])
+        return remote(at, at, r.g_send.at[c, k], r.g_recv.at[c, k], device)
 
     def last_copy(c):
         at = w.at[:, part(c)]
-        k = nz - 1 + (PLANE - 1) * nz
+        k = nz - 1 + 4 * nz
         return remote(at, at, r.g_send.at[c, k], r.g_recv.at[c, k], sibling)
 
     def gather_own(c):
@@ -180,70 +208,82 @@
         second = jnp.where(seq == 0, theirs, mine)
         w[slab_of(f), cols] = jnp.concatenate([first, second], axis=0).astype(BF)
 
-    def gather_1(c):
+    def gather_0(c):
         for j in range(1, nz):
             chain_copy(c, j).start()
-        for j in range(1, PLANE):
-            plane_copy(c, j, 0).start()
+
+    def gather_1(c):
+        for kind in range(2):
+            plane_copy(c, kind, 0).start()
 
     def gather_2(c):
         for back in range(1, nz):
             chain_copy(c, back).wait_recv()
-            for j in range(1, PLANE):
-                plane_copy(c, j, back).start()
+            for kind in range(2):
+                plane_copy(c, kind, back).start()
 
     def gather_3(c):
-        for j in range(1, PLANE):
-            for back in range(nz):
-                plane_copy(c, j, back).wait_recv()
+        for back in range(nz):
+            for kind in range(2):
+                plane_copy(c, kind, back).wait_recv()
+                plane_copy(c, kind + 2, back).start()
+
+    def gather_4(c):
+        for back in range(nz):
+            for kind in range(2, 4):
+                plane_copy(c, kind, back).wait_recv()
         last_copy(c).start()
 
-    def gather_4(c):
+    def gather_5(c):
         last_copy(c).wait_recv()
 
     def gather_end(c):
         for j in range(1, nz):
             chain_copy(c, j).wait_send()
-        for j in range(1, PLANE):
+        for kind in range(4):
             for back in range(nz):
-                plane_copy(c, j, back).wait_send()
+                plane_copy(c, kind, back).wait_send()
         last_copy(c).wait_send()
 
-    def size_of(g):
-        return 256 if isinstance(g, int) and g == QUADS else CHUNK // 2
-
-    def lanes_of(g, which):
-        size = size_of(g)
-        return span(which * size, size, 128)
-
-    def place_of(g):
-        return g % SLOTS
+    def wide_chunk(i):
+        return i, i, 0, CHUNK // 2, i, 0
+
+    def quad_chunk(q):
+        return WIDE_CHUNKS + q, q // 3, (q % 3) * 256, 128, WIDE_CHUNKS + q // 3, (q % 3) * 128
+
+    last_chunk = (WIDE_CHUNKS + QUADS, 2, 0, AT_X // 2, UNITS - 1, 0)
+
+    def source(g, which):
+        return span(g[2] + which * g[3], g[3], 128)
+
+    def target(g):
+        return span(g[5], g[3], 128)
 
     def sum_copy_0(g):
-        n = size_of(g)
-        src = r.wg.at[place_of(g), :, :, :, lanes_of(g, 1 - seq)]
-        dst = r.r0.at[g, :, :, :, 0:n]
-        return remote(src, dst, r.s_send.at[g, 0], r.s_recv.at[g, 0], sibling)
+        src = r.wg.at[g[1], :, :, :, source(g, 1 - seq)]
+        dst = r.r0.at[g[4], :, :, :, target(g)]
+        return remote(src, dst, r.s_send.at[g[0], 0], r.s_recv.at[g[0], 0], sibling)
 
     def sum_copy_1(g, j):
-        n = size_of(g)
-        src = r.wg.at[place_of(g), :, plane_peer(j), :, lanes_of(g, seq)]
-        dst = r.r1.at[g, j - 1, :, :, 0:n]
-        return remote(src, dst, r.s_send.at[g, j], r.s_recv.at[g, j], on_plane(j))
+        src = r.wg.at[g[1], :, plane_peer(j), :, source(g, seq)]
+        dst = r.r1.at[g[4], j - 1, :, :, target(g)]
+        return remote(src, dst, r.s_send.at[g[0], j], r.s_recv.at[g[0], j], on_plane(j))
 
     def sum_copy_2(g, j):
-        n = size_of(g)
         k = PLANE - 1 + j
-        src = r.wg.at[place_of(g), z_peer(j), p_at, :, lanes_of(g, seq)]
-        dst = r.r2.at[g, j - 1, :, 0:n]
-        return remote(src, dst, r.s_send.at[g, k], r.s_recv.at[g, k], on_chain(j))
+        src = r.wg.at[g[1], z_peer(j), p_at, :, source(g, seq)]
+        dst = r.r2.at[g[4], j - 1, :, target(g)]
+        return remote(src, dst, r.s_send.at[g[0], k], r.s_recv.at[g[0], k], on_chain(j))
 
     def sum_copy_3(g):
-        n = size_of(g)
         k = PLANE - 1 + nz
-        src = r.fin.at[g, span((1 - seq) * own, own, 8), 0:n]
-        dst = r.gsum.at[g, :, 0:n]
-        return remote(src, dst, r.s_send.at[g, k], r.s_recv.at[g, k], sibling)
+        src = r.fin.at[g[4], span((1 - seq) * own, own, 8), target(g)]
+        dst = r.gsum.at[g[4], :, target(g)]
+        return remote(src, dst, r.s_send.at[g[0], k], r.s_recv.at[g[0], k], sibling)
+
+    def finish(copy):
+        copy.wait_send()
+        copy.wait_recv()
 
     def sum_0(g):
         if fused:
@@ -252,15 +292,12 @@
     def sum_1(g):
         if not fused:
             return
-        copy = sum_copy_0(g)
-        copy.wait_send()
-        copy.wait_recv()
-        n, here, lanes = size_of(g), place_of(g), lanes_of(g, seq)
+        finish(sum_copy_0(g))
 
         def add(i):
-            zi, pi = i // PLANE, i % PLANE
-            mine = r.wg[here, zi, pi, :, lanes].astype(F32)
-            r.wg[here, zi, pi, :, lanes] = (mine + r.r0[g, zi, pi, :, 0:n].astype(F32)).astype(BF)
+            at = (g[1], i // PLANE, i % PLANE, slice(None), source(g, seq))
+            theirs = r.r0[g[4], i // PLANE, i % PLANE, :, target(g)]
+            r.wg[at] = (r.wg[at].astype(F32) + theirs.astype(F32)).astype(BF)
 
         loop(nz * PLANE, add)
         for j in (3, 1, 2):
@@ -269,17 +306,15 @@
     def sum_2(g):
         if not fused:
             return
-        n, here, lanes = size_of(g), place_of(g), lanes_of(g, seq)
         for j in range(1, PLANE):
-            copy = sum_copy_1(g, j)
-            copy.wait_send()
-            copy.wait_recv()
+            finish(sum_copy_1(g, j))
 
         def add(zi):
-            total = r.wg[here, zi, p_at, :, lanes].astype(F32)
+            at = (g[1], zi, p_at, slice(None), source(g, seq))
+            value = r.wg[at].astype(F32)
             for j in range(PLANE - 1):
-                total = total + r.r1[g, j, zi, :, 0:n].astype(F32)
-            r.wg[here, zi, p_at, :, lanes] = total.astype(BF)
+                value = value + r.r1[g[4], j, zi, :, target(g)].astype(F32)
+            r.wg[at] = value.astype(BF)
 
         loop(nz, add)
         for j in range(1, nz):
@@ -288,37 +323,34 @@
     def sum_3(g):
         if not fused:
             return
-        n, here, lanes = size_of(g), place_of(g), lanes_of(g, seq)
         for j in range(1, nz):
-            copy = sum_copy_2(g, j)
-            copy.wait_send()
-            copy.wait_recv()
-        total = r.wg[here, z_at, p_at, :, lanes].astype(F32)
+            finish(sum_copy_2(g, j))
+        value = r.wg[g[1], z_at, p_at, :, source(g, seq)].astype(F32)
         for j in range(nz - 1):
-            total = total + r.r2[g, j, :, 0:n].astype(F32)
-        r.fin[g, :, 0:n] = total
+            value = value + r.r2[g[4], j, :, target(g)].astype(F32)
+        r.fin[g[4], :, target(g)] = value
         sum_copy_3(g).start()
 
     def sum_4(g):
-        if not fused:
-            return
-        copy = sum_copy_3(g)
-        copy.wait_send()
-        copy.wait_recv()
+        finish(sum_copy_3(g))
 
     def put_grad(g, low, value):
         size = value.shape[1]
         if fused:
             parts = value.astype(BF).reshape(nz, PLANE, slab, size)
-            r.wg[place_of(g), :, :, :, low : low + size] = parts
+            r.wg[g[1], :, :, :, span(g[2] + low, size, 128)] = parts
         else:
-            r.wgrad[:, span(g * CHUNK + low, size, 128)] = value.astype(BF)
-
-    edge_copy = pair_copy(0, r.tok.at[2 * GROUP - EDGE : 2 * GROUP, :], r.edge_in)
-    edge_copy.start()
+            first = g[4] * CHUNK + (g[2] if g[3] == 128 else 0)
+            r.wgrad[:, span(first + low, size, 128)] = value.astype(BF)
+
+    def shard_copy(c):
+        low, size = GATHERS[c]
+        cols = span(low + (1 - seq) * (size // 2), size // 2, 128)
+        return pair_copy(4 + c, r.shard.at[:, cols], r.shard_in.at[:, cols])
+
     if fused:
-        shard_copy = pair_copy(1, r.shard, r.shard_in)
-        shard_copy.start()
+        for c in range(len(GATHERS)):
+            shard_copy(c).start()
 
     def make_spread(q):
         shape = (256, 256)
@@ -326,13 +358,49 @@
         r.spread[:, span(q * 256, 256)] = (head == (iota(shape, 0) & 127)).astype(F32).astype(BF)
 
     if fused:
-        shard_copy.wait()
         for c in range(len(GATHERS)):
+            shard_copy(c).wait()
             gather_own(c)
             if c < 2:
+                gather_0(c)
                 gather_1(c)
+        gather_0(2)
+
+    r.convp[0:CONV, 0:CX] = r.conv_weight[:, INNER:]
+    r.convp[0:CONV, CX:] = r.conv_weight[:, 0:INNER]
+    bias = r.conv_bias[...].reshape(1, CONVCH)
+    r.convp[4:5, 0:CX] = bias[:, INNER:]
+    r.convp[4:5, CX:] = bias[:, 0:INNER]
+    r.headp[...] = jnp.zeros_like(r.headp)
+    for i, v in enumerate((r.dt_bias, r.a_log, r.skip_gain)):
+        r.headp[i : i + 1, 0:HEADS] = v[...].reshape(1, HEADS)
+    norm_gain = r.norm_gain[...].reshape(1, D)
+
+    first_long = r.lengths[0, 0] > r.lengths[1, 0]
+    shortest = jnp.minimum(r.lengths[0, 0], r.lengths[1, 0])
+    for i in range(4):
+        raw_copies[i].wait()
+
+    def pick_rows(i):
+        here = span(i * 64, 64)
+        for to, k in ((r.tok, 0), (r.og, 2)):
+            to[here, :] = jnp.where(first_long, raw[k][here, :], raw[k + 1][here, :])
+
+    def pick_short(i):
+        here, there = span(i * 64, 64), span(2 * GROUP + i * 64, 64)
+        r.tok[there, :] = jnp.where(first_long, raw[1][here, :], raw[0][here, :])
+        valid = (seq * part_rows + i * 64 + iota((64, D), 0) < shortest).astype(F32)
+        picked = jnp.where(first_long, raw[3][here, :], raw[2][here, :])
+        r.og[there, :] = (picked.astype(F32) * valid).astype(BF)
+
+    loop(2 * GROUP // 64, pick_rows)
+    edge_copy = pair_copy(0, r.tok.at[2 * GROUP - EDGE : 2 * GROUP, :], r.edge_in)
+    edge_copy.start()
+    loop(GROUP // 64, pick_short)
 
     loop(QUADS, make_spread)
+    r.innerp[0:1, :] = r.out_gain[...].reshape(1, INNER)
+    r.innerp[1:2, :] = dot(side_by_side(r.headp[...]), r.spread[...])[2:3, :]
     tri_shape = (GROUP, GROUP)
     lower = (iota(tri_shape, 0) >= iota(tri_shape, 1)).astype(F32).astype(BF)
     upper = (iota(tri_shape, 0) <= iota(tri_shape, 1)).astype(F32).astype(BF)
@@ -351,7 +419,7 @@
 
     def norm_of(v):
         root = lax.rsqrt(jnp.mean(v * v, axis=1, keepdims=True) + EPS)
-        return (v * root * r.norm_gain[...]).astype(BF)
+        return (v * root * norm_gain).astype(BF)
 
     def norm_rows(i):
         rows = span(i * 64, 64)
@@ -361,6 +429,11 @@
     edge_copy.wait()
     r.normed[ROWS:, :] = norm_of(r.edge_in[...].astype(F32) * is_second)
 
+    if fused:
+        gather_2(0)
+        gather_1(2)
+        gather_0(3)
+
     def turn(b):
         rows = rows_of(b)
         r.normed_t[:, rows] = r.normed[rows, :].T
@@ -369,11 +442,11 @@
     loop(BLOCKS, turn)
 
     if fused:
-        gather_2(0)
         gather_2(1)
-        gather_1(2)
         gather_3(0)
         gather_4(0)
+        gather_3(1)
+        gather_5(0)
 
     def conv_acc(values, before, cols):
         rows = values.shape[0]
@@ -475,20 +548,23 @@
 
             @pl.when(q == 0)
             def _():
-                gather_3(1)
                 gather_2(2)
+                gather_0(4)
+                gather_4(1)
                 gather_1(3)
-                gather_4(1)
+                gather_5(1)
 
             @pl.when(q == 1)
             def _():
                 gather_3(2)
-                gather_1(4)
+                gather_2(3)
 
             @pl.when(q == 2)
             def _():
                 gather_4(2)
-                gather_2(3)
+                gather_1(4)
+                gather_3(3)
+                gather_5(2)
 
             @pl.when(q == 3)
             def _():
@@ -496,7 +572,11 @@
 
             @pl.when(q == 4)
             def _():
-                gather_3(3)
+                gather_4(3)
+
+            @pl.when(q == 5)
+            def _():
+                gather_3(4)
 
         project(span(AT_X + q * 256, 256), span(CX + q * 256, 256))
         loop(BLOCKS, lambda b: forward_block(b, q))
@@ -512,8 +592,8 @@
     state_copy = pair_copy(2, r.runs.at[1], r.state_in)
     state_copy.start()
     if fused:
-        gather_3(4)
-        gather_4(3)
+        gather_4(4)
+        gather_5(3)
 
     def carry_block(b):
         rows = rows_of(b)
@@ -570,7 +650,7 @@
 
     gate_project(2)
     if fused:
-        gather_4(4)
+        gather_5(4)
     out_back(2)
     gate_block(2)
     state_copy.wait()
@@ -588,6 +668,21 @@
 
     loop(2, gate_long)
 
+    def wide_grad(i):
+        g = wide_chunk(i)
+        left = r.db_t if i < 2 else r.normed_t
+        first = (AT_X if i < 2 else AT_GATE) + (i % 2) * CHUNK
+
+        def tile(k):
+            put_grad(g, k * 256, dot(left[...], r.dproj[:, span(first + k * 256, 256)]))
+
+        loop(CHUNK // 256, tile)
+        sum_0(g)
+
+    for i in range(WIDE_CHUNKS):
+        wide_grad(i)
+    sum_1(wide_chunk(0))
+
     def state_back(b):
         rows = rows_of(b)
 
@@ -605,6 +700,7 @@
     r.dheld[0] = r.dheld[0] + decay_0 * r.dheld[1]
     dstate_copy = pair_copy(3, r.dheld.at[0], r.dstate_in)
     dstate_copy.start()
+    sum_1(wide_chunk(1))
 
     def out_block(b):
         rows = rows_of(b)
@@ -614,6 +710,7 @@
     loop(BLOCKS, out_block)
     mixed_copy = pltpu.make_async_copy(r.normed.at[0:ROWS, :], r.mixed, r.local.at[0])
     mixed_copy.start()
+    sum_1(wide_chunk(2))
 
     def ds_of(b):
         return r.back.at[:, heads_of(b)]
@@ -740,30 +837,42 @@
             conv_back(1, *chunk(k), r.dedge_in[:, chunk(k)[1]] * is_first)
 
     def backward_quad(q):
-        heads = span(q * 256, 256)
-        put_grad(q, 512, dot(r.db_t[...], r.dproj[:, span(AT_X + q * 256, 256)]))
-        put_grad(q, 256, dot(r.normed_t[...], r.dproj[:, span(AT_GATE + q * 256, 256)]))
+        for i in range(WIDE_CHUNKS):
+
+            @pl.when(q == i)
+            def _():
+                sum_2(wide_chunk(i))
+
+        @pl.when(q == 0)
+        def _():
+            sum_1(wide_chunk(3))
+
+        loop(BLOCKS, lambda b: backward_block(b, q))
+
+        for i in range(WIDE_CHUNKS):
+
+            @pl.when(q == i)
+            def _():
+                sum_3(wide_chunk(i))
 
         @pl.when(q >= 1)
         def _():
-            sum_1(q - 1)
-
-        loop(BLOCKS, lambda b: backward_block(b, q))
+            sum_1(quad_chunk(q - 1))
 
         @pl.when(q >= 2)
         def _():
-            sum_2(q - 2)
+            sum_2(quad_chunk(q - 2))
 
         @pl.when(q >= 3)
         def _():
-            sum_3(q - 3)
+            sum_3(quad_chunk(q - 3))
 
         conv_back_all(q, CX + q * 256, AT_X + q * 256)
-        put_grad(q, 0, dot(r.normed_t[...], r.dproj[:, span(AT_X + q * 256, 256)]))
-        sum_0(q)
+        g = quad_chunk(q)
+        put_grad(g, 0, dot(r.normed_t[...], r.dproj[:, span(AT_X + q * 256, 256)]))
+        sum_0(g)
 
     loop(QUADS, backward_quad)
-    last = QUADS
 
     def backward_rest(b):
         rows = rows_of(b)
@@ -800,24 +909,24 @@
         r.dproj[rows, AT_DT : AT_DT + LANES] = d_pre.astype(BF)
 
     loop(BLOCKS, step_grad)
-    sum_1(last - 1)
-    conv_back_all(last, 0, 0)
-    put_grad(last, 0, dot(r.normed_t[...], r.dproj[:, 0:AT_X]))
-    sum_0(last)
-    sum_2(last - 2)
-    sum_3(last - 3)
+    sum_1(quad_chunk(5))
+    conv_back_all(QUADS, 0, 0)
+    put_grad(last_chunk, 0, dot(r.normed_t[...], r.dproj[:, 0:AT_X]))
+    sum_0(last_chunk)
+    sum_2(quad_chunk(4))
+    sum_3(quad_chunk(3))
 
     def in_block(b):
         rows = rows_of(b)
         r.ssd[rows, 0:D] = dot_nt(r.dproj[rows, :], w[:, 0:AT_OUT])
 
     in_block(2)
-    sum_1(last)
-    sum_2(last - 1)
-    sum_3(last - 2)
+    sum_1(last_chunk)
+    sum_2(quad_chunk(5))
+    sum_3(quad_chunk(4))
     loop(2, in_block)
-    sum_2(last)
-    sum_3(last - 1)
+    sum_2(last_chunk)
+    sum_3(quad_chunk(5))
 
     def norm_back(i):
         rows = span(i * 32, 32)
@@ -826,7 +935,7 @@
         y = v * root
         dn = r.ssd[rows, 0:D]
         r.g_norm[...] += fold(dn * y)
-        bb = r.norm_gain[...] * dn
+        bb = norm_gain * dn
         d_v = root * (bb - y * jnp.mean(y * bb, axis=1, keepdims=True))
         r.ssd[rows, 0:D] = r.og[rows, :].astype(F32) + d_v
 
@@ -842,8 +951,10 @@
     r.small[0, 5:6, 0:INNER] = total(r.g_inner[0:8, :])
     r.small[0, 5:6, INNER : INNER + LANES] = total(r.g_head[0:8, :])
     r.small[0, 5:6, INNER + LANES :] = total(r.g_head[8:16, :])
-    r.small[0, 6:7, 0:INNER] = total(r.g_inner[8:16, :])
-    r.small[0, 6:7, INNER:] = jnp.zeros((1, CX), F32)
+    high, low = halves(r.g_inner[8:16, :])
+    skips = dot_nt(high, r.spread[0:LANES, :]) + dot_nt(low, r.spread[0:LANES, :])
+    r.small[0, 6:7, 0:LANES] = total(skips)
+    r.small[0, 6:7, LANES:] = jnp.zeros((1, CONVCH - LANES), F32)
     r.small[0, 7:8, 0:D] = total(r.g_norm[...])
     r.small[0, 7:8, D:] = jnp.zeros((1, CONVCH - D), F32)
     if fused:
@@ -868,14 +979,23 @@
         r.small[1] = exchange(0, 0, 1, lambda j: sibling)
         r.small[2] = exchange(1, 1, PLANE - 1, on_plane)
         r.small_out[...] = exchange(2, PLANE, nz - 1, on_chain)
-        sum_3(last)
-        for g in range(CHUNKS):
+        sum_3(last_chunk)
+        def hand_out(g, dst, first, count):
             sum_4(g)
-            n = size_of(g)
-            mine = r.fin[g, span(seq * own, own, 8), 0:n]
-            theirs = r.gsum[g, :, 0:n]
-            r.wsum[g, 0, :, 0:n] = jnp.where(seq == 0, mine, theirs)
-            r.wsum[g, 1, :, 0:n] = jnp.where(seq == 0, theirs, mine)
+            mine = r.fin[g[4], span(seq * own, own, 8), target(g)]
+            theirs = r.gsum[g[4], :, target(g)]
+            for half_at in range(2):
+                value = jnp.where(seq == half_at, mine, theirs)
+                size = min(g[3], count - half_at * g[3])
+                at = first + half_at * g[3]
+                dst[:, at : at + size] = value[:, 0:size]
+
+        for i in range(WIDE_CHUNKS):
+            dst = r.grad_out if i < 2 else r.grad_in
+            hand_out(wide_chunk(i), dst, (i % 2) * CHUNK, CHUNK)
+        for q in range(QUADS):
+            hand_out(quad_chunk(q), r.grad_in, INNER + q * 256, 256)
+        hand_out(last_chunk, r.grad_in, 2 * INNER, CX + HEADS)
         for c in range(len(GATHERS)):
             gather_end(c)
     else:
@@ -884,13 +1004,16 @@
     tgrad_copy.wait()
 
 
-def call_mixer(fused, nz, tok, og, weights, norm_gain, convp, headp, innerp):
+def call_mixer(fused, nz, arrays):
     vmem = pl.BlockSpec(memory_space=pltpu.VMEM)
     hbm = pl.BlockSpec(memory_space=pl.ANY)
+    places = {"lengths": pl.BlockSpec(memory_space=pltpu.SMEM), "tokens": hbm, "out_grad": hbm}
     own = D // (2 * nz * PLANE) if fused else 0
-    ins = ["tok", "og", "shard" if fused else "w", "norm_gain", "convp", "headp", "innerp"]
+    ins = list(arrays)
     outs = {"mixed": ((ROWS, D), BF), "tgrad": ((ROWS, D), F32), "small_out": ((8, CONVCH), F32)}
     scratch = {
+        "tok": ((ROWS, D), BF), "og": ((ROWS, D), BF), "convp": ((8, CONVCH), F32),
+        "headp": ((8, LANES), F32), "innerp": ((8, INNER), F32),
         "normed": ((ROWS + EDGE, D), BF), "normed_t": ((D, ROWS), BF), "db_t": ((D, ROWS), BF),
         "clow": ((ROWS + EDGE, CONVCH), BF), "cout": ((ROWS, CONVCH), BF),
         "gate": ((GROUP, INNER), F32), "back": ((GROUP, INNER), F32), "ssd": ((ROWS, INNER), F32),
@@ -909,40 +1032,98 @@
     }
     dma = pltpu.SemaphoreType.DMA
     sems = {
-        "pair_send": dma((4,)), "pair_recv": dma((4,)), "edge_send": dma((CHUNKS,)),
-        "edge_recv": dma((CHUNKS,)), "local": dma((2,)),
+        "pair_send": dma((9,)), "pair_recv": dma((9,)), "edge_send": dma((QUADS + 1,)),
+        "edge_recv": dma((QUADS + 1,)), "local": dma((6,)),
     }
     if fused:
         part = CHUNK // 2
-        outs["wsum"] = ((CHUNKS, 2, own, part), F32)
+        outs |= {"grad_in": ((own, PROJ), F32), "grad_out": ((own, INNER), F32)}
         scratch |= {
-            "w": ((D, WIDE), BF), "shard_in": ((own, WIDE), F32),
+            "w": ((D, WIDE), BF), "shard": ((own, WIDE), F32), "shard_in": ((own, WIDE), F32),
             "wg": ((SLOTS, nz, PLANE, 2 * own, CHUNK), BF),
-            "r0": ((CHUNKS, nz, PLANE, 2 * own, part), BF),
-            "r1": ((CHUNKS, PLANE - 1, nz, 2 * own, part), BF),
-            "r2": ((CHUNKS, nz - 1, 2 * own, part), BF), "fin": ((CHUNKS, 2 * own, part), F32),
-            "gsum": ((CHUNKS, own, part), F32), "small_in": ((PLANE + nz - 1, 8, CONVCH), F32),
+            "r0": ((UNITS, nz, PLANE, 2 * own, part), BF),
+            "r1": ((UNITS, PLANE - 1, nz, 2 * own, part), BF),
+            "r2": ((UNITS, nz - 1, 2 * own, part), BF), "fin": ((UNITS, 2 * own, part), F32),
+            "gsum": ((UNITS, own, part), F32), "small_in": ((PLANE + nz - 1, 8, CONVCH), F32),
         }
-        arrivals = nz - 1 + (PLANE - 1) * nz + 1
+        arrivals = nz - 1 + 4 * nz + 1
         sems |= {
             "g_send": dma((len(GATHERS), arrivals)), "g_recv": dma((len(GATHERS), arrivals)),
             "s_send": dma((CHUNKS, PLANE + nz)), "s_recv": dma((CHUNKS, PLANE + nz)),
             "t_send": dma((PLANE + nz - 1,)), "t_recv": dma((PLANE + nz - 1,)),
         }
     else:
-        outs["wgrad"] = ((D, QUADS * CHUNK + AT_X), BF)
+        outs["wgrad"] = ((D, WIDE), BF)
     names = ins + list(outs) + list(scratch) + list(sems)
     return pl.pallas_call(
         functools.partial(mixer, names, fused, nz),
         out_shape=[jax.ShapeDtypeStruct(s, t) for s, t in outs.values()],
-        in_specs=[vmem] * len(ins),
-        out_specs=[hbm, hbm, vmem, vmem],
+        in_specs=[places.get(name, vmem) for name in ins],
+        out_specs=[hbm, hbm] + [vmem] * (len(outs) - 2),
         scratch_shapes=[pltpu.VMEM(s, t) for s, t in scratch.values()] + list(sems.values()),
         compiler_params=pltpu.CompilerParams(
             collective_id=0, has_side_effects=True, vmem_limit_bytes=63 * 1024 * 1024
         ),
         name="mixer",
-    )(tok, og, weights, norm_gain, convp, headp, innerp)
+    )(*arrays.values())
+
+
+def place_results(
+    lengths, mixed, tgrad, small, grad_in, grad_out, mixed_at, tgrad_at, norm, in_at, conv, bias,
+    step, rates, skip, gain, out_at, blank, blank_low, sems,
+):
+    seq = lax.axis_index("seq")
+    long = jnp.where(lengths[0, 0] > lengths[1, 0], 0, 1)
+    rows = mixed_at.shape[2]
+    blank[...] = jnp.zeros_like(blank)
+    blank_low[...] = jnp.zeros_like(blank_low)
+    copies = []
+    for i, (src, dst, zero) in enumerate(((tgrad, tgrad_at, blank), (mixed, mixed_at, blank_low))):
+        first, after = dst.at[1 - long, 0, 0:GROUP, :], dst.at[1 - long, 0, GROUP:rows, :]
+        whole = pltpu.make_async_copy(src.at[0:rows, :], dst.at[long, 0], sems.at[3 * i])
+        used = pltpu.make_async_copy(src.at[rows : rows + GROUP, :], first, sems.at[3 * i + 1])
+        unused = pltpu.make_async_copy(zero.at[0:GROUP, :], first, sems.at[3 * i + 1])
+        end = pltpu.make_async_copy(zero.at[0 : rows - GROUP, :], after, sems.at[3 * i + 2])
+        whole.start()
+        pl.when(seq == 0)(used.start)
+        pl.when(seq > 0)(unused.start)
+        end.start()
+        copies += [whole, used, end]
+    in_at[...] = grad_in[...]
+    out_at[...] = grad_out[...]
+    conv[:, 0:INNER] = small[0:CONV, CX:]
+    conv[:, INNER:] = small[0:CONV, 0:CX]
+    bias[...] = jnp.concatenate([small[4:5, CX:], small[4:5, 0:CX]], axis=1).reshape(CONVCH)
+    gain[...] = small[5:6, 0:INNER].reshape(INNER)
+    step[...] = small[5:6, INNER : INNER + HEADS].reshape(HEADS)
+    rates[...] = small[5:6, INNER + LANES : INNER + LANES + HEADS].reshape(HEADS)
+    skip[...] = small[6:7, 0:HEADS].reshape(HEADS)
+    norm[...] = small[7:8, 0:D].reshape(D)
+    for c in copies:
+        c.wait()
+
+
+def call_place(shape, lengths, *arrays):
+    vmem = pl.BlockSpec(memory_space=pltpu.VMEM)
+    hbm = pl.BlockSpec(memory_space=pl.ANY)
+    own = arrays[3].shape[0]
+    outs = (
+        (shape, BF), (shape, F32), ((D,), F32), ((own, PROJ), F32), ((CONV, CONVCH), F32),
+        ((CONVCH,), F32), ((HEADS,), F32), ((HEADS,), F32), ((HEADS,), F32), ((INNER,), F32),
+        ((own, INNER), F32),
+    )
+    rest = max(shape[2] - GROUP, GROUP)
+    results = pl.pallas_call(
+        place_results,
+        out_shape=[jax.ShapeDtypeStruct(s, t) for s, t in outs],
+        in_specs=[pl.BlockSpec(memory_space=pltpu.SMEM)] + [vmem] * len(arrays),
+        out_specs=[hbm, hbm] + [vmem] * (len(outs) - 2),
+        scratch_shapes=[
+            pltpu.VMEM((rest, D), F32), pltpu.VMEM((rest, D), BF), pltpu.SemaphoreType.DMA((6,)),
+        ],
+        name="place_results",
+    )(lengths, *arrays)
+    return (*results[:-1], results[-1].T)
 
 
 def shards(
@@ -950,69 +1131,32 @@
     out_gain, out_weight, out_grad,
 ):
     both = ("fsdp", "seq")
-    row_count = tokens.shape[2]
     own = in_weight.shape[0]
     nf = lax.axis_size("fsdp")
     fused = nf % PLANE == 0 and (2 * own) % 16 == 0 and own % 8 == 0
     nz = nf // PLANE if fused else 1
-    positions = lax.axis_index("seq") * row_count + jnp.arange(row_count, dtype=jnp.int32)
-    first_long = lengths[0, 0] > lengths[1, 0]
-    short_valid = (positions < jnp.minimum(lengths[0, 0], lengths[1, 0]))[:, None]
-
-    def packed(a):
-        return jnp.concatenate(
-            [jnp.where(first_long, a[0, 0], a[1, 0]),
-             jnp.where(first_long, a[1, 0, :GROUP], a[0, 0, :GROUP])], axis=0)
-
-    tok = packed(tokens)
-    og = packed(out_grad)
-    mask = jnp.concatenate([jnp.ones((row_count, 1), bool), short_valid[:GROUP]], axis=0)
-    og = jnp.where(mask, og, jnp.zeros_like(og))
-    kind = F32 if fused else BF
-    own_weights = jnp.concatenate(
-        [in_weight[:, 2 * INNER :], jnp.zeros((own, 2 * LANES - HEADS), BF),
-         in_weight[:, INNER : 2 * INNER], in_weight[:, :INNER], out_weight.T], axis=1
-    ).astype(kind)
-    weights = own_weights
-    if not fused:
-        weights = lax.all_gather(own_weights, both, axis=0, tiled=True)
-
-    def key_first(a):
-        return jnp.concatenate([a[..., INNER:], a[..., :INNER]], axis=-1)
-
-    convp = key_first(
-        jnp.concatenate([conv_weight, conv_bias[None], jnp.zeros((3, CONVCH), F32)], axis=0)
-    )
-    headp = jnp.pad(jnp.stack([dt_bias, a_log]), ((0, 6), (0, LANES - HEADS)))
-    innerp = jnp.pad(jnp.stack([out_gain, jnp.repeat(skip_gain, HEADDIM)]), ((0, 6), (0, 0)))
-    mixed, tgrad, small, wsum = call_mixer(
-        fused, nz, tok, og, weights, norm_gain[None], convp, headp, innerp
-    )
+    arrays = {
+        "lengths": lengths, "tokens": tokens, "out_grad": out_grad, "norm_gain": norm_gain,
+        "conv_weight": conv_weight, "conv_bias": conv_bias, "dt_bias": dt_bias, "a_log": a_log,
+        "skip_gain": skip_gain, "out_gain": out_gain,
+    }
     if fused:
-        chunks = wsum[:QUADS].transpose(2, 0, 1, 3).reshape(own, QUADS, 3, 256)
-        rest = wsum[QUADS, :, :, :256].transpose(1, 0, 2).reshape(own, AT_X)
+        arrays |= {"in_weight": in_weight, "out_weight": out_weight.T}
+        mixed, tgrad, small, grad_in, grad_out = call_mixer(fused, nz, arrays)
     else:
-        summed = lax.psum_scatter(wsum, both, scatter_dimension=0, tiled=True).astype(F32)
-        chunks = summed[:, : QUADS * CHUNK].reshape(own, QUADS, 3, 256)
-        rest = summed[:, QUADS * CHUNK :]
+        fill = jnp.zeros((own, AT_X - CX - HEADS), BF)
+        sent = jnp.concatenate(
+            [in_weight[:, 2 * INNER :], fill, in_weight[:, INNER : 2 * INNER],
+             in_weight[:, :INNER], out_weight.T], axis=1)
+        arrays["w"] = lax.all_gather(sent, both, axis=0, tiled=True)
+        mixed, tgrad, small, wgrad = call_mixer(fused, nz, arrays)
+        summed = lax.psum_scatter(wgrad, both, scatter_dimension=0, tiled=True).astype(F32)
+        grad_out = summed[:, :INNER]
+        grad_in = jnp.concatenate(
+            [summed[:, INNER : 3 * INNER], summed[:, 3 * INNER : 3 * INNER + CX + HEADS]], axis=1
+        )
         small = lax.psum(small, both)
-    x_grad, gate_grad, out_w_grad = (chunks[:, :, i].reshape(own, INNER) for i in range(3))
-    in_grad = jnp.concatenate([gate_grad, x_grad, rest[:, : AT_DT + HEADS]], axis=1)
-    conv_g = jnp.concatenate([small[:5, CX:], small[:5, :CX]], axis=1)
-
-    def unpacked(a):
-        long = a[:row_count]
-        short = jnp.where(short_valid, jnp.pad(a[row_count:], ((0, row_count - GROUP), (0, 0))), 0)
-        short = short.astype(a.dtype)
-        return jnp.stack([jnp.where(first_long, long, short), jnp.where(first_long, short, long)])[
-            :, None
-        ]
-
-    return (
-        unpacked(mixed), unpacked(tgrad), small[7, :D], in_grad, conv_g[:4], conv_g[4],
-        small[5, INNER : INNER + HEADS], small[5, INNER + LANES : INNER + LANES + HEADS],
-        small[6, :INNER].reshape(HEADS, HEADDIM).sum(1), small[5, :INNER], out_w_grad.T,
-    )
+    return call_place(tokens.shape, lengths, mixed, tgrad, small, grad_in, grad_out)
 
 
 def solution(mesh):

time: 199 us -> 182 us (0.915)
  other arithmetic: 13.8 us -> 0 us
  local copies, waits for them, and re-layouts: 9.39 us -> 1.32 us
  Pallas kernels: 172 us -> 179 us
  between operations: 3.49 us -> 0.81 us
    pallas_call x0 -> x1, Pallas kernels: none -> 5.14 us  [call_place(): pl.pallas_call(place_results, out_shape=[jax.ShapeDtypeStruct(s, t) for s...]
    slice x15 -> x0, local copies, waits for them, and re-layouts: 3.81 us -> none  [the longest x1 1.31 us: shards(): first_long = lengths[0, 0] > lengths[1, 0]]
    select_n x3 -> x0, other arithmetic: 3.52 us -> none  [the longest x1 2.15 us: packed(): jnp.where(first_long, a[0, 0], a[1, 0])]
    concatenate x5 -> x0, other arithmetic: 3.16 us -> none  [the longest x1 1.09 us: packed(): jnp.concatenate([jnp.where(first_long, a[0, 0], a[1, 0]), jnp.where(first...]
    unnamed x2 -> x0, other arithmetic: 3.15 us -> none
    pallas_call x1, Pallas kernels: 172 us -> 174 us  [call_mixer(): pl.pallas_call(functools.partial(mixer, names, fused, nz), out_shape=[jax...]
where the time goes in v3:
time: 182 us; the launch traced here: 181 us
  Pallas kernels  179 us (98%)
    pallas_call x1, Pallas kernels, call_mixer(): pl.pallas_call(functools.partial(mixer, names, fused, nz), out_shape=[jax...  174 us
    pallas_call x1, Pallas kernels, call_place(): pl.pallas_call(place_results, out_shape=[jax.ShapeDtypeStruct(s, t) for s...  5.14 us

profile of v3, /device:TPU:0, one launch (start us, length us, event | category | flops | bytes accessed | tf_op | source)
XLA Modules:
  0.0 181.3 jit_solution(3565656812312288285)
XLA Ops:
  0.6 1.3 copy.24.refs_0_.lengths
  2.0 174.1 %mixer.1 = (bf16[768,768]{1,0:T(8,128)(2,1)}, f32[768,768]{1,0:T(8,128)}, f32[8,1792]{1,0:T(8,128)}, f32[24,3352]{1,0:T(8,128)}, f32[24,1536]{1,0:T(8,128)}) custom-call(s32[2,1]{1,0:T(2,128)} %copy.24.refs_0_.lengths, bf16[2,1,512,768]{3,2,1,0:T(8,128)(2,1)} %refs_1_.1, bf16[2,1,512,768]{3,2,1,0:T(8,128)(2,1)} %refs_2_.1, f32[768]{0:T(1024)} %refs_3_.1, ...), custom_call_target="tpu_custom_call" | custom-call | tf_op jit(solution)/shard_map/mixer/pallas_call | solution.py:1058
  176.0 5.1 %place_results.1 = (bf16[2,1,512,768]{3,2,1,0:T(8,128)(2,1)}, f32[2,1,512,768]{3,2,1,0:T(8,128)}, f32[768]{0:T(1024)}, f32[24,3352]{1,0:T(8,128)}, f32[4,1792]{1...) custom-call(s32[2,1]{1,0:T(2,128)} %copy.24.refs_0_.lengths, ...), custom_call_target="tpu_custom_call" | custom-call | tf_op jit(solution)/shard_map/place_results/pallas_call | solution.py:1116

commit v4 on v3

--- a/solution.py
+++ b/solution.py
@@ -131,12 +131,16 @@
     def on_chain(j):
         return {"fsdp": z_peer(j) * PLANE + p_at}
 
+    own = D // (2 * nz * PLANE) if fused else 0
     peers = [sibling]
     if fused:
         peers += [on_plane(j) for j in range(1, PLANE)] + [on_chain(j) for j in range(1, nz)]
     barrier = pltpu.get_barrier_semaphore()
     for peer in peers:
         pl.semaphore_signal(barrier, inc=1, device_id=peer, device_id_type=MESH)
+
+    def own_columns(ref, c):
+        return ref.at[c * own : (c + 1) * own, 0 : GATHERS[c][1]]
 
     part_rows = r.tokens.shape[2]
     raw = [buf.at[0:part_rows, m * D : (m + 1) * D] for buf in (r.dssd, r.cout) for m in range(2)]
@@ -148,13 +152,14 @@
 
     if fused:
         wide = 2 * INNER
-        r.shard[:, 0:CX] = r.in_weight[:, wide : wide + CX].astype(F32)
         steps = r.in_weight[:, wide + CX :].astype(F32)
         fill = jnp.zeros((steps.shape[0], AT_X - CX - HEADS), F32)
-        r.shard[:, CX:AT_X] = jnp.concatenate([steps, fill], axis=1)
-        r.shard[:, AT_X:AT_GATE] = r.in_weight[:, INNER:wide].astype(F32)
-        r.shard[:, AT_GATE:AT_OUT] = r.in_weight[:, 0:INNER].astype(F32)
-        r.shard[:, AT_OUT:] = r.out_weight[...].astype(F32)
+        key_query = r.in_weight[:, wide : wide + CX].astype(F32)
+        own_columns(r.gate, 0)[...] = jnp.concatenate([key_query, steps, fill], axis=1)
+        own_columns(r.gate, 1)[...] = r.in_weight[:, INNER : INNER + 512].astype(F32)
+        own_columns(r.gate, 2)[...] = r.in_weight[:, INNER + 512 : wide].astype(F32)
+        own_columns(r.gate, 3)[...] = r.in_weight[:, 0:INNER].astype(F32)
+        own_columns(r.gate, 4)[...] = r.out_weight[...].astype(F32)
 
     pl.semaphore_wait(barrier, len(peers))
 
@@ -168,7 +173,6 @@
         return remote(src, dst, r.pair_send.at[i], r.pair_recv.at[i], sibling)
 
     w = r.w
-    own = D // (2 * nz * PLANE) if fused else 0
     slab = 2 * own
 
     def part(c):
@@ -180,10 +184,10 @@
 
     def gather_copy(c, k, index, device):
         at = w.at[slab_of(index), part(c)]
-        return remote(at, at, r.g_send.at[c, k], r.g_recv.at[c, k], device)
+        return remote(at, at, r.g_send.at[c, 0], r.g_recv.at[c, k], device)
 
     def chain_copy(c, j):
-        return gather_copy(c, j - 1, f, on_chain(j))
+        return gather_copy(c, 0, f, on_chain(j))
 
     def plane_copy(c, kind, back):
         low, size = GATHERS[c]
@@ -192,18 +196,21 @@
         if kind >= 2:
             cols = span(low + seq * (size // 2) + (kind - 2) * (size // 4), size // 4, 128)
         at = w.at[slab_of((z_at - back + nz) % nz * PLANE + owner), cols]
-        k = nz - 1 + back * 4 + kind
         device = on_plane((1, 2, 2, 1)[kind])
-        return remote(at, at, r.g_send.at[c, k], r.g_recv.at[c, k], device)
+        return remote(at, at, r.g_send.at[c, 0], r.g_recv.at[c, 1 + kind // 2], device)
 
     def last_copy(c):
         at = w.at[:, part(c)]
-        k = nz - 1 + 4 * nz
-        return remote(at, at, r.g_send.at[c, k], r.g_recv.at[c, k], sibling)
+        return remote(at, at, r.g_send.at[c, 1], r.g_recv.at[c, 3], sibling)
+
+    def wait_bytes(rows, cols, sem):
+        at = w.at[0 : rows * slab // 2, cols]
+        pltpu.make_async_copy(at, at, sem).wait()
 
     def gather_own(c):
         cols = part(c)
-        mine, theirs = r.shard[:, cols], r.shard_in[:, cols]
+        half_cols = span(seq * (GATHERS[c][1] // 2), GATHERS[c][1] // 2, 128)
+        mine, theirs = (own_columns(ref, c)[:, half_cols] for ref in (r.gate, r.back))
         first = jnp.where(seq == 0, mine, theirs)
         second = jnp.where(seq == 0, theirs, mine)
         w[slab_of(f), cols] = jnp.concatenate([first, second], axis=0).astype(BF)
@@ -217,32 +224,26 @@
             plane_copy(c, kind, 0).start()
 
     def gather_2(c):
+        wait_bytes(2 * (nz - 1), part(c), r.g_recv.at[c, 0])
         for back in range(1, nz):
-            chain_copy(c, back).wait_recv()
             for kind in range(2):
                 plane_copy(c, kind, back).start()
 
     def gather_3(c):
+        wait_bytes(4 * nz, part(c), r.g_recv.at[c, 1])
         for back in range(nz):
             for kind in range(2):
-                plane_copy(c, kind, back).wait_recv()
                 plane_copy(c, kind + 2, back).start()
 
     def gather_4(c):
-        for back in range(nz):
-            for kind in range(2, 4):
-                plane_copy(c, kind, back).wait_recv()
+        wait_bytes(2 * nz, part(c), r.g_recv.at[c, 2])
         last_copy(c).start()
 
     def gather_5(c):
         last_copy(c).wait_recv()
 
     def gather_end(c):
-        for j in range(1, nz):
-            chain_copy(c, j).wait_send()
-        for kind in range(4):
-            for back in range(nz):
-                plane_copy(c, kind, back).wait_send()
+        wait_bytes(2 * (nz - 1) + 6 * nz, part(c), r.g_send.at[c, 0])
         last_copy(c).wait_send()
 
     def wide_chunk(i):
@@ -262,24 +263,26 @@
     def sum_copy_0(g):
         src = r.wg.at[g[1], :, :, :, source(g, 1 - seq)]
         dst = r.r0.at[g[4], :, :, :, target(g)]
-        return remote(src, dst, r.s_send.at[g[0], 0], r.s_recv.at[g[0], 0], sibling)
+        return remote(src, dst, r.s_send.at[g[0]], r.s_recv.at[g[0], 0], sibling)
 
     def sum_copy_1(g, j):
         src = r.wg.at[g[1], :, plane_peer(j), :, source(g, seq)]
         dst = r.r1.at[g[4], j - 1, :, :, target(g)]
-        return remote(src, dst, r.s_send.at[g[0], j], r.s_recv.at[g[0], j], on_plane(j))
+        return remote(src, dst, r.s_send.at[g[0]], r.s_recv.at[g[0], 1], on_plane(j))
 
     def sum_copy_2(g, j):
-        k = PLANE - 1 + j
         src = r.wg.at[g[1], z_peer(j), p_at, :, source(g, seq)]
         dst = r.r2.at[g[4], j - 1, :, target(g)]
-        return remote(src, dst, r.s_send.at[g[0], k], r.s_recv.at[g[0], k], on_chain(j))
+        return remote(src, dst, r.s_send.at[g[0]], r.s_recv.at[g[0], 2], on_chain(j))
 
     def sum_copy_3(g):
-        k = PLANE - 1 + nz
         src = r.fin.at[g[4], span((1 - seq) * own, own, 8), target(g)]
         dst = r.gsum.at[g[4], :, target(g)]
-        return remote(src, dst, r.s_send.at[g[0], k], r.s_recv.at[g[0], k], sibling)
+        return remote(src, dst, r.s_send.at[g[0]], r.s_recv.at[g[0], 3], sibling)
+
+    def finish_all(g, level, at):
+        pltpu.make_async_copy(at, at, r.s_send.at[g[0]]).wait()
+        pltpu.make_async_copy(at, at, r.s_recv.at[g[0], level]).wait()
 
     def finish(copy):
         copy.wait_send()
@@ -306,8 +309,7 @@
     def sum_2(g):
         if not fused:
             return
-        for j in range(1, PLANE):
-            finish(sum_copy_1(g, j))
+        finish_all(g, 1, r.r1.at[g[4], :, :, :, target(g)])
 
         def add(zi):
             at = (g[1], zi, p_at, slice(None), source(g, seq))
@@ -323,8 +325,7 @@
     def sum_3(g):
         if not fused:
             return
-        for j in range(1, nz):
-            finish(sum_copy_2(g, j))
+        finish_all(g, 2, r.r2.at[g[4], :, :, target(g)])
         value = r.wg[g[1], z_at, p_at, :, source(g, seq)].astype(F32)
         for j in range(nz - 1):
             value = value + r.r2[g[4], j, :, target(g)].astype(F32)
@@ -344,9 +345,9 @@
             r.wgrad[:, span(first + low, size, 128)] = value.astype(BF)
 
     def shard_copy(c):
-        low, size = GATHERS[c]
-        cols = span(low + (1 - seq) * (size // 2), size // 2, 128)
-        return pair_copy(4 + c, r.shard.at[:, cols], r.shard_in.at[:, cols])
+        size = GATHERS[c][1] // 2
+        rows, cols = slice(c * own, (c + 1) * own), span((1 - seq) * size, size, 128)
+        return pair_copy(1, r.gate.at[rows, cols], r.back.at[rows, cols])
 
     if fused:
         for c in range(len(GATHERS)):
@@ -358,8 +359,10 @@
         r.spread[:, span(q * 256, 256)] = (head == (iota(shape, 0) & 127)).astype(F32).astype(BF)
 
     if fused:
+        at = r.back.at[0 : own * (WIDE // 2) // INNER, :]
+        for sem in (r.pair_send.at[1], r.pair_recv.at[1]):
+            pltpu.make_async_copy(at, at, sem).wait()
         for c in range(len(GATHERS)):
-            shard_copy(c).wait()
             gather_own(c)
             if c < 2:
                 gather_0(c)
@@ -444,6 +447,7 @@
     if fused:
         gather_2(1)
         gather_3(0)
+        gather_1(3)
         gather_4(0)
         gather_3(1)
         gather_5(0)
@@ -497,6 +501,27 @@
         r.sco[b] = dot_nt(query, key)
 
     loop(BLOCKS, prepare)
+    if fused:
+        gather_2(2)
+        gather_0(4)
+        gather_4(1)
+        gather_1(4)
+        gather_5(1)
+
+    gather_steps = (
+        (1, gather_3, 2), (1, gather_2, 3), (2, gather_4, 2), (2, gather_5, 2), (3, gather_2, 4),
+        (4, gather_3, 3),
+    )
+
+    def gather_on(q):
+        if fused:
+            for point in range(QUADS):
+
+                @pl.when(q == point)
+                def _():
+                    for at, step, c in gather_steps:
+                        if at == point:
+                            step(c)
 
     def to_first(v, q):
         return pltpu.roll(v, (LANES - 4 * q) % LANES, 1)
@@ -509,8 +534,7 @@
             conv_forward(b, span(CX + q * 256 + i * LANES, LANES))
         xq = r.cout[rows, cols]
 
-        @pl.when(b < 2)
-        def _():
+        if b < 2:
             spread_w = dot(r.weight[rows, :], r.spread[:, heads])
             scaled = (xq.astype(F32) * spread_w).astype(BF)
             r.runs[b, :, heads] = dot(r.turned[b, 0:NSTATE, :], scaled)
@@ -544,42 +568,10 @@
             r.ssd[span(b * GROUP + half, half), place] = out_bottom + xf[half:]
 
     def forward_quad(q):
-        if fused:
-
-            @pl.when(q == 0)
-            def _():
-                gather_2(2)
-                gather_0(4)
-                gather_4(1)
-                gather_1(3)
-                gather_5(1)
-
-            @pl.when(q == 1)
-            def _():
-                gather_3(2)
-                gather_2(3)
-
-            @pl.when(q == 2)
-            def _():
-                gather_4(2)
-                gather_1(4)
-                gather_3(3)
-                gather_5(2)
-
-            @pl.when(q == 3)
-            def _():
-                gather_2(4)
-
-            @pl.when(q == 4)
-            def _():
-                gather_4(3)
-
-            @pl.when(q == 5)
-            def _():
-                gather_3(4)
-
+        gather_on(q)
         project(span(AT_X + q * 256, 256), span(CX + q * 256, 256))
-        loop(BLOCKS, lambda b: forward_block(b, q))
+        for b in range(BLOCKS):
+            forward_block(b, q)
 
     loop(QUADS, forward_quad)
 
@@ -592,8 +584,7 @@
     state_copy = pair_copy(2, r.runs.at[1], r.state_in)
     state_copy.start()
     if fused:
-        gather_4(4)
-        gather_5(3)
+        gather_4(3)
 
     def carry_block(b):
         rows = rows_of(b)
@@ -613,8 +604,10 @@
         rows = rows_of(b)
 
         def quad(q):
-            cols = span(q * 256, 256)
-            r.gate[:, cols] = dot(r.normed[rows, :], w[:, span(AT_GATE + q * 256, 256)])
+            at = span(AT_GATE + q * 256, 256)
+            high, low = halves(dot(r.normed[rows, :], w[:, at]))
+            r.dssd[rows, span(q * 256, 256)] = high
+            r.dproj[rows, at] = low
 
         loop(QUADS, quad)
 
@@ -627,20 +620,31 @@
 
         loop(QUADS, quad)
 
+    def gated_rows(here):
+        g = r.dssd[here, :].astype(F32) + r.dproj[here, AT_GATE:AT_OUT].astype(F32)
+        s = r.ssd[here, :]
+        sg = sigmoid(g)
+        silu = g * sg
+        gated = s * silu
+        root = lax.rsqrt(jnp.mean(gated * gated, axis=1, keepdims=True) + EPS)
+        return g, s, sg, silu, gated, root
+
+    def gate_forward(i):
+        for k in range(2):
+            here = span(i * 32 + k * 16, 16)
+            _, _, _, _, gated, root = gated_rows(here)
+            r.dproj[here, AT_X:AT_GATE] = (gated * root * gain).astype(BF)
+
     def gate_block(b):
         def gate_rows(i):
             here = span(b * GROUP + i * 16, 16)
-            local = span(i * 16, 16)
-            d_out, g, s = r.back[local, :], r.gate[local, :], r.ssd[here, :]
-            sg = sigmoid(g)
-            silu = g * sg
-            gated = s * silu
-            root = lax.rsqrt(jnp.mean(gated * gated, axis=1, keepdims=True) + EPS)
+            d_out = r.back[span(i * 16, 16), :]
+            g, s, sg, silu, gated, root = gated_rows(here)
+            a = gain * d_out
+            lean = root * jnp.mean(gated * a, axis=1, keepdims=True)
             v = gated * root
-            r.dproj[here, AT_X:AT_GATE] = (v * gain).astype(BF)
             r.g_inner[0:8, :] += fold(d_out * v)
-            a = gain * d_out
-            d_gated = root * (a - v * jnp.mean(v * a, axis=1, keepdims=True))
+            d_gated = root * (a - v * lean)
             d_s = (d_gated * silu).astype(BF)
             r.dssd[here, :] = d_s
             r.g_inner[8:16, :] += fold(d_s.astype(F32) * r.cout[here, CX:].astype(F32))
@@ -648,11 +652,6 @@
 
         loop(GROUP // 16, gate_rows)
 
-    gate_project(2)
-    if fused:
-        gather_5(4)
-    out_back(2)
-    gate_block(2)
     state_copy.wait()
     r.state_in[...] = r.state_in[...] * is_second
     r.held[0] = r.state_in[...].astype(BF)
@@ -660,13 +659,11 @@
     r.held[1] = r.runs[0].astype(BF)
     r.runs[1] = r.state_in[...]
 
-    def gate_long(b):
-        gate_project(b)
-        out_back(b)
-        carry_block(b)
-        gate_block(b)
-
-    loop(2, gate_long)
+    @pl.when(seq > 0)
+    def _():
+        carry_block(0)
+
+    carry_block(1)
 
     def wide_grad(i):
         g = wide_chunk(i)
@@ -679,9 +676,26 @@
         loop(CHUNK // 256, tile)
         sum_0(g)
 
-    for i in range(WIDE_CHUNKS):
-        wide_grad(i)
-    sum_1(wide_chunk(0))
+    if fused:
+        gather_5(3)
+    loop(BLOCKS, gate_project)
+    if fused:
+        gather_3(4)
+    loop(ROWS // 32, gate_forward)
+    if fused:
+        gather_4(4)
+    wide_grad(0)
+    wide_grad(1)
+    if fused:
+        gather_5(4)
+    for b in range(BLOCKS):
+        out_back(b)
+        gate_block(b)
+        if b < 2:
+            sum_1(wide_chunk(b))
+    wide_grad(2)
+    wide_grad(3)
+    sum_2(wide_chunk(0))
 
     def state_back(b):
         rows = rows_of(b)
@@ -695,12 +709,18 @@
 
         r.dqb[rows, :] = lax.fori_loop(0, QUADS, quad, jnp.zeros((GROUP, NSTATE), F32))
 
-    loop(2, state_back)
+    def no_state():
+        r.dheld[0] = jnp.zeros((NSTATE, INNER), F32)
+
+    r.dqb[0:GROUP, :] = jnp.zeros((GROUP, NSTATE), F32)
+    pl.when(seq > 0)(lambda: state_back(0))
+    pl.when(seq == 0)(no_state)
+    state_back(1)
     r.dqb[2 * GROUP :, :] = jnp.zeros((GROUP, NSTATE), F32)
     r.dheld[0] = r.dheld[0] + decay_0 * r.dheld[1]
     dstate_copy = pair_copy(3, r.dheld.at[0], r.dstate_in)
     dstate_copy.start()
-    sum_1(wide_chunk(1))
+    sum_1(wide_chunk(2))
 
     def out_block(b):
         rows = rows_of(b)
@@ -710,7 +730,9 @@
     loop(BLOCKS, out_block)
     mixed_copy = pltpu.make_async_copy(r.normed.at[0:ROWS, :], r.mixed, r.local.at[0])
     mixed_copy.start()
-    sum_1(wide_chunk(2))
+    sum_1(wide_chunk(3))
+    sum_2(wide_chunk(1))
+    sum_3(wide_chunk(0))
 
     def ds_of(b):
         return r.back.at[:, heads_of(b)]
@@ -718,8 +740,14 @@
     def give_of(b):
         return r.back.at[:, span(CHUNK + b * LANES, LANES)]
 
-    def take_of(b):
+    def kept_of(b):
         return r.back.at[:, span(CHUNK + (BLOCKS + b) * LANES, LANES)]
+
+    def pick_heads(q):
+        row, lane = iota((8 * LANES, LANES), 0), iota((8 * LANES, LANES), 1)
+        pair, kind, second = row >> 9, (row >> 8) & 1, (row & 127) >> 6
+        head = 4 * q + 2 * pair + second + 64 * kind
+        r.pick[...] = (lane == head).astype(F32).astype(BF)
 
     def prepare_back(b):
         rows = rows_of(b)
@@ -728,7 +756,6 @@
         nothing = jnp.zeros((GROUP, LANES), F32)
         r.dkb[rows, :] = nothing
         give_of(b)[...] = nothing
-        take_of(b)[...] = nothing
 
     loop(BLOCKS, prepare_back)
     dstate_copy.wait()
@@ -744,22 +771,16 @@
         dq4 = r.dssd[rows, heads]
         skip = r.innerp[1:2, heads]
         dx, ds = r.gate.at[:, heads_of(b)], ds_of(b)
-        give, take = give_of(b), take_of(b)
-
-        @pl.when(b < 2)
-        def _():
+
+        if b < 2:
             spread_w = dot(r.weight[rows, :], r.spread[:, heads])
             d_states = r.dst[b, :, heads]
             dx_state = spread_w * dot(r.cout[rows, 0:NSTATE], d_states)
             r.flow[b, 0:8, heads] = fold(xq.astype(F32) * dx_state)
             r.dkb[rows, :] += dot_nt((xq.astype(F32) * spread_w).astype(BF), d_states)
-            dx[...] = dx_state
-
-        @pl.when(b == 2)
-        def _():
-            dx[...] = jnp.zeros((GROUP, 256), F32)
 
         near = to_first(r.moved[rows, :], q)
+        products = []
         for j in range(2):
             lanes = slice(j * LANES, (j + 1) * LANES)
             xp, dp = xq[:, lanes], dq4[:, lanes]
@@ -786,15 +807,15 @@
             dx_bottom = dot(
                 jnp.concatenate(bottom, axis=1), jnp.concatenate([v[half:] for v in d_ab], axis=0)
             )
-            dxp = jnp.concatenate([dx_top, dx_bottom], axis=0) + dx[:, lanes]
+            dxp = jnp.concatenate([dx_top, dx_bottom], axis=0)
+            if b < 2:
+                dxp = dxp + dx_state[:, lanes]
             xf, df = xp.astype(F32), dp.astype(F32)
             kept = skip[:, lanes]
-            head = 4 * q + 2 * j + ((iota((2 * LANES, LANES), 0) & 127) >> 6)
-            pick = (iota((2 * LANES, LANES), 1) == head).astype(F32).astype(BF)
             ssd = r.ssd[rows, span(q * 256 + j * LANES, LANES)]
-            give[...] += dot(side_by_side(xf * dxp), pick)
-            take[...] += dot(side_by_side(df * (ssd - kept * xf)), pick)
+            products += [*halves(xf * dxp), *halves(df * (ssd - kept * xf))]
             dx[:, lanes] = dxp + kept * df
+        give_of(b)[...] += dot(jnp.concatenate(products, axis=1), r.pick[...])
 
     def edge_grad(b, source, cols):
         first = r.clow[b * GROUP : b * GROUP + 16, cols].astype(F32)
@@ -819,6 +840,11 @@
         src, dst = r.halo_next.at[0, :, cols], r.dedge_in.at[:, cols]
         return remote(src, dst, r.edge_send.at[i], r.edge_recv.at[i], sibling)
 
+    def first_edge(i, at):
+        for k in range(2):
+            edge_grad(0, k * LANES, span(at + k * LANES, LANES))
+        edge_copy_back(i, span(at, 256)).start()
+
     def conv_back_all(i, at, to):
         cols = span(at, 256)
 
@@ -826,9 +852,7 @@
             return k * LANES, span(at + k * LANES, LANES), span(to + k * LANES, LANES)
 
         for k in range(2):
-            edge_grad(0, *chunk(k)[:2])
             edge_grad(1, *chunk(k)[:2])
-        edge_copy_back(i, cols).start()
         for k in range(2):
             conv_back(2, *chunk(k), jnp.zeros((8, LANES), F32))
             conv_back(0, *chunk(k), r.halo_next[1, :, chunk(k)[1]])
@@ -837,23 +861,28 @@
             conv_back(1, *chunk(k), r.dedge_in[:, chunk(k)[1]] * is_first)
 
     def backward_quad(q):
-        for i in range(WIDE_CHUNKS):
-
-            @pl.when(q == i)
-            def _():
-                sum_2(wide_chunk(i))
+        @pl.when(q == 1)
+        def _():
+            sum_2(wide_chunk(2))
+
+        @pl.when(q == 2)
+        def _():
+            sum_3(wide_chunk(2))
+            sum_2(wide_chunk(3))
+
+        @pl.when(q == 3)
+        def _():
+            sum_3(wide_chunk(3))
+
+        pick_heads(q)
+        for b in range(BLOCKS):
+            backward_block(b, q)
+            if b == 0:
+                first_edge(q, CX + q * 256)
 
         @pl.when(q == 0)
         def _():
-            sum_1(wide_chunk(3))
-
-        loop(BLOCKS, lambda b: backward_block(b, q))
-
-        for i in range(WIDE_CHUNKS):
-
-            @pl.when(q == i)
-            def _():
-                sum_3(wide_chunk(i))
+            sum_3(wide_chunk(1))
 
         @pl.when(q >= 1)
         def _():
@@ -874,17 +903,22 @@
 
     loop(QUADS, backward_quad)
 
+    def ratio_of(b):
+        z, step = head_rows(b)
+        return jnp.where(z < -15.0, 1.0, sigmoid(z) / jnp.maximum(step, 1e-37))
+
     def backward_rest(b):
         rows = rows_of(b)
         key, query = r.cout[rows, 0:NSTATE], r.cout[rows, NSTATE:CX]
         d_scores = ds_of(b)[...].astype(BF)
         r.gate[:, span(b * 256, NSTATE, 128)] = r.dkb[rows, :] + dot(d_scores, query)
         r.gate[:, span(b * 256 + NSTATE, NSTATE, 128)] = r.dqb[rows, :] + dot(d_scores.T, key)
-        give = give_of(b)[...]
-        give_of(b)[...] = exact_sum(upper, take_of(b)[...] - give)
-        z, step = head_rows(b)
-        ratio = jnp.where(z < -15.0, 1.0, sigmoid(z) / jnp.maximum(step, 1e-37))
-        take_of(b)[...] = give * ratio
+        both_sums = give_of(b)[...]
+        in_low = iota((GROUP, LANES), 1) < HEADS
+        give = jnp.where(in_low, both_sums, 0.0)
+        take = jnp.where(in_low, pltpu.roll(both_sums, 64, 1), 0.0)
+        kept_of(b)[...] = give * ratio_of(b)
+        give_of(b)[...] = exact_sum(upper, take - give)
 
     loop(BLOCKS, backward_rest)
 
@@ -903,13 +937,14 @@
         rows = rows_of(b)
         z, step = head_rows(b)
         back_sum = give_of(b)[...]
-        d_pre = take_of(b)[...] + rate * back_sum * sigmoid(z)
+        d_pre = kept_of(b)[...] + rate * back_sum * sigmoid(z)
         r.g_head[0:8, :] += fold(d_pre)
         r.g_head[8:16, :] += fold(back_sum * (step * rate))
         r.dproj[rows, AT_DT : AT_DT + LANES] = d_pre.astype(BF)
 
     loop(BLOCKS, step_grad)
     sum_1(quad_chunk(5))
+    first_edge(QUADS, 0)
     conv_back_all(QUADS, 0, 0)
     put_grad(last_chunk, 0, dot(r.normed_t[...], r.dproj[:, 0:AT_X]))
     sum_0(last_chunk)
@@ -925,7 +960,6 @@
     sum_2(quad_chunk(5))
     sum_3(quad_chunk(4))
     loop(2, in_block)
-    sum_2(last_chunk)
     sum_3(quad_chunk(5))
 
     def norm_back(i):
@@ -959,27 +993,29 @@
     r.small[0, 7:8, D:] = jnp.zeros((1, CONVCH - D), F32)
     if fused:
 
-        def exchange(level, first, count, device):
-            copies = []
+        def send_small(level, first, count, device):
             for j in range(count):
-                k = first + j
-                copy = remote(
-                    r.small.at[level], r.small_in.at[k], r.t_send.at[k], r.t_recv.at[k],
-                    device(j + 1),
-                )
-                copy.start()
-                copies.append(copy)
-            for copy in copies:
-                copy.wait()
+                sems = r.t_send.at[level], r.t_recv.at[level]
+                dst = r.small_in.at[first + j]
+                remote(r.small.at[level], dst, *sems, device(j + 1)).start()
+
+        def add_small(level, first, count):
+            at = r.small_in.at[first : first + count]
+            for sem in (r.t_send.at[level], r.t_recv.at[level]):
+                pltpu.make_async_copy(at, at, sem).wait()
             value = r.small[level]
             for j in range(count):
                 value = value + r.small_in[first + j]
             return value
 
-        r.small[1] = exchange(0, 0, 1, lambda j: sibling)
-        r.small[2] = exchange(1, 1, PLANE - 1, on_plane)
-        r.small_out[...] = exchange(2, PLANE, nz - 1, on_chain)
+        send_small(0, 0, 1, lambda j: sibling)
+        sum_2(last_chunk)
+        r.small[1] = add_small(0, 0, 1)
+        send_small(1, 1, PLANE - 1, on_plane)
         sum_3(last_chunk)
+        r.small[2] = add_small(1, 1, PLANE - 1)
+        send_small(2, PLANE, nz - 1, on_chain)
+
         def hand_out(g, dst, first, count):
             sum_4(g)
             mine = r.fin[g[4], span(seq * own, own, 8), target(g)]
@@ -996,6 +1032,7 @@
         for q in range(QUADS):
             hand_out(quad_chunk(q), r.grad_in, INNER + q * 256, 256)
         hand_out(last_chunk, r.grad_in, 2 * INNER, CX + HEADS)
+        r.small_out[...] = add_small(2, PLANE, nz - 1)
         for c in range(len(GATHERS)):
             gather_end(c)
     else:
@@ -1020,6 +1057,7 @@
         "dssd": ((ROWS, INNER), BF), "dproj": ((ROWS, AT_OUT), BF),
         "dtb": ((ROWS, LANES), F32), "cumb": ((ROWS, LANES), F32), "moved": ((ROWS, LANES), F32),
         "weight": ((ROWS, 256), BF), "fade": ((ROWS, 256), BF),
+        "pick": ((8 * LANES, LANES), BF),
         "cut": ((BLOCKS, QUADS, 8, GROUP), F32), "spread": ((256, INNER), BF),
         "turned": ((BLOCKS, CX, GROUP), BF), "sco": ((BLOCKS, GROUP, GROUP), F32), "dkb": ((ROWS, LANES), F32), "dqb": ((ROWS, LANES), F32),
         "runs": ((2, NSTATE, INNER), F32), "held": ((2, NSTATE, INNER), BF),
@@ -1032,25 +1070,24 @@
     }
     dma = pltpu.SemaphoreType.DMA
     sems = {
-        "pair_send": dma((9,)), "pair_recv": dma((9,)), "edge_send": dma((QUADS + 1,)),
+        "pair_send": dma((4,)), "pair_recv": dma((4,)), "edge_send": dma((QUADS + 1,)),
         "edge_recv": dma((QUADS + 1,)), "local": dma((6,)),
     }
     if fused:
         part = CHUNK // 2
         outs |= {"grad_in": ((own, PROJ), F32), "grad_out": ((own, INNER), F32)}
         scratch |= {
-            "w": ((D, WIDE), BF), "shard": ((own, WIDE), F32), "shard_in": ((own, WIDE), F32),
+            "w": ((D, WIDE), BF),
             "wg": ((SLOTS, nz, PLANE, 2 * own, CHUNK), BF),
             "r0": ((UNITS, nz, PLANE, 2 * own, part), BF),
             "r1": ((UNITS, PLANE - 1, nz, 2 * own, part), BF),
             "r2": ((UNITS, nz - 1, 2 * own, part), BF), "fin": ((UNITS, 2 * own, part), F32),
             "gsum": ((UNITS, own, part), F32), "small_in": ((PLANE + nz - 1, 8, CONVCH), F32),
         }
-        arrivals = nz - 1 + 4 * nz + 1
         sems |= {
-            "g_send": dma((len(GATHERS), arrivals)), "g_recv": dma((len(GATHERS), arrivals)),
-            "s_send": dma((CHUNKS, PLANE + nz)), "s_recv": dma((CHUNKS, PLANE + nz)),
-            "t_send": dma((PLANE + nz - 1,)), "t_recv": dma((PLANE + nz - 1,)),
+            "g_send": dma((len(GATHERS), 2)), "g_recv": dma((len(GATHERS), 4)),
+            "s_send": dma((CHUNKS,)), "s_recv": dma((CHUNKS, 4)),
+            "t_send": dma((3,)), "t_recv": dma((3,)),
         }
     else:
         outs["wgrad"] = ((D, WIDE), BF)

time: 182 us -> 163 us (0.90)
  Pallas kernels: 179 us -> 160 us
    pallas_call x1, Pallas kernels: 174 us -> 155 us  [call_mixer(): pl.pallas_call(functools.partial(mixer, names, fused, nz), out_shape=[jax...]
where the time goes in v4:
time: 163 us; the launch traced here: 162 us
  Pallas kernels  160 us (98%)
    pallas_call x1, Pallas kernels, call_mixer(): pl.pallas_call(functools.partial(mixer, names, fused, nz), out_shape=[jax...  155 us
    pallas_call x1, Pallas kernels, call_place(): pl.pallas_call(place_results, out_shape=[jax.ShapeDtypeStruct(s, t) for s...  5.14 us

profile of v4, /device:TPU:0, one launch (start us, length us, event | category | flops | bytes accessed | tf_op | source)
XLA Modules:
  0.0 162.4 jit_solution(16499488945606582803)
XLA Ops:
  0.6 1.3 copy.24.refs_0_.lengths
  2.0 155.2 %mixer.1 = (bf16[768,768]{1,0:T(8,128)(2,1)}, f32[768,768]{1,0:T(8,128)}, f32[8,1792]{1,0:T(8,128)}, f32[24,3352]{1,0:T(8,128)}, f32[24,1536]{1,0:T(8,128)}) custom-call(s32[2,1]{1,0:T(2,128)} %copy.24.refs_0_.lengths, bf16[2,1,512,768]{3,2,1,0:T(8,128)(2,1)} %refs_1_.1, bf16[2,1,512,768]{3,2,1,0:T(8,128)(2,1)} %refs_2_.1, f32[768]{0:T(1024)} %refs_3_.1, ...), custom_call_target="tpu_custom_call" | custom-call | tf_op jit(solution)/shard_map/mixer/pallas_call | solution.py:1095
  157.2 5.1 %place_results.1 = (bf16[2,1,512,768]{3,2,1,0:T(8,128)(2,1)}, f32[2,1,512,768]{3,2,1,0:T(8,128)}, f32[768]{0:T(1024)}, f32[24,3352]{1,0:T(8,128)}, f32[4,1792]{1...) custom-call(s32[2,1]{1,0:T(2,128)} %copy.24.refs_0_.lengths, ...), custom_call_target="tpu_custom_call" | custom-call | tf_op jit(solution)/shard_map/place_results/pallas_call | solution.py:1153

commit v5 on v4

--- a/solution.py
+++ b/solution.py
@@ -94,12 +94,13 @@
     return lax.broadcasted_iota(jnp.int32, shape, dim)
 
 
-def loop(count, body):
+def loop(count, body, together=1):
     def step(i, _):
-        body(i)
+        for k in range(together):
+            body(i * together + k)
         return 0
 
-    lax.fori_loop(0, count, step, 0)
+    lax.fori_loop(0, count // together, step, 0)
 
 
 def silu_slope(v, sg):
@@ -302,7 +303,7 @@
             theirs = r.r0[g[4], i // PLANE, i % PLANE, :, target(g)]
             r.wg[at] = (r.wg[at].astype(F32) + theirs.astype(F32)).astype(BF)
 
-        loop(nz * PLANE, add)
+        loop(nz * PLANE, add, PLANE)
         for j in (3, 1, 2):
             sum_copy_1(g, j).start()
 
@@ -318,7 +319,7 @@
                 value = value + r.r1[g[4], j, zi, :, target(g)].astype(F32)
             r.wg[at] = value.astype(BF)
 
-        loop(nz, add)
+        loop(nz, add, 2 if nz % 2 == 0 else 1)
         for j in range(1, nz):
             sum_copy_2(g, j).start()
 
@@ -428,7 +429,7 @@
         rows = span(i * 64, 64)
         r.normed[rows, :] = norm_of(r.tok[rows, :].astype(F32))
 
-    loop(ROWS // 64, norm_rows)
+    loop(ROWS // 64, norm_rows, 2)
     edge_copy.wait()
     r.normed[ROWS:, :] = norm_of(r.edge_in[...].astype(F32) * is_second)
 
@@ -442,7 +443,7 @@
         r.normed_t[:, rows] = r.normed[rows, :].T
         r.db_t[:, rows] = r.og[rows, :].T
 
-    loop(BLOCKS, turn)
+    loop(BLOCKS, turn, BLOCKS)
 
     if fused:
         gather_2(1)
@@ -500,7 +501,7 @@
         r.turned[b, NSTATE:CX, :] = query.T
         r.sco[b] = dot_nt(query, key)
 
-    loop(BLOCKS, prepare)
+    loop(BLOCKS, prepare, BLOCKS)
     if fused:
         gather_2(2)
         gather_0(4)
@@ -596,20 +597,15 @@
                 r.fade[rows, :], r.spread[:, cols]
             )
 
-        loop(QUADS, quad)
+        loop(QUADS, quad, 3)
 
     gain = r.innerp[0:1, :]
 
-    def gate_project(b):
-        rows = rows_of(b)
-
-        def quad(q):
-            at = span(AT_GATE + q * 256, 256)
-            high, low = halves(dot(r.normed[rows, :], w[:, at]))
-            r.dssd[rows, span(q * 256, 256)] = high
-            r.dproj[rows, at] = low
-
-        loop(QUADS, quad)
+    def gate_project(q):
+        at = span(AT_GATE + q * 256, 256)
+        high, low = halves(dot(r.normed[0:ROWS, :], w[:, at]))
+        r.dssd[:, span(q * 256, 256)] = high
+        r.dproj[:, at] = low
 
     def out_back(b):
         rows = rows_of(b)
@@ -618,39 +614,63 @@
             cols = span(q * 256, 256)
             r.back[:, cols] = dot(r.og[rows, :], w[:, span(AT_OUT + q * 256, 256)])
 
-        loop(QUADS, quad)
-
-    def gated_rows(here):
-        g = r.dssd[here, :].astype(F32) + r.dproj[here, AT_GATE:AT_OUT].astype(F32)
-        s = r.ssd[here, :]
+        loop(QUADS, quad, 3)
+
+    def gated_tile(here, k):
+        cols = slice(k * 256, (k + 1) * 256)
+        low = r.dproj[here, AT_GATE + k * 256 : AT_GATE + (k + 1) * 256]
+        g = r.dssd[here, cols].astype(F32) + low.astype(F32)
+        s = r.ssd[here, cols]
         sg = sigmoid(g)
-        silu = g * sg
-        gated = s * silu
-        root = lax.rsqrt(jnp.mean(gated * gated, axis=1, keepdims=True) + EPS)
-        return g, s, sg, silu, gated, root
+        return cols, g, s, sg
+
+    def row_mean(v):
+        return jnp.sum(v, axis=1, keepdims=True) * (1.0 / INNER)
 
     def gate_forward(i):
-        for k in range(2):
-            here = span(i * 32 + k * 16, 16)
-            _, _, _, _, gated, root = gated_rows(here)
-            r.dproj[here, AT_X:AT_GATE] = (gated * root * gain).astype(BF)
+        here = span(i * 32, 32)
+        square = 0.0
+        for k in range(QUADS):
+            cols, g, s, sg = gated_tile(here, k)
+            gated = s * (g * sg)
+            square = square + gated * gated
+            r.gate[0:32, cols] = gated
+        root = lax.rsqrt(row_mean(square) + EPS)
+        for k in range(QUADS):
+            cols = slice(k * 256, (k + 1) * 256)
+            to = slice(AT_X + k * 256, AT_X + (k + 1) * 256)
+            r.dproj[here, to] = (r.gate[0:32, cols] * root * gain[:, cols]).astype(BF)
 
     def gate_block(b):
         def gate_rows(i):
-            here = span(b * GROUP + i * 16, 16)
-            d_out = r.back[span(i * 16, 16), :]
-            g, s, sg, silu, gated, root = gated_rows(here)
-            a = gain * d_out
-            lean = root * jnp.mean(gated * a, axis=1, keepdims=True)
-            v = gated * root
-            r.g_inner[0:8, :] += fold(d_out * v)
-            d_gated = root * (a - v * lean)
-            d_s = (d_gated * silu).astype(BF)
-            r.dssd[here, :] = d_s
-            r.g_inner[8:16, :] += fold(d_s.astype(F32) * r.cout[here, CX:].astype(F32))
-            r.dproj[here, AT_GATE:AT_OUT] = (d_gated * s * silu_slope(g, sg)).astype(BF)
-
-        loop(GROUP // 16, gate_rows)
+            here = span(b * GROUP + i * 32, 32)
+            local = span(i * 32, 32)
+            square, mixed = 0.0, 0.0
+            for k in range(QUADS):
+                cols, g, s, sg = gated_tile(here, k)
+                silu = g * sg
+                gated = s * silu
+                square = square + gated * gated
+                mixed = mixed + gated * (gain[:, cols] * r.back[local, cols])
+                r.gate[0:32, cols] = gated
+                r.gate[32:64, cols] = silu
+                r.gate[64:96, cols] = s * silu_slope(g, sg)
+            root = lax.rsqrt(row_mean(square) + EPS)
+            lean = root * row_mean(mixed)
+            for k in range(QUADS):
+                cols = slice(k * 256, (k + 1) * 256)
+                d_out = r.back[local, cols]
+                v = r.gate[0:32, cols] * root
+                r.g_inner[0:8, cols] += fold(d_out * v)
+                d_gated = root * (gain[:, cols] * d_out - v * lean)
+                d_s = (d_gated * r.gate[32:64, cols]).astype(BF)
+                r.dssd[here, cols] = d_s
+                x = r.cout[here, CX + k * 256 : CX + (k + 1) * 256]
+                r.g_inner[8:16, cols] += fold(d_s.astype(F32) * x.astype(F32))
+                to = slice(AT_GATE + k * 256, AT_GATE + (k + 1) * 256)
+                r.dproj[here, to] = (d_gated * r.gate[64:96, cols]).astype(BF)
+
+        loop(GROUP // 32, gate_rows)
 
     state_copy.wait()
     r.state_in[...] = r.state_in[...] * is_second
@@ -665,20 +685,28 @@
 
     carry_block(1)
 
+    def add_norm(value, cols):
+        product = value * w[:, cols].astype(F32)
+        for k in range(value.shape[1] // LANES):
+            r.g_norm[...] += product[:, k * LANES : (k + 1) * LANES]
+
     def wide_grad(i):
         g = wide_chunk(i)
         left = r.db_t if i < 2 else r.normed_t
         first = (AT_X if i < 2 else AT_GATE) + (i % 2) * CHUNK
 
         def tile(k):
-            put_grad(g, k * 256, dot(left[...], r.dproj[:, span(first + k * 256, 256)]))
-
-        loop(CHUNK // 256, tile)
+            value = dot(left[...], r.dproj[:, span(first + k * 256, 256)])
+            put_grad(g, k * 256, value)
+            if i >= 2:
+                add_norm(value, span(first + k * 256, 256))
+
+        loop(CHUNK // 256, tile, 3)
         sum_0(g)
 
     if fused:
         gather_5(3)
-    loop(BLOCKS, gate_project)
+    loop(QUADS, gate_project, 2)
     if fused:
         gather_3(4)
     loop(ROWS // 32, gate_forward)
@@ -700,14 +728,19 @@
     def state_back(b):
         rows = rows_of(b)
 
-        def quad(q, dq):
-            cols = span(q * 256, 256)
-            spread_f = dot(r.fade[rows, :], r.spread[:, cols])
-            dz = (spread_f * r.dssd[rows, cols].astype(F32)).astype(BF)
-            r.dheld[b, :, cols] = dot(r.turned[b, NSTATE:CX, :], dz)
-            return dq + dot_nt(dz, r.held[b, :, cols])
-
-        r.dqb[rows, :] = lax.fori_loop(0, QUADS, quad, jnp.zeros((GROUP, NSTATE), F32))
+        r.dqb[rows, :] = jnp.zeros((GROUP, NSTATE), F32)
+
+        def quads(i):
+            dq = 0.0
+            for q in (3 * i, 3 * i + 1, 3 * i + 2):
+                cols = heads_of(q)
+                spread_f = dot(r.fade[rows, :], r.spread[:, cols])
+                dz = (spread_f * r.dssd[rows, cols].astype(F32)).astype(BF)
+                r.dheld[b, :, cols] = dot(r.turned[b, NSTATE:CX, :], dz)
+                dq = dq + dot_nt(dz, r.held[b, :, cols])
+            r.dqb[rows, :] += dq
+
+        loop(QUADS // 3, quads)
 
     def no_state():
         r.dheld[0] = jnp.zeros((NSTATE, INNER), F32)
@@ -760,9 +793,9 @@
     loop(BLOCKS, prepare_back)
     dstate_copy.wait()
     r.dstate_in[...] = r.dstate_in[...] * is_first
-    r.dst[1] = r.dstate_in[...].astype(BF)
+    r.held[1] = r.dstate_in[...].astype(BF)
     r.state_in[...] = r.dheld[1] + decay_1 * r.dstate_in[...]
-    r.dst[0] = r.state_in[...].astype(BF)
+    r.held[0] = r.state_in[...].astype(BF)
 
     def backward_block(b, q):
         rows = rows_of(b)
@@ -774,7 +807,7 @@
 
         if b < 2:
             spread_w = dot(r.weight[rows, :], r.spread[:, heads])
-            d_states = r.dst[b, :, heads]
+            d_states = r.held[b, :, heads]
             dx_state = spread_w * dot(r.cout[rows, 0:NSTATE], d_states)
             r.flow[b, 0:8, heads] = fold(xq.astype(F32) * dx_state)
             r.dkb[rows, :] += dot_nt((xq.astype(F32) * spread_w).astype(BF), d_states)
@@ -898,8 +931,10 @@
 
         conv_back_all(q, CX + q * 256, AT_X + q * 256)
         g = quad_chunk(q)
-        put_grad(g, 0, dot(r.normed_t[...], r.dproj[:, span(AT_X + q * 256, 256)]))
+        value = dot(r.normed_t[...], r.dproj[:, span(AT_X + q * 256, 256)])
+        put_grad(g, 0, value)
         sum_0(g)
+        add_norm(value, span(AT_X + q * 256, 256))
 
     loop(QUADS, backward_quad)
 
@@ -920,7 +955,7 @@
         kept_of(b)[...] = give * ratio_of(b)
         give_of(b)[...] = exact_sum(upper, take - give)
 
-    loop(BLOCKS, backward_rest)
+    loop(BLOCKS, backward_rest, BLOCKS)
 
     def block_total(b, run, grad, decay):
         kept = jnp.sum(run[...] * grad[...], axis=0, keepdims=True)
@@ -942,40 +977,14 @@
         r.g_head[8:16, :] += fold(back_sum * (step * rate))
         r.dproj[rows, AT_DT : AT_DT + LANES] = d_pre.astype(BF)
 
-    loop(BLOCKS, step_grad)
+    loop(BLOCKS, step_grad, BLOCKS)
     sum_1(quad_chunk(5))
     first_edge(QUADS, 0)
     conv_back_all(QUADS, 0, 0)
-    put_grad(last_chunk, 0, dot(r.normed_t[...], r.dproj[:, 0:AT_X]))
+    value = dot(r.normed_t[...], r.dproj[:, 0:AT_X])
+    put_grad(last_chunk, 0, value)
     sum_0(last_chunk)
-    sum_2(quad_chunk(4))
-    sum_3(quad_chunk(3))
-
-    def in_block(b):
-        rows = rows_of(b)
-        r.ssd[rows, 0:D] = dot_nt(r.dproj[rows, :], w[:, 0:AT_OUT])
-
-    in_block(2)
-    sum_1(last_chunk)
-    sum_2(quad_chunk(5))
-    sum_3(quad_chunk(4))
-    loop(2, in_block)
-    sum_3(quad_chunk(5))
-
-    def norm_back(i):
-        rows = span(i * 32, 32)
-        v = r.tok[rows, :].astype(F32)
-        root = lax.rsqrt(jnp.mean(v * v, axis=1, keepdims=True) + EPS)
-        y = v * root
-        dn = r.ssd[rows, 0:D]
-        r.g_norm[...] += fold(dn * y)
-        bb = norm_gain * dn
-        d_v = root * (bb - y * jnp.mean(y * bb, axis=1, keepdims=True))
-        r.ssd[rows, 0:D] = r.og[rows, :].astype(F32) + d_v
-
-    loop(ROWS // 32, norm_back)
-    tgrad_copy = pltpu.make_async_copy(r.ssd.at[:, 0:D], r.tgrad, r.local.at[1])
-    tgrad_copy.start()
+    add_norm(value, slice(0, AT_X))
 
     def total(v):
         return jnp.sum(v, axis=0, keepdims=True)
@@ -989,7 +998,7 @@
     skips = dot_nt(high, r.spread[0:LANES, :]) + dot_nt(low, r.spread[0:LANES, :])
     r.small[0, 6:7, 0:LANES] = total(skips)
     r.small[0, 6:7, LANES:] = jnp.zeros((1, CONVCH - LANES), F32)
-    r.small[0, 7:8, 0:D] = total(r.g_norm[...])
+    r.small[0, 7:8, 0:D] = total(r.g_norm[...].T) / norm_gain
     r.small[0, 7:8, D:] = jnp.zeros((1, CONVCH - D), F32)
     if fused:
 
@@ -1009,12 +1018,44 @@
             return value
 
         send_small(0, 0, 1, lambda j: sibling)
-        sum_2(last_chunk)
+
+    def in_block(b):
+        rows = rows_of(b)
+        r.ssd[rows, 0:D] = dot_nt(r.dproj[rows, :], w[:, 0:AT_OUT])
+
+    sum_1(last_chunk)
+    sum_2(quad_chunk(4))
+    sum_3(quad_chunk(3))
+    in_block(2)
+    if fused:
         r.small[1] = add_small(0, 0, 1)
         send_small(1, 1, PLANE - 1, on_plane)
-        sum_3(last_chunk)
+    sum_2(quad_chunk(5))
+    sum_3(quad_chunk(4))
+    in_block(0)
+    sum_2(last_chunk)
+    if fused:
         r.small[2] = add_small(1, 1, PLANE - 1)
         send_small(2, PLANE, nz - 1, on_chain)
+    in_block(1)
+    sum_3(quad_chunk(5))
+
+    def norm_back(i):
+        rows = span(i * 32, 32)
+        v = r.tok[rows, :].astype(F32)
+        root = lax.rsqrt(jnp.mean(v * v, axis=1, keepdims=True) + EPS)
+        y = v * root
+        dn = r.ssd[rows, 0:D]
+        bb = norm_gain * dn
+        d_v = root * (bb - y * jnp.mean(y * bb, axis=1, keepdims=True))
+        r.ssd[rows, 0:D] = r.og[rows, :].astype(F32) + d_v
+
+    loop(ROWS // 32, norm_back, 3)
+    tgrad_copy = pltpu.make_async_copy(r.ssd.at[:, 0:D], r.tgrad, r.local.at[1])
+    tgrad_copy.start()
+
+    if fused:
+        sum_3(last_chunk)
 
         def hand_out(g, dst, first, count):
             sum_4(g)
@@ -1061,11 +1102,11 @@
         "cut": ((BLOCKS, QUADS, 8, GROUP), F32), "spread": ((256, INNER), BF),
         "turned": ((BLOCKS, CX, GROUP), BF), "sco": ((BLOCKS, GROUP, GROUP), F32), "dkb": ((ROWS, LANES), F32), "dqb": ((ROWS, LANES), F32),
         "runs": ((2, NSTATE, INNER), F32), "held": ((2, NSTATE, INNER), BF),
-        "dheld": ((2, NSTATE, INNER), F32), "dst": ((2, NSTATE, INNER), BF),
+        "dheld": ((2, NSTATE, INNER), F32),
         "flow": ((2, 8, INNER), F32), "halo": ((BLOCKS, 8, CONVCH), F32),
         "halo_next": ((2, 8, CONVCH), F32), "edge_in": ((EDGE, D), BF),
         "state_in": ((NSTATE, INNER), F32), "dstate_in": ((NSTATE, INNER), F32),
-        "dedge_in": ((8, CONVCH), F32), "g_norm": ((8, D), F32), "g_conv": ((40, CONVCH), F32),
+        "dedge_in": ((8, CONVCH), F32), "g_norm": ((D, LANES), F32), "g_conv": ((40, CONVCH), F32),
         "g_head": ((16, LANES), F32), "g_inner": ((16, INNER), F32), "small": ((3, 8, CONVCH), F32),
     }
     dma = pltpu.SemaphoreType.DMA

time: 163 us -> 145 us (0.89)
  Pallas kernels: 160 us -> 143 us
    pallas_call x1, Pallas kernels: 155 us -> 138 us  [call_mixer(): pl.pallas_call(functools.partial(mixer, names, fused, nz), out_shape=[jax...]
where the time goes in v5:
time: 145 us
  Pallas kernels  143 us (99%)
    pallas_call x1, Pallas kernels, call_mixer(): pl.pallas_call(functools.partial(mixer, names, fused, nz), out_shape=[jax...  138 us
    pallas_call x1, Pallas kernels, call_place(): pl.pallas_call(place_results, out_shape=[jax.ShapeDtypeStruct(s, t) for s...  5.14 us

profile of v5, /device:TPU:0, one launch (start us, length us, event | category | flops | bytes accessed | tf_op | source)
XLA Modules:
  0.0 145.1 jit_solution(145350237097449733)
XLA Ops:
  0.6 1.3 copy.24.refs_0_.lengths
  2.0 137.8 %mixer.1 = (bf16[768,768]{1,0:T(8,128)(2,1)}, f32[768,768]{1,0:T(8,128)}, f32[8,1792]{1,0:T(8,128)}, f32[24,3352]{1,0:T(8,128)}, f32[24,1536]{1,0:T(8,128)}) custom-call(s32[2,1]{1,0:T(2,128)} %copy.24.refs_0_.lengths, bf16[2,1,512,768]{3,2,1,0:T(8,128)(2,1)} %refs_1_.1, bf16[2,1,512,768]{3,2,1,0:T(8,128)(2,1)} %refs_2_.1, f32[768]{0:T(1024)} %refs_3_.1, ...), custom_call_target="tpu_custom_call" | custom-call | tf_op jit(solution)/shard_map/mixer/pallas_call | solution.py:1136
  139.7 5.1 %place_results.1 = (bf16[2,1,512,768]{3,2,1,0:T(8,128)(2,1)}, f32[2,1,512,768]{3,2,1,0:T(8,128)}, f32[768]{0:T(1024)}, f32[24,3352]{1,0:T(8,128)}, f32[4,1792]{1...) custom-call(s32[2,1]{1,0:T(2,128)} %copy.24.refs_0_.lengths, ...), custom_call_target="tpu_custom_call" | custom-call | tf_op jit(solution)/shard_map/place_results/pallas_call | solution.py:1194

commit v6 on v5

--- a/solution.py
+++ b/solution.py
@@ -32,10 +32,13 @@
 CX = 2 * NSTATE
 CHUNK = 768
 WIDE_CHUNKS = 4
-CHUNKS = WIDE_CHUNKS + QUADS + 1
+CHUNKS = WIDE_CHUNKS + QUADS + 2
 UNITS = 7
 SLOTS = 4
-GATHERS = ((0, 512), (512, 512), (1024, 1024), (AT_GATE, INNER), (AT_OUT, INNER))
+GATHERS = (
+    (0, 512), (512, 512), (1024, 512), (1536, 512), (AT_GATE, INNER), (AT_OUT, 1024),
+    (AT_OUT + 1024, 512),
+)
 PLANE = 4
 
 BF = jnp.bfloat16
@@ -158,9 +161,11 @@
         key_query = r.in_weight[:, wide : wide + CX].astype(F32)
         own_columns(r.gate, 0)[...] = jnp.concatenate([key_query, steps, fill], axis=1)
         own_columns(r.gate, 1)[...] = r.in_weight[:, INNER : INNER + 512].astype(F32)
-        own_columns(r.gate, 2)[...] = r.in_weight[:, INNER + 512 : wide].astype(F32)
-        own_columns(r.gate, 3)[...] = r.in_weight[:, 0:INNER].astype(F32)
-        own_columns(r.gate, 4)[...] = r.out_weight[...].astype(F32)
+        own_columns(r.gate, 2)[...] = r.in_weight[:, INNER + 512 : INNER + 1024].astype(F32)
+        own_columns(r.gate, 3)[...] = r.in_weight[:, INNER + 1024 : wide].astype(F32)
+        own_columns(r.gate, 4)[...] = r.in_weight[:, 0:INNER].astype(F32)
+        own_columns(r.gate, 5)[...] = r.out_weight[:, 0:1024].astype(F32)
+        own_columns(r.gate, 6)[...] = r.out_weight[:, 1024:].astype(F32)
 
     pl.semaphore_wait(barrier, len(peers))
 
@@ -240,6 +245,24 @@
         wait_bytes(2 * nz, part(c), r.g_recv.at[c, 2])
         last_copy(c).start()
 
+    def turned_copy(c, j):
+        at = w.at[span(z_at * PLANE * slab, PLANE * slab, 16), part(c)]
+        return remote(at, at, r.g_send.at[c, 0], r.g_recv.at[c, 0], on_chain(j))
+
+    def turned_2(c):
+        wait_bytes(4, part(c), r.g_recv.at[c, 1])
+        for kind in range(2):
+            plane_copy(c, kind + 2, 0).start()
+
+    def turned_3(c):
+        wait_bytes(2, part(c), r.g_recv.at[c, 2])
+        for j in range(1, nz):
+            turned_copy(c, j).start()
+
+    def turned_4(c):
+        wait_bytes(2 * PLANE * (nz - 1), part(c), r.g_recv.at[c, 0])
+        last_copy(c).start()
+
     def gather_5(c):
         last_copy(c).wait_recv()
 
@@ -253,7 +276,8 @@
     def quad_chunk(q):
         return WIDE_CHUNKS + q, q // 3, (q % 3) * 256, 128, WIDE_CHUNKS + q // 3, (q % 3) * 128
 
-    last_chunk = (WIDE_CHUNKS + QUADS, 2, 0, AT_X // 2, UNITS - 1, 0)
+    step_chunk = (WIDE_CHUNKS + QUADS, 2, AT_DT, LANES, UNITS - 1, 0)
+    last_chunk = (WIDE_CHUNKS + QUADS + 1, 2, 0, LANES, UNITS - 1, LANES)
 
     def source(g, which):
         return span(g[2] + which * g[3], g[3], 128)
@@ -369,6 +393,7 @@
                 gather_0(c)
                 gather_1(c)
         gather_0(2)
+        gather_1(6)
 
     r.convp[0:CONV, 0:CX] = r.conv_weight[:, INNER:]
     r.convp[0:CONV, CX:] = r.conv_weight[:, 0:INNER]
@@ -380,8 +405,8 @@
         r.headp[i : i + 1, 0:HEADS] = v[...].reshape(1, HEADS)
     norm_gain = r.norm_gain[...].reshape(1, D)
 
-    first_long = r.lengths[0, 0] > r.lengths[1, 0]
-    shortest = jnp.minimum(r.lengths[0, 0], r.lengths[1, 0])
+    first_long = r.lengths[0, 0] > r.lengths[0, 1]
+    shortest = jnp.minimum(r.lengths[0, 0], r.lengths[0, 1])
     for i in range(4):
         raw_copies[i].wait()
 
@@ -400,6 +425,10 @@
     loop(2 * GROUP // 64, pick_rows)
     edge_copy = pair_copy(0, r.tok.at[2 * GROUP - EDGE : 2 * GROUP, :], r.edge_in)
     edge_copy.start()
+    if fused:
+        gather_2(0)
+        gather_1(2)
+        gather_0(3)
     loop(GROUP // 64, pick_short)
 
     loop(QUADS, make_spread)
@@ -430,14 +459,12 @@
         r.normed[rows, :] = norm_of(r.tok[rows, :].astype(F32))
 
     loop(ROWS // 64, norm_rows, 2)
+    if fused:
+        gather_3(0)
+        gather_2(1)
     edge_copy.wait()
     r.normed[ROWS:, :] = norm_of(r.edge_in[...].astype(F32) * is_second)
 
-    if fused:
-        gather_2(0)
-        gather_1(2)
-        gather_0(3)
-
     def turn(b):
         rows = rows_of(b)
         r.normed_t[:, rows] = r.normed[rows, :].T
@@ -446,11 +473,11 @@
     loop(BLOCKS, turn, BLOCKS)
 
     if fused:
-        gather_2(1)
-        gather_3(0)
-        gather_1(3)
         gather_4(0)
         gather_3(1)
+        turned_2(6)
+        gather_1(3)
+        gather_0(4)
         gather_5(0)
 
     def conv_acc(values, before, cols):
@@ -504,25 +531,27 @@
     loop(BLOCKS, prepare, BLOCKS)
     if fused:
         gather_2(2)
-        gather_0(4)
         gather_4(1)
+        gather_2(3)
         gather_1(4)
+        gather_0(5)
         gather_5(1)
 
-    gather_steps = (
-        (1, gather_3, 2), (1, gather_2, 3), (2, gather_4, 2), (2, gather_5, 2), (3, gather_2, 4),
-        (4, gather_3, 3),
-    )
-
-    def gather_on(q):
-        if fused:
-            for point in range(QUADS):
-
-                @pl.when(q == point)
+    gather_steps = {
+        (0, -1): ((gather_3, 2),), (1, -1): ((gather_4, 2), (gather_3, 3), (gather_1, 5)),
+        (2, -1): ((gather_5, 2), (gather_4, 3), (gather_2, 4)),
+        (3, -1): ((gather_2, 5), (turned_3, 6)), (4, -1): ((gather_5, 3), (gather_3, 4)),
+        (5, -1): ((gather_3, 5),),
+    }
+
+    def gather_on(q, b):
+        for at, steps in gather_steps.items():
+            if fused and at[1] == b:
+
+                @pl.when(q == at[0])
                 def _():
-                    for at, step, c in gather_steps:
-                        if at == point:
-                            step(c)
+                    for step, c in steps:
+                        step(c)
 
     def to_first(v, q):
         return pltpu.roll(v, (LANES - 4 * q) % LANES, 1)
@@ -569,9 +598,10 @@
             r.ssd[span(b * GROUP + half, half), place] = out_bottom + xf[half:]
 
     def forward_quad(q):
-        gather_on(q)
+        gather_on(q, -1)
         project(span(AT_X + q * 256, 256), span(CX + q * 256, 256))
         for b in range(BLOCKS):
+            gather_on(q, b)
             forward_block(b, q)
 
     loop(QUADS, forward_quad)
@@ -585,7 +615,8 @@
     state_copy = pair_copy(2, r.runs.at[1], r.state_in)
     state_copy.start()
     if fused:
-        gather_4(3)
+        gather_4(4)
+        turned_4(6)
 
     def carry_block(b):
         rows = rows_of(b)
@@ -705,22 +736,30 @@
         sum_0(g)
 
     if fused:
-        gather_5(3)
+        gather_4(5)
+        gather_5(4)
     loop(QUADS, gate_project, 2)
-    if fused:
-        gather_3(4)
     loop(ROWS // 32, gate_forward)
-    if fused:
-        gather_4(4)
     wide_grad(0)
     wide_grad(1)
     if fused:
-        gather_5(4)
-    for b in range(BLOCKS):
+        gather_5(5)
+        gather_5(6)
+    for b in range(2):
         out_back(b)
         gate_block(b)
-        if b < 2:
-            sum_1(wide_chunk(b))
+        sum_1(wide_chunk(b))
+
+    @pl.when(seq == 0)
+    def _():
+        out_back(2)
+        gate_block(2)
+
+    @pl.when(seq > 0)
+    def _():
+        r.dssd[2 * GROUP :, :] = jnp.zeros((GROUP, INNER), BF)
+        r.dproj[2 * GROUP :, AT_GATE:AT_OUT] = jnp.zeros((GROUP, INNER), BF)
+
     wide_grad(2)
     wide_grad(3)
     sum_2(wide_chunk(0))
@@ -980,11 +1019,16 @@
     loop(BLOCKS, step_grad, BLOCKS)
     sum_1(quad_chunk(5))
     first_edge(QUADS, 0)
+    value = dot(r.normed_t[...], r.dproj[:, AT_DT:AT_X])
+    put_grad(step_chunk, 0, value)
+    sum_0(step_chunk)
+    add_norm(value, slice(AT_DT, AT_X))
     conv_back_all(QUADS, 0, 0)
-    value = dot(r.normed_t[...], r.dproj[:, 0:AT_X])
+    value = dot(r.normed_t[...], r.dproj[:, 0:CX])
     put_grad(last_chunk, 0, value)
     sum_0(last_chunk)
-    add_norm(value, slice(0, AT_X))
+    sum_1(step_chunk)
+    add_norm(value, slice(0, CX))
 
     def total(v):
         return jnp.sum(v, axis=0, keepdims=True)
@@ -1031,6 +1075,7 @@
         r.small[1] = add_small(0, 0, 1)
         send_small(1, 1, PLANE - 1, on_plane)
     sum_2(quad_chunk(5))
+    sum_2(step_chunk)
     sum_3(quad_chunk(4))
     in_block(0)
     sum_2(last_chunk)
@@ -1039,6 +1084,7 @@
         send_small(2, PLANE, nz - 1, on_chain)
     in_block(1)
     sum_3(quad_chunk(5))
+    sum_3(step_chunk)
 
     def norm_back(i):
         rows = span(i * 32, 32)
@@ -1065,14 +1111,16 @@
                 value = jnp.where(seq == half_at, mine, theirs)
                 size = min(g[3], count - half_at * g[3])
                 at = first + half_at * g[3]
-                dst[:, at : at + size] = value[:, 0:size]
+                if size > 0:
+                    dst[:, at : at + size] = value[:, 0:size]
 
         for i in range(WIDE_CHUNKS):
             dst = r.grad_out if i < 2 else r.grad_in
             hand_out(wide_chunk(i), dst, (i % 2) * CHUNK, CHUNK)
         for q in range(QUADS):
             hand_out(quad_chunk(q), r.grad_in, INNER + q * 256, 256)
-        hand_out(last_chunk, r.grad_in, 2 * INNER, CX + HEADS)
+        hand_out(step_chunk, r.grad_in, 2 * INNER + CX, HEADS)
+        hand_out(last_chunk, r.grad_in, 2 * INNER, CX)
         r.small_out[...] = add_small(2, PLANE, nz - 1)
         for c in range(len(GATHERS)):
             gather_end(c)
@@ -1151,10 +1199,8 @@
     step, rates, skip, gain, out_at, blank, blank_low, sems,
 ):
     seq = lax.axis_index("seq")
-    long = jnp.where(lengths[0, 0] > lengths[1, 0], 0, 1)
+    long = jnp.where(lengths[0, 0] > lengths[0, 1], 0, 1)
     rows = mixed_at.shape[2]
-    blank[...] = jnp.zeros_like(blank)
-    blank_low[...] = jnp.zeros_like(blank_low)
     copies = []
     for i, (src, dst, zero) in enumerate(((tgrad, tgrad_at, blank), (mixed, mixed_at, blank_low))):
         first, after = dst.at[1 - long, 0, 0:GROUP, :], dst.at[1 - long, 0, GROUP:rows, :]
@@ -1164,6 +1210,7 @@
         end = pltpu.make_async_copy(zero.at[0 : rows - GROUP, :], after, sems.at[3 * i + 2])
         whole.start()
         pl.when(seq == 0)(used.start)
+        zero[...] = jnp.zeros_like(zero)
         pl.when(seq > 0)(unused.start)
         end.start()
         copies += [whole, used, end]
@@ -1214,7 +1261,7 @@
     fused = nf % PLANE == 0 and (2 * own) % 16 == 0 and own % 8 == 0
     nz = nf // PLANE if fused else 1
     arrays = {
-        "lengths": lengths, "tokens": tokens, "out_grad": out_grad, "norm_gain": norm_gain,
+        "lengths": lengths.T, "tokens": tokens, "out_grad": out_grad, "norm_gain": norm_gain,
         "conv_weight": conv_weight, "conv_bias": conv_bias, "dt_bias": dt_bias, "a_log": a_log,
         "skip_gain": skip_gain, "out_gain": out_gain,
     }
@@ -1234,7 +1281,7 @@
             [summed[:, INNER : 3 * INNER], summed[:, 3 * INNER : 3 * INNER + CX + HEADS]], axis=1
         )
         small = lax.psum(small, both)
-    return call_place(tokens.shape, lengths, mixed, tgrad, small, grad_in, grad_out)
+    return call_place(tokens.shape, lengths.T, mixed, tgrad, small, grad_in, grad_out)
 
 
 def solution(mesh):

time: 145 us -> 141 us (0.972)
  Pallas kernels: 143 us -> 140 us
    pallas_call x1, Pallas kernels: 138 us -> 135 us  [call_mixer(): pl.pallas_call(functools.partial(mixer, names, fused, nz), out_shape=[jax...]
where the time goes in v6:
time: 141 us
  Pallas kernels  140 us (99%)
    pallas_call x1, Pallas kernels, call_mixer(): pl.pallas_call(functools.partial(mixer, names, fused, nz), out_shape=[jax...  135 us
    pallas_call x1, Pallas kernels, call_place(): pl.pallas_call(place_results, out_shape=[jax.ShapeDtypeStruct(s, t) for s...  5.14 us

profile of v6, /device:TPU:0, one launch (start us, length us, event | category | flops | bytes accessed | tf_op | source)
XLA Modules:
  0.0 140.9 jit_solution(7363301002965967923)
XLA Ops:
  0.6 135.0 %mixer.1 = (bf16[768,768]{1,0:T(8,128)(2,1)}, f32[768,768]{1,0:T(8,128)}, f32[8,1792]{1,0:T(8,128)}, f32[24,3352]{1,0:T(8,128)}, f32[24,1536]{1,0:T(8,128)}) custom-call(s32[1,2]{1,0:T(1,128)} %bitcast.4, bf16[2,1,512,768]{3,2,1,0:T(8,128)(2,1)} %refs_1_.1, bf16[2,1,512,768]{3,2,1,0:T(8,128)(2,1)} %refs_2_.1, f32[768]{0:T(1024)} %refs_3_.1, ...), custom_call_target="tpu_custom_call" | custom-call | tf_op jit(solution)/shard_map/mixer/pallas_call | solution.py:1184
  135.6 5.1 %place_results.1 = (bf16[2,1,512,768]{3,2,1,0:T(8,128)(2,1)}, f32[2,1,512,768]{3,2,1,0:T(8,128)}, f32[768]{0:T(1024)}, f32[24,3352]{1,0:T(8,128)}, f32[4,1792]{1...) custom-call(s32[1,2]{1,0:T(1,128)} %bitcast.5, ...), custom_call_target="tpu_custom_call" | custom-call | tf_op jit(solution)/shard_map/place_results/pallas_call | solution.py:1241

commit v7 on v6

--- a/solution.py
+++ b/solution.py
@@ -160,12 +160,6 @@
         fill = jnp.zeros((steps.shape[0], AT_X - CX - HEADS), F32)
         key_query = r.in_weight[:, wide : wide + CX].astype(F32)
         own_columns(r.gate, 0)[...] = jnp.concatenate([key_query, steps, fill], axis=1)
-        own_columns(r.gate, 1)[...] = r.in_weight[:, INNER : INNER + 512].astype(F32)
-        own_columns(r.gate, 2)[...] = r.in_weight[:, INNER + 512 : INNER + 1024].astype(F32)
-        own_columns(r.gate, 3)[...] = r.in_weight[:, INNER + 1024 : wide].astype(F32)
-        own_columns(r.gate, 4)[...] = r.in_weight[:, 0:INNER].astype(F32)
-        own_columns(r.gate, 5)[...] = r.out_weight[:, 0:1024].astype(F32)
-        own_columns(r.gate, 6)[...] = r.out_weight[:, 1024:].astype(F32)
 
     pl.semaphore_wait(barrier, len(peers))
 
@@ -197,13 +191,13 @@
 
     def plane_copy(c, kind, back):
         low, size = GATHERS[c]
-        owner = (p_at, p_at, plane_peer(1), plane_peer(2))[kind]
+        owner = (p_at, p_at, plane_peer(1), plane_peer(2), p_at)[kind]
         cols = part(c)
-        if kind >= 2:
+        if kind in (2, 3):
             cols = span(low + seq * (size // 2) + (kind - 2) * (size // 4), size // 4, 128)
         at = w.at[slab_of((z_at - back + nz) % nz * PLANE + owner), cols]
-        device = on_plane((1, 2, 2, 1)[kind])
-        return remote(at, at, r.g_send.at[c, 0], r.g_recv.at[c, 1 + kind // 2], device)
+        device = on_plane((1, 2, 2, 1, 3)[kind])
+        return remote(at, at, r.g_send.at[c, 0], r.g_recv.at[c, 1 + min(kind // 2, 1)], device)
 
     def last_copy(c):
         at = w.at[:, part(c)]
@@ -226,18 +220,18 @@
             chain_copy(c, j).start()
 
     def gather_1(c):
-        for kind in range(2):
+        for kind in (0, 1) if c else (4, 0, 1):
             plane_copy(c, kind, 0).start()
 
     def gather_2(c):
         wait_bytes(2 * (nz - 1), part(c), r.g_recv.at[c, 0])
         for back in range(1, nz):
-            for kind in range(2):
+            for kind in (0, 1) if c else (4, 0, 1):
                 plane_copy(c, kind, back).start()
 
     def gather_3(c):
         wait_bytes(4 * nz, part(c), r.g_recv.at[c, 1])
-        for back in range(nz):
+        for back in range(nz if c else 0):
             for kind in range(2):
                 plane_copy(c, kind + 2, back).start()
 
@@ -325,7 +319,7 @@
         def add(i):
             at = (g[1], i // PLANE, i % PLANE, slice(None), source(g, seq))
             theirs = r.r0[g[4], i // PLANE, i % PLANE, :, target(g)]
-            r.wg[at] = (r.wg[at].astype(F32) + theirs.astype(F32)).astype(BF)
+            r.wg[at] = r.wg[at] + theirs
 
         loop(nz * PLANE, add, PLANE)
         for j in (3, 1, 2):
@@ -372,11 +366,23 @@
     def shard_copy(c):
         size = GATHERS[c][1] // 2
         rows, cols = slice(c * own, (c + 1) * own), span((1 - seq) * size, size, 128)
-        return pair_copy(1, r.gate.at[rows, cols], r.back.at[rows, cols])
-
-    if fused:
-        for c in range(len(GATHERS)):
+        return pair_copy(1 if c else 4, r.gate.at[rows, cols], r.back.at[rows, cols])
+
+    if fused:
+        shard_copy(0).start()
+        own_columns(r.gate, 1)[...] = r.in_weight[:, INNER : INNER + 512].astype(F32)
+        own_columns(r.gate, 2)[...] = r.in_weight[:, INNER + 512 : INNER + 1024].astype(F32)
+        own_columns(r.gate, 3)[...] = r.in_weight[:, INNER + 1024 : wide].astype(F32)
+        own_columns(r.gate, 4)[...] = r.in_weight[:, 0:INNER].astype(F32)
+        own_columns(r.gate, 5)[...] = r.out_weight[:, 0:1024].astype(F32)
+        own_columns(r.gate, 6)[...] = r.out_weight[:, 1024:].astype(F32)
+        for c in range(1, len(GATHERS)):
             shard_copy(c).start()
+
+    def pick_heads():
+        row, lane = iota((8 * LANES, LANES), 0), iota((8 * LANES, LANES), 1)
+        pair, kind, second = row >> 9, (row >> 8) & 1, (row & 127) >> 6
+        r.pick[...] = (lane == 2 * pair + second + 64 * kind).astype(F32).astype(BF)
 
     def make_spread(q):
         shape = (256, 256)
@@ -384,14 +390,17 @@
         r.spread[:, span(q * 256, 256)] = (head == (iota(shape, 0) & 127)).astype(F32).astype(BF)
 
     if fused:
-        at = r.back.at[0 : own * (WIDE // 2) // INNER, :]
+        shard_copy(0).wait()
+        gather_own(0)
+        gather_0(0)
+        gather_1(0)
+        at = r.back.at[0 : own * (WIDE - GATHERS[0][1]) // 2 // 768, 0:768]
         for sem in (r.pair_send.at[1], r.pair_recv.at[1]):
             pltpu.make_async_copy(at, at, sem).wait()
-        for c in range(len(GATHERS)):
+        for c in range(1, len(GATHERS)):
             gather_own(c)
-            if c < 2:
-                gather_0(c)
-                gather_1(c)
+        gather_0(1)
+        gather_1(1)
         gather_0(2)
         gather_1(6)
 
@@ -432,6 +441,7 @@
     loop(GROUP // 64, pick_short)
 
     loop(QUADS, make_spread)
+    pick_heads()
     r.innerp[0:1, :] = r.out_gain[...].reshape(1, INNER)
     r.innerp[1:2, :] = dot(side_by_side(r.headp[...]), r.spread[...])[2:3, :]
     tri_shape = (GROUP, GROUP)
@@ -814,12 +824,6 @@
 
     def kept_of(b):
         return r.back.at[:, span(CHUNK + (BLOCKS + b) * LANES, LANES)]
-
-    def pick_heads(q):
-        row, lane = iota((8 * LANES, LANES), 0), iota((8 * LANES, LANES), 1)
-        pair, kind, second = row >> 9, (row >> 8) & 1, (row & 127) >> 6
-        head = 4 * q + 2 * pair + second + 64 * kind
-        r.pick[...] = (lane == head).astype(F32).astype(BF)
 
     def prepare_back(b):
         rows = rows_of(b)
@@ -887,7 +891,8 @@
             ssd = r.ssd[rows, span(q * 256 + j * LANES, LANES)]
             products += [*halves(xf * dxp), *halves(df * (ssd - kept * xf))]
             dx[:, lanes] = dxp + kept * df
-        give_of(b)[...] += dot(jnp.concatenate(products, axis=1), r.pick[...])
+        sums = dot(jnp.concatenate(products, axis=1), r.pick[...])
+        give_of(b)[...] += pltpu.roll(sums, 4 * q, 1)
 
     def edge_grad(b, source, cols):
         first = r.clow[b * GROUP : b * GROUP + 16, cols].astype(F32)
@@ -940,13 +945,15 @@
         @pl.when(q == 2)
         def _():
             sum_3(wide_chunk(2))
-            sum_2(wide_chunk(3))
 
         @pl.when(q == 3)
         def _():
+            sum_2(wide_chunk(3))
+
+        @pl.when(q == 4)
+        def _():
             sum_3(wide_chunk(3))
 
-        pick_heads(q)
         for b in range(BLOCKS):
             backward_block(b, q)
             if b == 0:
@@ -1159,7 +1166,7 @@
     }
     dma = pltpu.SemaphoreType.DMA
     sems = {
-        "pair_send": dma((4,)), "pair_recv": dma((4,)), "edge_send": dma((QUADS + 1,)),
+        "pair_send": dma((5,)), "pair_recv": dma((5,)), "edge_send": dma((QUADS + 1,)),
         "edge_recv": dma((QUADS + 1,)), "local": dma((6,)),
     }
     if fused:

time: 141 us -> 140 us (level)
  no operation moved by 1% of the time
where the time goes in v7:
time: 140 us
  Pallas kernels  139 us (99%)
    pallas_call x1, Pallas kernels, call_mixer(): pl.pallas_call(functools.partial(mixer, names, fused, nz), out_shape=[jax...  134 us
    pallas_call x1, Pallas kernels, call_place(): pl.pallas_call(place_results, out_shape=[jax.ShapeDtypeStruct(s, t) for s...  5.14 us

profile of v7, /device:TPU:0, one launch (start us, length us, event | category | flops | bytes accessed | tf_op | source)
XLA Modules:
  0.0 139.8 jit_solution(3126101764348189292)
XLA Ops:
  0.6 133.8 %mixer.1 = (bf16[768,768]{1,0:T(8,128)(2,1)}, f32[768,768]{1,0:T(8,128)}, f32[8,1792]{1,0:T(8,128)}, f32[24,3352]{1,0:T(8,128)}, f32[24,1536]{1,0:T(8,128)}) custom-call(s32[1,2]{1,0:T(1,128)} %bitcast.4, bf16[2,1,512,768]{3,2,1,0:T(8,128)(2,1)} %refs_1_.1, bf16[2,1,512,768]{3,2,1,0:T(8,128)(2,1)} %refs_2_.1, f32[768]{0:T(1024)} %refs_3_.1, ...), custom_call_target="tpu_custom_call" | custom-call | tf_op jit(solution)/shard_map/mixer/pallas_call | solution.py:1191
  134.5 5.1 %place_results.1 = (bf16[2,1,512,768]{3,2,1,0:T(8,128)(2,1)}, f32[2,1,512,768]{3,2,1,0:T(8,128)}, f32[768]{0:T(1024)}, f32[24,3352]{1,0:T(8,128)}, f32[4,1792]{1...) custom-call(s32[1,2]{1,0:T(1,128)} %bitcast.5, ...), custom_call_target="tpu_custom_call" | custom-call | tf_op jit(solution)/shard_map/place_results/pallas_call | solution.py:1248

commit v8 on v7

--- a/solution.py
+++ b/solution.py
@@ -551,7 +551,6 @@
         (0, -1): ((gather_3, 2),), (1, -1): ((gather_4, 2), (gather_3, 3), (gather_1, 5)),
         (2, -1): ((gather_5, 2), (gather_4, 3), (gather_2, 4)),
         (3, -1): ((gather_2, 5), (turned_3, 6)), (4, -1): ((gather_5, 3), (gather_3, 4)),
-        (5, -1): ((gather_3, 5),),
     }
 
     def gather_on(q, b):
@@ -625,6 +624,7 @@
     state_copy = pair_copy(2, r.runs.at[1], r.state_in)
     state_copy.start()
     if fused:
+        gather_3(5)
         gather_4(4)
         turned_4(6)
 

time: 140 us -> 140 us (level)
  no operation moved by 1% of the time
where the time goes in v8:
time: 140 us; the launch traced here: 139 us
  Pallas kernels  139 us (99%)
    pallas_call x1, Pallas kernels, call_mixer(): pl.pallas_call(functools.partial(mixer, names, fused, nz), out_shape=[jax...  133 us
    pallas_call x1, Pallas kernels, call_place(): pl.pallas_call(place_results, out_shape=[jax.ShapeDtypeStruct(s, t) for s...  5.14 us

profile of v8, /device:TPU:0, one launch (start us, length us, event | category | flops | bytes accessed | tf_op | source)
XLA Modules:
  0.0 139.3 jit_solution(13245754553432274081)
XLA Ops:
  0.6 133.4 %mixer.1 = (bf16[768,768]{1,0:T(8,128)(2,1)}, f32[768,768]{1,0:T(8,128)}, f32[8,1792]{1,0:T(8,128)}, f32[24,3352]{1,0:T(8,128)}, f32[24,1536]{1,0:T(8,128)}) custom-call(s32[1,2]{1,0:T(1,128)} %bitcast.4, bf16[2,1,512,768]{3,2,1,0:T(8,128)(2,1)} %refs_1_.1, bf16[2,1,512,768]{3,2,1,0:T(8,128)(2,1)} %refs_2_.1, f32[768]{0:T(1024)} %refs_3_.1, ...), custom_call_target="tpu_custom_call" | custom-call | tf_op jit(solution)/shard_map/mixer/pallas_call | solution.py:1191
  134.0 5.1 %place_results.1 = (bf16[2,1,512,768]{3,2,1,0:T(8,128)(2,1)}, f32[2,1,512,768]{3,2,1,0:T(8,128)}, f32[768]{0:T(1024)}, f32[24,3352]{1,0:T(8,128)}, f32[4,1792]{1...) custom-call(s32[1,2]{1,0:T(1,128)} %bitcast.5, ...), custom_call_target="tpu_custom_call" | custom-call | tf_op jit(solution)/shard_map/place_results/pallas_call | solution.py:1248
